TPU v7x, 256 devices: a whole 4x4x8 slice. The times are simulated.
256 devices in a mesh: net: 4 (over z_hi, core), fsdp: 64 (over z_lo, x, y).
Axes of the slice: x: 4, y: 4, z: 8 (z_hi: 2, z_lo: 4; z = z_hi * 4 + z_lo), core: 2. Of those that a mesh axis runs over, the one named last changes fastest.
Arguments:
- noise_in: bfloat16 [8, 4096, 64], P(None, 'fsdp'), may hold values from -48 to 48
- renoise: bfloat16 [8, 4096, 64], P(None, 'fsdp'), may hold values from -6 to 6
- timesteps: int32 [8], replicated, may hold values from 20 to 979
- prompt_ids: int32 [8, 77], replicated, may hold values from 0 to 49407
- embed_w: bfloat16 [4, 64, 2432], P('net', None, 'fsdp'), may hold values from -0.75 to 0.75
- proj_w: bfloat16 [4, 2432, 2432], P('net', 'fsdp'), may hold values from -0.125 to 0.125
- final_w: bfloat16 [4, 2432, 64], P('net', 'fsdp'), may hold values from -0.125 to 0.125
- text_table: bfloat16 [49408, 64], P(('net', 'fsdp')), may hold values from -6 to 6
Outputs:
- sample_grad: float32 [8, 4096, 64], P(None, 'fsdp')
All inputs are finite; a program needn't handle non-finite values. Where the computation divides by a largest or mean magnitude, that divisor is 1e-20 or more.
Results may differ from a plain program's by a relative error of at most 0.0048.
Values may be sent and summed in bfloat16 or wider, within the bound.
No kernel may reach another device: no remote copies, remote signals or barrier semaphores. Data moves between devices by JAX's collectives and lax.ppermute only.
A program may use at most 128 MiB of HBM per device.

v0:
```python
import jax
import jax.numpy as jnp
from jax import lax
from jax.experimental import pallas as pl
from jax.experimental.pallas import tpu as pltpu
from jax.sharding import Mesh, PartitionSpec as P

epsilon = 1e-06
NET = ("h", "c")
FSDP = ("z", "x", "y")
ROWS, CH, D, SHARD, PADDED = 512, 64, 2432, 38, 40
PIECE = 4 * PADDED
KDIM = 64 * PADDED
HALF = ROWS // 2
VM = pl.BlockSpec(memory_space=pltpu.VMEM)
SM = pl.BlockSpec(memory_space=pltpu.SMEM)
NT = (((1,), (1,)), ((), ()))
f32, bf16 = jnp.float32, jnp.bfloat16


def call(body, outs, scratch=(), smem=0, ins=0):
    return pl.pallas_call(
        body,
        out_shape=[jax.ShapeDtypeStruct(s, t) for s, t in outs],
        in_specs=[SM] * smem + [VM] * ins,
        out_specs=[VM] * len(outs),
        scratch_shapes=list(scratch),
        compiler_params=pltpu.CompilerParams(vmem_limit_bytes=28 * 1024 * 1024),
    )


def mm(a, b):
    return jnp.dot(a, b, preferred_element_type=f32)


def mm_nt(a, b):
    return lax.dot_general(a, b, NT, preferred_element_type=f32)


def unpack(v):
    return jnp.concatenate([v[:, :CH], v[:, CH:]], axis=0)


def pack(v):
    return jnp.concatenate([v[:HALF], v[HALF:]], axis=1)


def prep_body(where_ref, *refs):
    pieces, (full_ref, en_ref, fin_ref), wide = refs[:16], refs[16:19], refs[19]
    core, x, y = where_ref[0], where_ref[1], where_ref[2]
    for side in range(2):
        parity = core if side == 0 else 1 - core
        for part in range(2):
            z = 2 * part + parity
            for k in range(4):
                at_k = (side * 8 + part * 4 + k) * PIECE
                ref = pieces[side * 8 + part * 4 + k]

                def move(r, _, ref=ref, at_k=at_k):
                    at = pl.multiple_of(r * 16, 16)
                    full_ref[pl.ds(at_k + at, 16), :] = ref[pl.ds(at, 16), :]
                    return 0

                lax.fori_loop(0, PIECE // 16, move, 0)
                tail = ref[:, D:].astype(f32)
                for i in range(4):
                    xs = i if part == 0 else lax.rem(x + 4 - k, 4)
                    ys = lax.rem(y + 4 - k, 4) if part == 0 else i
                    at = ((z * 4 + xs) * 4 + ys) * PADDED
                    wide[pl.ds(pl.multiple_of(at, 8), PADDED), :] = tail[
                        i * PADDED : (i + 1) * PADDED
                    ]
    for d in range(64):
        wide[d * SHARD : (d + 1) * SHARD, :] = wide[d * PADDED : d * PADDED + SHARD, :]
    for at in range(0, D, 128):
        rows = wide[at : at + 128, :]
        en_ref[at : at + 128, :] = rows[:, :CH].astype(bf16)
        fin_ref[at : at + 128, :] = rows[:, CH:].astype(bf16)


def prep(where, pieces):
    return call(
        prep_body,
        [((KDIM, KDIM), bf16), ((D, CH), bf16), ((D, CH), bf16)],
        [pltpu.VMEM((KDIM, 2 * CH), f32)],
        1,
        16,
    )(where, *pieces)


def forward(rows, full_ref, en_ref, fin_ref, active, wide, normed, squares):
    def act(i, _):
        at = pl.multiple_of(i * 256, 256)
        hidden = mm_nt(rows, full_ref[pl.ds(at, 256), D : D + CH])
        active[:, pl.ds(at, 256)] = jax.nn.gelu(hidden).astype(bf16)
        return 0

    lax.fori_loop(0, KDIM // 256, act, 0)
    squares[...] = jnp.zeros((ROWS, 128), f32)

    def tile(at, size):
        total = mm(active[...], full_ref[:, pl.ds(at, size)])
        total += mm_nt(rows, en_ref[pl.ds(at, size), :])
        wide[:, pl.ds(at, size)] = total
        part = total[:, :128] * total[:, :128]
        if size > 128:
            part += total[:, 128:] * total[:, 128:]
        squares[...] += part

    def step(i, _):
        tile(pl.multiple_of(i * 256, 256), 256)
        return 0

    lax.fori_loop(0, 9, step, 0)
    tile(2304, 128)
    mean = jnp.sum(squares[...], axis=1, keepdims=True) / D
    factor = lax.rsqrt(mean + epsilon)
    squares[...] = jnp.broadcast_to(factor, (ROWS, 128))

    def scale(i, _):
        at = pl.multiple_of(i * 128, 128)
        normed[:, pl.ds(at, 128)] = (wide[:, pl.ds(at, 128)] * squares[...]).astype(bf16)
        return 0

    lax.fori_loop(0, D // 128, scale, 0)
    return mm(normed[...], fin_ref[...])


ACTIVE = pltpu.VMEM((ROWS, KDIM), bf16)
WIDE = pltpu.VMEM((ROWS, D), f32)
NORMED = pltpu.VMEM((ROWS, D), bf16)
SQUARES = pltpu.VMEM((ROWS, 128), f32)


def student_body(rows_ref, full_ref, en_ref, fin_ref, out_ref, active, wide, normed, squares):
    rows = unpack(rows_ref[...])
    projected = forward(rows, full_ref, en_ref, fin_ref, active, wide, normed, squares)
    out_ref[...] = pack((rows.astype(f32) + projected)).astype(bf16)


def student(rows, tables):
    return call(
        student_body, [((HALF, 128), bf16)], [ACTIVE, WIDE, NORMED, SQUARES], 0, 4
    )(rows, *tables)[0]


def second_body(sample_ref, renoise_ref, level_ref, text_ref, full_ref, en_ref, fin_ref, *refs):
    rows_ref, pred_ref, sums_ref, proj_ref, squares, normed, active, wide = refs
    level = level_ref[...]
    sample = sample_ref[...].astype(f32)
    packed = ((1.0 - level) * sample + level * renoise_ref[...].astype(f32)).astype(bf16)
    rows_ref[...] = packed
    rows = unpack(packed)
    projected = forward(rows, full_ref, en_ref, fin_ref, active, wide, normed, squares)
    proj_ref[...] = projected
    judged = rows.astype(f32) + projected
    pred = packed.astype(f32) - level * pack(judged)
    pred_ref[...] = pred
    spread = jnp.abs(sample - pred)
    for p in range(4):
        part = jnp.sum(spread[p * 64 : p * 64 + 64], axis=0, keepdims=True)
        for q, cut in ((p, part[:, :CH]), (p + 4, part[:, CH:])):
            pool = jnp.sum(judged[q * 64 : q * 64 + 64], axis=0, keepdims=True)
            sums_ref[q : q + 1, :] = jnp.concatenate([pool, cut], axis=1)
    sums_ref[8:16, :] = text_ref[...]


def second(sample, renoise, level, text, tables):
    return call(
        second_body,
        [
            ((HALF, 128), bf16),
            ((HALF, 128), f32),
            ((16, 128), f32),
            ((ROWS, CH), f32),
            ((ROWS, 128), f32),
            ((ROWS, D), bf16),
        ],
        [ACTIVE, WIDE],
        0,
        7,
    )(sample, renoise, level, text, *tables)


def pf_body(full_ref, en_ref, fin_ref, out_ref, ef_ref):
    def tile(i, _):
        at = pl.multiple_of(i * 256, 256)
        out_ref[pl.ds(at, 256), :] = mm(full_ref[pl.ds(at, 256), :D], fin_ref[...])
        return 0

    lax.fori_loop(0, KDIM // 256, tile, 0)
    ef_ref[...] = lax.dot_general(
        en_ref[...], fin_ref[...], (((0,), (0,)), ((), ())), preferred_element_type=f32
    )


def proj_final(tables):
    return call(pf_body, [((KDIM, CH), f32), ((CH, CH), f32)], (), 0, 3)(*tables)


CHUNKS = ((0, 3), (3, 3), (6, 2), (8, 2))


def back_body(base, tiles, rows_ref, normed_ref, full_ref, en_ref, sum_ref, out_ref, slope_ref):
    rows = unpack(rows_ref[...])
    if base == 0:
        out_ref[...] = mm(normed_ref[...], en_ref[...])
    else:
        out_ref[...] = sum_ref[...]

    def tile(i, _):
        at = pl.multiple_of(base * 256 + i * 256, 256)
        embed = full_ref[pl.ds(at, 256), D : D + CH]
        hidden = mm_nt(rows, embed)
        s = 0.7978845608028654
        square = hidden * hidden
        th = jnp.tanh(s * hidden * (1.0 + 0.044715 * square))
        slope = 0.5 * (1.0 + th) + (0.5 * s) * hidden * (1.0 - th * th) * (1.0 + 0.134145 * square)
        slope_ref[:, pl.ds(pl.multiple_of(i * 256, 256), 256)] = slope.astype(bf16)
        moved = mm_nt(normed_ref[...], full_ref[pl.ds(at, 256), :D]) * slope
        out_ref[...] += mm(moved.astype(bf16), embed)
        return 0

    lax.fori_loop(0, tiles, tile, 0)


def back_step(chunk, rows, normed, tables, total):
    base, tiles = chunk
    return call(
        lambda *refs: back_body(base, tiles, *refs),
        [((ROWS, CH), f32), ((ROWS, tiles * 256), bf16)],
        (),
        0,
        5,
    )(rows, normed, tables[0], tables[1], total)


def finish_body(sums_ref, full_ref, pf_ref, ef_ref, proj_ref, factor_ref, total_ref, *refs):
    slopes, out_ref, (carried, result) = refs[:4], refs[4], refs[5:]
    high = lax.Precision.HIGHEST
    pooled = sums_ref[:8, :CH] / 4096.0
    text = sums_ref[8:16, :CH]
    pooled_norm = jnp.sqrt(jnp.sum(pooled * pooled, axis=-1, keepdims=True) + epsilon)
    text_norm = jnp.sqrt(jnp.sum(text * text, axis=-1, keepdims=True) + epsilon)
    unit_pool = pooled / pooled_norm
    unit_text = text / text_norm
    reward = jnp.sum(unit_pool * unit_text, axis=-1, keepdims=True)
    cot = (unit_text - reward * unit_pool) / pooled_norm
    carried[...] = lax.dot_general(
        cot, pf_ref[...], NT, precision=high, preferred_element_type=f32
    )
    direct = lax.dot_general(cot, ef_ref[...], NT, precision=high, preferred_element_type=f32)

    def rows_of(v):
        return jnp.concatenate(
            [jnp.broadcast_to(v[p : p + 1], (64, v.shape[1])) for p in range(8)], axis=0
        )

    result[...] = rows_of(direct)
    for (base, tiles), ref in zip(CHUNKS, slopes):

        def tile(i, _, base=base, ref=ref):
            at = pl.multiple_of(base * 256 + i * 256, 256)
            local = pl.multiple_of(i * 256, 256)
            scaled = ref[:, pl.ds(local, 256)].astype(f32) * rows_of(carried[:, pl.ds(at, 256)])
            result[...] += mm(scaled.astype(bf16), full_ref[pl.ds(at, 256), D : D + CH])
            return 0

        lax.fori_loop(0, tiles, tile, 0)
    cot_rows = rows_of(cot)
    along = jnp.sum(cot_rows * proj_ref[...], axis=1, keepdims=True) / D
    out_ref[...] = pack(
        factor_ref[:, :CH] * (result[...] - along * total_ref[...]) + cot_rows
    )


def finish(sums, full, pf, ef, projected, factor, total, slopes):
    return call(
        finish_body,
        [((HALF, 128), f32)],
        [pltpu.VMEM((8, KDIM), f32), pltpu.VMEM((ROWS, CH), f32)],
        0,
        11,
    )(sums, full, pf, ef, projected, factor, total, *slopes)[0]


def shift(n, k):
    return [(i, (i + k) % n) for i in range(n)]


Z1 = [(0, 1), (1, 0), (2, 3), (3, 2)]
Z2 = [(0, 2), (2, 0), (1, 3), (3, 1)]
CORE = [(0, 1), (1, 0)]


def gather_axis(piece, axis):
    return [piece] + [lax.ppermute(piece, axis, shift(4, k)) for k in range(1, 4)]


def place(me, moved):
    out = jnp.zeros((4,) + moved[0].shape, moved[0].dtype)
    for k, piece in enumerate(moved):
        out = lax.dynamic_update_index_in_dim(out, piece, lax.rem(me - k + 4, 4), 0)
    return out.reshape((4 * moved[0].shape[0],) + moved[0].shape[1:])


def gather_weights(slab):
    core, z, x, y = (lax.axis_index(a) for a in ("c", "z", "x", "y"))
    swapped = lax.ppermute(slab, ("c", "z"), [(4, 1), (1, 4), (6, 3), (3, 6)])
    mine = jnp.where(core == lax.rem(z, 2), slab, swapped)
    far = lax.ppermute(mine, "z", Z2)
    part_a, part_b = jnp.where(z < 2, mine, far), jnp.where(z < 2, far, mine)
    part_a, part_b = lax.optimization_barrier((part_a, part_b))
    moved_a, moved_b = gather_axis(part_a, "x"), gather_axis(part_b, "y")
    moved_a, moved_b = lax.optimization_barrier((moved_a, moved_b))
    part_a, part_b = lax.optimization_barrier((place(x, moved_a), place(y, moved_b)))
    pieces = gather_axis(part_a, "y") + gather_axis(part_b, "x")
    near = [0, 4, 1, 3, 5, 7]
    ready = lax.optimization_barrier([pieces[i] for i in near])
    swaps = {i: lax.ppermute(v, "c", CORE) for i, v in zip(near, ready)}
    pieces = [ready[near.index(i)] if i in near else pieces[i] for i in range(8)]
    for i in (2, 6):
        swaps[i] = lax.ppermute(pieces[i], "c", CORE)
    return pieces + [swaps[i] for i in range(8)]


def packed_rows(block):
    flat = block.reshape(ROWS, CH)
    return jnp.concatenate([flat[:HALF], flat[HALF:]], axis=1)


def on_device(noise_in, renoise, timesteps, prompt_ids, embed_w, proj_w, final_w, text_table):
    h, core, z, x, y = (lax.axis_index(a) for a in NET + FSDP)
    parity = lax.rem(z, 2)
    slab = jnp.concatenate([proj_w[0], embed_w[0].T, final_w[0]], axis=1)
    slab = jnp.pad(slab, ((0, PADDED - SHARD), (0, 0)))
    pieces = gather_weights(slab)

    anchor, noise_in, renoise, prompt_ids = lax.optimization_barrier(
        (pieces[1], noise_in, renoise, prompt_ids)
    )
    pieces[1] = anchor
    both = jnp.concatenate([packed_rows(noise_in), packed_rows(renoise)], axis=0)
    other = lax.ppermute(both, "z", Z1)
    both = jnp.where(core == parity, both, other)
    noise, fresh = both[:HALF], both[HALF:]

    table_rows = text_table.shape[0]
    first_row = lax.axis_index(NET + FSDP) * table_rows
    offsets = prompt_ids - first_row
    matches = offsets[:, :, None] == jnp.arange(table_rows, dtype=jnp.int32)[None, None, :]
    counts = jnp.sum(matches.astype(f32), axis=1).astype(bf16)
    text = jnp.dot(counts, text_table, preferred_element_type=f32) / prompt_ids.shape[1]
    text = jnp.concatenate([text, jnp.zeros_like(text)], axis=1)
    text = text + lax.ppermute(text, "z", Z1)
    text = text + lax.ppermute(text, "h", CORE)

    judge = (h == 1) & (parity == 1)
    level = timesteps.astype(f32) / 1000.0
    level = jnp.where(judge, 0.0, level)
    level = jnp.broadcast_to(level[:, None, None], (8, 64, CH))
    level = packed_rows(level)

    where = jnp.stack([core, x, y]).astype(jnp.int32)
    tables = prep(where, pieces)
    sample = student(noise, tables)
    is_student = (h == 0) & (parity == 0)
    got = [
        lax.ppermute(sample, ("h", "z"), [(0, 5), (2, 7)]),
        lax.ppermute(sample, ("h", "z"), [(0, 4), (2, 6)]),
        lax.ppermute(sample, ("h", "z"), [(0, 1), (2, 3)]),
    ]
    sample, full, en, fin = lax.optimization_barrier((sample, *tables))
    pf, ef = proj_final((full, en, fin))
    got, sample, pf, text = lax.optimization_barrier((got, sample, pf, text))
    sample = jnp.where(
        is_student, sample, jnp.where(h == 0, got[2], jnp.where(parity == 1, got[0], got[1]))
    )
    rows, pred, sums, projected, factor, normed = second(sample, fresh, level, text, tables)

    real = lax.ppermute(pred, ("h", "z"), [(1, 5), (3, 7)])
    fake = lax.ppermute(pred, ("h", "z"), [(4, 5), (6, 7)])
    total = jnp.zeros((ROWS, CH), f32)
    slopes = []
    rounds = [[("c", CORE)], [("z", Z2)]] + [[(a, shift(4, k)) for k in (1, 2, 3)] for a in "xy"]
    for chunk, sends in zip(CHUNKS, rounds):
        sums, rows = lax.optimization_barrier((sums, rows))
        moved = [lax.ppermute(sums, axis, pairs) for axis, pairs in sends]
        total, slope = back_step(chunk, rows, normed, tables, total)
        total, moved = lax.optimization_barrier((total, moved))
        slopes.append(slope)
        sums = sum(moved, sums)
    absolute = lax.ppermute(sums[:8], ("h", "z"), [(1, 5), (3, 7)])
    reward = finish(sums, full, pf, ef, projected, factor, total, slopes)
    weight = jnp.sum(absolute[:, CH:], axis=1) / (4096.0 * CH)
    weight = 1.0 / (weight + epsilon)
    weight = packed_rows(jnp.broadcast_to(weight[:, None, None], (8, 64, CH)))
    result = weight * (fake - real) - reward
    landed = 0.0
    for to_h in range(2):
        for to_c in range(2):
            pairs = [
                (9 + 4 * c + 2 * q, 8 * to_h + 4 * to_c + 2 * q + c)
                for c in range(2)
                for q in range(2)
            ]
            landed = landed + lax.ppermute(result, NET + ("z",), pairs)
    out = jnp.concatenate([landed[:, :CH], landed[:, CH:]], axis=0)
    return out.reshape(8, 64, CH)


def solution(mesh):
    cube = Mesh(mesh.devices.reshape(2, 2, 4, 4, 4), NET + FSDP)
    placed = (
        P(None, FSDP, None),
        P(None, FSDP, None),
        P(),
        P(),
        P(NET, None, FSDP),
        P(NET, FSDP, None),
        P(NET, FSDP, None),
        P(NET + FSDP, None),
    )
    return jax.shard_map(
        on_device, mesh=cube, in_specs=placed, out_specs=P(None, FSDP, None), check_vma=False
    )
```

profile of v0, /device:TPU:35, one launch (start us, length us, event | category | flops | bytes accessed | tf_op | source)
XLA Modules:
  0.0 204.5 jit_solution(17755072038880272021)
XLA Ops:
  0.0 1.0 concatenate.24
  1.1 0.7 collective-permute-start
  1.8 3.1 %collective-permute-start.1 = (bf16[40,2560]{1,0:T(8,128)(2,1)S(1)}, bf16[40,2560]{1,0:T(8,128)(2,1)S(1)}, u32[]{:S(2)}, u32[]{:S(2)}) collective-permute-start(bf16[40,2560]{1,0:T(8,128)(2,1)S(1)} %broadcast_select_fusion), channel_id=1, source_target_pairs={{0,32},{32,0},{16,48},{48,16},{1,33},{33,1},{17,49},{49,17},{2,34}... | collective-permute-start | bytes 614408 | tf_op jit(solution)/shard_map/ppermute | solution.py:311
  4.9 4.9 %collective-permute-done.1 = bf16[40,2560]{1,0:T(8,128)(2,1)S(1)} collective-permute-done((bf16[40,2560]{1,0:T(8,128)(2,1)S(1)}, bf16[40,2560]{1,0:T(8,128)(2,1)S(1)}, u32[]{:S(2)}, u32[]{:S(2)}) %collective-permute-start.1) | collective-permute-done | bytes 204832 | tf_op jit(solution)/shard_map/ppermute | solution.py:311
  9.8 1.3 collective-permute-start.2
  11.1 0.8 collective-permute-start.3
  12.0 1.9 collective-permute-start.4
  13.8 1.3 collective-permute-start.5
  15.1 2.6 %collective-permute-start.6 = (bf16[40,2560]{1,0:T(8,128)(2,1)S(1)}, bf16[40,2560]{1,0:T(8,128)(2,1)S(1)}, u32[]{:S(2)}, u32[]{:S(2)}) collective-permute-start(bf16[40,2560]{1,0:T(8,128)(2,1)S(1)} %get-tuple-element.82), channel_id=1, source_target_pairs={{0,2},{1,3},{2,0},{3,1},{4,6},{5,7},{6,4},{7,5},{8,10},{9,11},{10,... | collective-permute-start | bytes 614408 | tf_op jit(solution)/shard_map/ppermute | solution.py:297
  17.8 1.1 collective-permute-start.7
  18.8 0.9 collective-permute-done.5
  19.7 3.4 %collective-permute-done.6 = bf16[40,2560]{1,0:T(8,128)(2,1)S(1)} collective-permute-done((bf16[40,2560]{1,0:T(8,128)(2,1)S(1)}, bf16[40,2560]{1,0:T(8,128)(2,1)S(1)}, u32[]{:S(2)}, u32[]{:S(2)}) %collective-permute-start.6) | collective-permute-done | bytes 204832 | tf_op jit(solution)/shard_map/ppermute | solution.py:297
  23.5 1.5 collective-permute-start.11
  25.0 1.0 collective-permute-start.8
  26.0 1.7 collective-permute-start.9
  27.7 1.4 collective-permute-start.13
  29.0 5.9 %collective-permute-done.10.refs_5_ = bf16[160,2560]{1,0:T(8,128)(2,1)S(1)} collective-permute-done((bf16[160,2560]{1,0:T(8,128)(2,1)S(1)}, bf16[160,2560]{1,0:T(8,128)(2,1)S(1)}, u32[]{:S(2)}, u32[]{:S(2)}) %collective-permute-start.10) | collective-permute-done | bytes 819232 | tf_op jit(solution)/shard_map/ppermute | solution.py:297
  35.0 0.8 collective-permute-start.14
  36.1 3.6 %collective-permute-done.8.refs_1_ = bf16[160,2560]{1,0:T(8,128)(2,1)} collective-permute-done((bf16[160,2560]{1,0:T(8,128)(2,1)S(1)}, bf16[160,2560]{1,0:T(8,128)(2,1)}, u32[]{:S(2)}, u32[]{:S(2)}) %collective-permute-start.8) | collective-permute-done | bytes 819232 | tf_op jit(solution)/shard_map/ppermute | solution.py:297
  39.7 1.0 collective-permute-done.9.refs_3_
  40.7 18.3 %collective-permute-start.16 = (bf16[160,2560]{1,0:T(8,128)(2,1)}, bf16[160,2560]{1,0:T(8,128)(2,1)}, u32[]{:S(2)}, u32[]{:S(2)}) collective-permute-start(bf16[160,2560]{1,0:T(8,128)(2,1)} %collective-permute-done.8.refs_1_), channel_id=1, source_target_pairs={{0,64},{64,0},{1,65},{65,1},{2,66},{66,2},{3,67},{67,3},{4,68},{68... | collective-permute-start | bytes 2457608 | tf_op jit(solution)/shard_map/ppermute | solution.py:320
  59.4 0.5 collective-permute-start.18
  60.2 11.5 %collective-permute-start.26 = (f32[8,128]{1,0:T(8,128)S(1)}, f32[8,128]{1,0:T(8,128)S(1)}, u32[]{:S(2)}, u32[]{:S(2)}) collective-permute-start(f32[8,128]{1,0:T(8,128)S(1)} %concatenate.28), channel_id=1, source_target_pairs={{0,16},{16,0},{32,48},{48,32},{1,17},{17,1},{33,49},{49,33},{2,18}... | collective-permute-start | bytes 12296 | tf_op jit(solution)/shard_map/ppermute | solution.py:355
  71.8 1.0 collective-permute-done.26
  72.7 1.7 collective-permute-start.19
  74.5 1.1 collective-permute-done.12
  75.5 2.3 %collective-permute-start.20 = (bf16[160,2560]{1,0:T(8,128)(2,1)S(1)}, bf16[160,2560]{1,0:T(8,128)(2,1)}, u32[]{:S(2)}, u32[]{:S(2)}) collective-permute-start(bf16[160,2560]{1,0:T(8,128)(2,1)S(1)} %collective-permute-done.10.refs_5_), channel_id=1, source_target_pairs={{0,64},{64,0},{1,65},{65,1},{2,66},{66,2},{3,67},{67,3},{4,68},{68... | collective-permute-start | bytes 2457608 | tf_op jit(solution)/shard_map/ppermute | solution.py:320
  77.9 0.9 copy-done.5
  78.8 0.5 collective-permute-start.17
  79.3 0.9 copy-done.7
  80.8 4.0 %collective-permute-start.27 = (f32[8,128]{1,0:T(8,128)S(1)}, f32[8,128]{1,0:T(8,128)S(1)}, u32[]{:S(2)}, u32[]{:S(2)}) collective-permute-start(f32[8,128]{1,0:T(8,128)S(1)} %pad_add_fusion.1), channel_id=1, source_target_pairs={{0,128},{128,0},{1,129},{129,1},{2,130},{130,2},{3,131},{131,3},{4... | collective-permute-start | bytes 12296 | tf_op jit(solution)/shard_map/ppermute | solution.py:356
  84.8 1.1 copy-done.4
  86.0 1.1 copy-done.6
  87.1 1.1 copy-done.8
  88.3 9.9 %shard_map.82 = (bf16[2560,2560]{1,0:T(8,128)(2,1)}, bf16[2432,64]{1,0:T(8,128)(2,1)S(1)}, bf16[2432,64]{1,0:T(8,128)(2,1)S(1)}) custom-call(s32[3]{0:T(128)S(1)} %pad_add_fusion.where_ref, bf16[160,2560]{1,0:T(8,128)(2,1)S(1)} %bitcast.42, bf16[160,2560]{1,0:T(8,128)(2,1)} %collective-permute-done.8.refs_1_, ...), custom_call_target="tpu_custom_call" | custom-call | tf_op jit(solution)/shard_map/pallas_call | solution.py:82
  98.1 4.7 %copy-done.1 = bf16[2560,2560]{1,0:T(8,128)(2,1)S(1)} copy-done((bf16[2560,2560]{1,0:T(8,128)(2,1)S(1)}, bf16[2560,2560]{1,0:T(8,128)(2,1)}, u32[]{:S(2)}) %copy-start.1) | copy-done | bytes 13107224
  102.9 15.4 %shard_map.83 = bf16[256,128]{1,0:T(8,128)(2,1)S(1)} custom-call(bf16[256,128]{1,0:T(8,128)(2,1)S(1)} %get-tuple-element.152.rows_ref, bf16[2560,2560]{1,0:T(8,128)(2,1)S(1)} %copy-done.1, bf16[2432,64]{1,0:T(8,128)(2,1)S(1)} %get-tuple-element.102.en_ref.refs_3_, bf16[2432,64]{1,0:T(8,128)(2,1)S(1)} %get-tuple-element.103.fin_ref), custom_call_target="tpu_custom_call" | custom-call | tf_op jit(solution)/shard_map/pallas_call | solution.py:142
  118.2 0.7 collective-permute-start.23
  118.9 0.7 collective-permute-start.24
  119.6 1.3 collective-permute-start.25
  121.2 4.7 %copy-done.2 = bf16[2560,2560]{1,0:T(8,128)(2,1)S(1)} copy-done((bf16[2560,2560]{1,0:T(8,128)(2,1)S(1)}, bf16[2560,2560]{1,0:T(8,128)(2,1)}, u32[]{:S(2)}) %copy-start.2) | copy-done | bytes 13107224
  126.0 5.1 %shard_map.84 = (f32[2560,64]{1,0:T(8,128)S(1)}, f32[64,64]{1,0:T(8,128)S(1)}) custom-call(bf16[2560,2560]{1,0:T(8,128)(2,1)S(1)} %copy-done.2, bf16[2432,64]{1,0:T(8,128)(2,1)S(1)} %get-tuple-element.102.en_ref.refs_3_, bf16[2432,64]{1,0:T(8,128)(2,1)S(1)} %get-tuple-element.103.fin_ref), custom_call_target="tpu_custom_call" | custom-call | tf_op jit(solution)/shard_map/pallas_call | solution.py:198
  131.2 15.5 %shard_map.85 = (bf16[256,128]{1,0:T(8,128)(2,1)S(1)}, f32[256,128]{1,0:T(8,128)S(1)}, f32[16,128]{1,0:T(8,128)S(1)}, f32[512,64]{1,0:T(8,128)S(1)}, f32[512,128...) custom-call(bf16[256,128]{1,0:T(8,128)(2,1)S(1)} %select_select_fusion.sample_ref, ...), custom_call_target="tpu_custom_call" | custom-call | tf_op jit(solution)/shard_map/pallas_call | solution.py:169
  146.6 1.0 collective-permute-start.28
  147.7 4.3 %shard_map.86 = (f32[512,64]{1,0:T(8,128)S(1)}, bf16[512,768]{1,0:T(8,128)(2,1)S(1)}) custom-call(bf16[256,128]{1,0:T(8,128)(2,1)S(1)} %get-tuple-element.131.refs_0_, bf16[512,2432]{1,0:T(8,128)(2,1)S(1)} %get-tuple-element.115.refs_1_, bf16[2560,2560]{1,0:T(8,128)(2,1)S(1)} %copy-done.2, bf16[2432,64]{1,0:T(8,128)(2,1)S(1)} %get-tuple-element.102.en_ref.refs_3_, ...), custom_call_target="tpu_custom_call" | custom-call | tf_op jit(solution)/shard_map/pallas_call | solution.py:229
  152.0 2.0 collective-permute-start.29
  154.1 3.6 %shard_map.87 = (f32[512,64]{1,0:T(8,128)S(1)}, bf16[512,768]{1,0:T(8,128)(2,1)S(1)}) custom-call(bf16[256,128]{1,0:T(8,128)(2,1)S(1)} %get-tuple-element.131.refs_0_, bf16[512,2432]{1,0:T(8,128)(2,1)S(1)} %get-tuple-element.115.refs_1_, bf16[2560,2560]{1,0:T(8,128)(2,1)S(1)} %copy-done.2, bf16[2432,64]{1,0:T(8,128)(2,1)S(1)} %get-tuple-element.102.en_ref.refs_3_, ...), custom_call_target="tpu_custom_call" | custom-call | tf_op jit(solution)/shard_map/pallas_call | solution.py:229
  157.7 1.3 collective-permute-start.30
  159.0 3.9 %collective-permute-start.31 = (f32[16,128]{1,0:T(8,128)S(1)}, f32[16,128]{1,0:T(8,128)S(1)}, u32[]{:S(2)}, u32[]{:S(2)}) collective-permute-start(f32[16,128]{1,0:T(8,128)S(1)} %add.156), channel_id=1, source_target_pairs={{0,8},{4,12},{8,0},{12,4},{1,9},{5,13},{9,1},{13,5},{2,10},{6,14},... | collective-permute-start | bytes 24584 | tf_op jit(solution)/shard_map/ppermute | solution.py:388
  162.8 2.4 %shard_map.88 = (f32[512,64]{1,0:T(8,128)S(1)}, bf16[512,512]{1,0:T(8,128)(2,1)S(1)}) custom-call(bf16[256,128]{1,0:T(8,128)(2,1)S(1)} %get-tuple-element.131.refs_0_, bf16[512,2432]{1,0:T(8,128)(2,1)S(1)} %get-tuple-element.115.refs_1_, bf16[2560,2560]{1,0:T(8,128)(2,1)S(1)} %copy-done.2, bf16[2432,64]{1,0:T(8,128)(2,1)S(1)} %get-tuple-element.102.en_ref.refs_3_, ...), custom_call_target="tpu_custom_call" | custom-call | tf_op jit(solution)/shard_map/pallas_call | solution.py:229
  165.3 2.7 %collective-permute-start.33 = (f32[16,128]{1,0:T(8,128)S(1)}, f32[16,128]{1,0:T(8,128)S(1)}, u32[]{:S(2)}, u32[]{:S(2)}) collective-permute-start(f32[16,128]{1,0:T(8,128)S(1)} %add_add_fusion.2), channel_id=1, source_target_pairs={{0,1},{1,2},{2,3},{3,0},{4,5},{5,6},{6,7},{7,4},{8,9},{9,10},{10,1... | collective-permute-start | bytes 24584 | tf_op jit(solution)/shard_map/ppermute | solution.py:388
  168.0 1.5 collective-permute-start.34
  169.5 1.0 collective-permute-start.35
  170.5 2.4 %shard_map.89 = (f32[512,64]{1,0:T(8,128)S(1)}, bf16[512,512]{1,0:T(8,128)(2,1)S(1)}) custom-call(bf16[256,128]{1,0:T(8,128)(2,1)S(1)} %get-tuple-element.131.refs_0_, bf16[512,2432]{1,0:T(8,128)(2,1)S(1)} %get-tuple-element.115.refs_1_, bf16[2560,2560]{1,0:T(8,128)(2,1)S(1)} %copy-done.2, bf16[2432,64]{1,0:T(8,128)(2,1)S(1)} %get-tuple-element.102.en_ref.refs_3_, ...), custom_call_target="tpu_custom_call" | custom-call | tf_op jit(solution)/shard_map/pallas_call | solution.py:229
  173.0 4.2 %collective-permute-start.36 = (f32[8,128]{1,0:T(8,128)S(1)}, f32[8,128]{1,0:T(8,128)S(1)}, u32[]{:S(2)}, u32[]{:S(2)}) collective-permute-start(f32[8,128]{1,0:T(8,128)S(1)} %slice.86), channel_id=1, source_target_pairs={{16,144},{48,176},{17,145},{49,177},{18,146},{50,178},{19,147},{51... | collective-permute-start | bytes 12296 | tf_op jit(solution)/shard_map/ppermute | solution.py:393
  177.2 0.7 collective-permute-start.37
  177.9 1.9 collective-permute-start.38
  179.8 3.9 %shard_map.90 = f32[256,128]{1,0:T(8,128)S(1)} custom-call(f32[16,128]{1,0:T(8,128)S(1)} %add_add_fusion.1.sums_ref, bf16[2560,2560]{1,0:T(8,128)(2,1)S(1)} %copy-done.2, f32[2560,64]{1,0:T(8,128)S(1)} %get-tuple-element.138.pf_ref, f32[64,64]{1,0:T(8,128)S(1)} %get-tuple-element.139.ef_ref, f32[512,64]{1,0:T(8,128)S(1)} %get-tuple-element.140.proj_ref, ...), custom_call_target="tpu_custom_call" | custom-call | tf_op jit(solution)/shard_map/pallas_call | solution.py:278
  184.6 0.7 collective-permute-start.39
  185.3 1.3 collective-permute-start.40
  186.6 0.7 collective-permute-start.41
  187.3 0.7 collective-permute-start.42
  188.0 15.7 %collective-permute-done.40 = f32[256,128]{1,0:T(8,128)S(1)} collective-permute-done((f32[256,128]{1,0:T(8,128)S(1)}, f32[256,128]{1,0:T(8,128)S(1)}, u32[]{:S(2)}, u32[]{:S(2)}) %collective-permute-start.40) | collective-permute-done | bytes 131104 | tf_op jit(solution)/shard_map/ppermute | solution.py:407
  203.8 0.7 pad_maximum_fusion
  (112 shorter events, 3.6 us)
Async XLA Ops:
  0.0 59.9 %copy-start = (bf16[193,64]{0,1:T(8,128)(2,1)S(1)}, bf16[193,64]{0,1:T(8,128)(2,1)}, u32[]{:S(2)}) copy-start(bf16[193,64]{0,1:T(8,128)(2,1)} %param.15) | copy-start | bytes 74116
  1.1 0.7 collective-permute-start
  1.8 8.0 %collective-permute-start.1 = (bf16[40,2560]{1,0:T(8,128)(2,1)S(1)}, bf16[40,2560]{1,0:T(8,128)(2,1)S(1)}, u32[]{:S(2)}, u32[]{:S(2)}) collective-permute-start(bf16[40,2560]{1,0:T(8,128)(2,1)S(1)} %broadcast_select_fusion), channel_id=1, source_target_pairs={{0,32},{32,0},{16,48},{48,16},{1,33},{33,1},{17,49},{49,17},{2,34}... | collective-permute-start | bytes 614408 | tf_op jit(solution)/shard_map/ppermute | solution.py:311
  9.8 7.9 %collective-permute-start.2 = (bf16[40,2560]{1,0:T(8,128)(2,1)S(1)}, bf16[40,2560]{1,0:T(8,128)(2,1)S(1)}, u32[]{:S(2)}, u32[]{:S(2)}) collective-permute-start(bf16[40,2560]{1,0:T(8,128)(2,1)S(1)} %get-tuple-element.78), channel_id=1, source_target_pairs={{0,4},{4,8},{8,12},{12,0},{1,5},{5,9},{9,13},{13,1},{2,6},{6,10},{... | collective-permute-start | bytes 614408 | tf_op jit(solution)/shard_map/ppermute | solution.py:297
  11.1 7.7 %collective-permute-start.3 = (bf16[40,2560]{1,0:T(8,128)(2,1)S(1)}, bf16[40,2560]{1,0:T(8,128)(2,1)S(1)}, u32[]{:S(2)}, u32[]{:S(2)}) collective-permute-start(bf16[40,2560]{1,0:T(8,128)(2,1)S(1)} %get-tuple-element.78), channel_id=1, source_target_pairs={{0,8},{4,12},{8,0},{12,4},{1,9},{5,13},{9,1},{13,5},{2,10},{6,14},... | collective-permute-start | bytes 614408 | tf_op jit(solution)/shard_map/ppermute | solution.py:297
  12.0 6.9 %collective-permute-start.4 = (bf16[40,2560]{1,0:T(8,128)(2,1)S(1)}, bf16[40,2560]{1,0:T(8,128)(2,1)S(1)}, u32[]{:S(2)}, u32[]{:S(2)}) collective-permute-start(bf16[40,2560]{1,0:T(8,128)(2,1)S(1)} %get-tuple-element.78), channel_id=1, source_target_pairs={{0,12},{4,0},{8,4},{12,8},{1,13},{5,1},{9,5},{13,9},{2,14},{6,2},{... | collective-permute-start | bytes 614408 | tf_op jit(solution)/shard_map/ppermute | solution.py:297
  13.8 5.9 %collective-permute-start.5 = (bf16[40,2560]{1,0:T(8,128)(2,1)S(1)}, bf16[40,2560]{1,0:T(8,128)(2,1)S(1)}, u32[]{:S(2)}, u32[]{:S(2)}) collective-permute-start(bf16[40,2560]{1,0:T(8,128)(2,1)S(1)} %get-tuple-element.82), channel_id=1, source_target_pairs={{0,1},{1,2},{2,3},{3,0},{4,5},{5,6},{6,7},{7,4},{8,9},{9,10},{10,1... | collective-permute-start | bytes 614408 | tf_op jit(solution)/shard_map/ppermute | solution.py:297
  15.1 8.0 %collective-permute-start.6 = (bf16[40,2560]{1,0:T(8,128)(2,1)S(1)}, bf16[40,2560]{1,0:T(8,128)(2,1)S(1)}, u32[]{:S(2)}, u32[]{:S(2)}) collective-permute-start(bf16[40,2560]{1,0:T(8,128)(2,1)S(1)} %get-tuple-element.82), channel_id=1, source_target_pairs={{0,2},{1,3},{2,0},{3,1},{4,6},{5,7},{6,4},{7,5},{8,10},{9,11},{10,... | collective-permute-start | bytes 614408 | tf_op jit(solution)/shard_map/ppermute | solution.py:297
  17.8 5.3 %collective-permute-start.7 = (bf16[40,2560]{1,0:T(8,128)(2,1)S(1)}, bf16[40,2560]{1,0:T(8,128)(2,1)S(1)}, u32[]{:S(2)}, u32[]{:S(2)}) collective-permute-start(bf16[40,2560]{1,0:T(8,128)(2,1)S(1)} %get-tuple-element.82), channel_id=1, source_target_pairs={{0,3},{1,0},{2,1},{3,2},{4,7},{5,4},{6,5},{7,6},{8,11},{9,8},{10,9... | collective-permute-start | bytes 614408 | tf_op jit(solution)/shard_map/ppermute | solution.py:297
  18.8 40.2 %copy-start.11 = (s32[8,77]{1,0:T(8,128)S(1)}, s32[8,77]{1,0:T(8,128)}, u32[]{:S(2)}) copy-start(s32[8,77]{1,0:T(8,128)} %param.11) | copy-start | bytes 7396
  18.8 41.2 %copy-start.9 = (bf16[8,64,64]{2,1,0:T(8,128)(2,1)S(1)}, bf16[8,64,64]{2,1,0:T(8,128)(2,1)}, u32[]{:S(2)}) copy-start(bf16[8,64,64]{2,1,0:T(8,128)(2,1)} %param.8) | copy-start | bytes 196612
  18.8 41.2 %copy-start.10 = (bf16[8,64,64]{2,1,0:T(8,128)(2,1)S(1)}, bf16[8,64,64]{2,1,0:T(8,128)(2,1)}, u32[]{:S(2)}) copy-start(bf16[8,64,64]{2,1,0:T(8,128)(2,1)} %param.9) | copy-start | bytes 196612
  23.2 48.6 %copy-start.12 = (s32[8]{0:T(128)S(1)}, s32[8]{0:T(128)}, u32[]{:S(2)}) copy-start(s32[8]{0:T(128)} %param.10) | copy-start | bytes 100
  23.5 11.5 %collective-permute-start.10 = (bf16[160,2560]{1,0:T(8,128)(2,1)S(1)}, bf16[160,2560]{1,0:T(8,128)(2,1)S(1)}, u32[]{:S(2)}, u32[]{:S(2)}) collective-permute-start(bf16[160,2560]{1,0:T(8,128)(2,1)S(1)} %bitcast.33), channel_id=1, source_target_pairs={{0,4},{4,8},{8,12},{12,0},{1,5},{5,9},{9,13},{13,1},{2,6},{6,10},{... | collective-permute-start | bytes 2457608 | tf_op jit(solution)/shard_map/ppermute | solution.py:297
  23.5 12.6 %collective-permute-start.11 = (bf16[160,2560]{1,0:T(8,128)(2,1)S(1)}, bf16[160,2560]{1,0:T(8,128)(2,1)}, u32[]{:S(2)}, u32[]{:S(2)}) collective-permute-start(bf16[160,2560]{1,0:T(8,128)(2,1)S(1)} %bitcast.34), channel_id=1, source_target_pairs={{0,12},{4,0},{8,4},{12,8},{1,13},{5,1},{9,5},{13,9},{2,14},{6,2},{... | collective-permute-start | bytes 2457608 | tf_op jit(solution)/shard_map/ppermute | solution.py:297
  25.0 14.7 %collective-permute-start.8 = (bf16[160,2560]{1,0:T(8,128)(2,1)S(1)}, bf16[160,2560]{1,0:T(8,128)(2,1)}, u32[]{:S(2)}, u32[]{:S(2)}) collective-permute-start(bf16[160,2560]{1,0:T(8,128)(2,1)S(1)} %bitcast.38), channel_id=1, source_target_pairs={{0,1},{1,2},{2,3},{3,0},{4,5},{5,6},{6,7},{7,4},{8,9},{9,10},{10,1... | collective-permute-start | bytes 2457608 | tf_op jit(solution)/shard_map/ppermute | solution.py:297
  26.0 14.7 %collective-permute-start.9 = (bf16[160,2560]{1,0:T(8,128)(2,1)S(1)}, bf16[160,2560]{1,0:T(8,128)(2,1)}, u32[]{:S(2)}, u32[]{:S(2)}) collective-permute-start(bf16[160,2560]{1,0:T(8,128)(2,1)S(1)} %bitcast.39), channel_id=1, source_target_pairs={{0,3},{1,0},{2,1},{3,2},{4,7},{5,4},{6,5},{7,6},{8,11},{9,8},{10,9... | collective-permute-start | bytes 2457608 | tf_op jit(solution)/shard_map/ppermute | solution.py:297
  27.7 32.5 %collective-permute-start.13 = (bf16[160,2560]{1,0:T(8,128)(2,1)S(1)}, bf16[160,2560]{1,0:T(8,128)(2,1)}, u32[]{:S(2)}, u32[]{:S(2)}) collective-permute-start(bf16[160,2560]{1,0:T(8,128)(2,1)S(1)} %bitcast.40), channel_id=1, source_target_pairs={{0,2},{1,3},{2,0},{3,1},{4,6},{5,7},{6,4},{7,5},{8,10},{9,11},{10,... | collective-permute-start | bytes 2457608 | tf_op jit(solution)/shard_map/ppermute | solution.py:297
  35.0 49.8 %copy-start.3 = (bf16[160,2560]{1,0:T(8,128)(2,1)}, bf16[160,2560]{1,0:T(8,128)(2,1)S(1)}, u32[]{:S(2)}) copy-start(bf16[160,2560]{1,0:T(8,128)(2,1)S(1)} %collective-permute-done.10.refs_5_) | copy-start | bytes 2457604
  35.0 36.7 %collective-permute-start.14 = (bf16[160,2560]{1,0:T(8,128)(2,1)S(1)}, bf16[160,2560]{1,0:T(8,128)(2,1)}, u32[]{:S(2)}, u32[]{:S(2)}) collective-permute-start(bf16[160,2560]{1,0:T(8,128)(2,1)S(1)} %bitcast.35), channel_id=1, source_target_pairs={{0,8},{4,12},{8,0},{12,4},{1,9},{5,13},{9,1},{13,5},{2,10},{6,14},... | collective-permute-start | bytes 2457608 | tf_op jit(solution)/shard_map/ppermute | solution.py:297
  40.7 38.1 %collective-permute-start.16 = (bf16[160,2560]{1,0:T(8,128)(2,1)}, bf16[160,2560]{1,0:T(8,128)(2,1)}, u32[]{:S(2)}, u32[]{:S(2)}) collective-permute-start(bf16[160,2560]{1,0:T(8,128)(2,1)} %collective-permute-done.8.refs_1_), channel_id=1, source_target_pairs={{0,64},{64,0},{1,65},{65,1},{2,66},{66,2},{3,67},{67,3},{4,68},{68... | collective-permute-start | bytes 2457608 | tf_op jit(solution)/shard_map/ppermute | solution.py:320
  59.3 18.6 %collective-permute-start.15 = (bf16[160,2560]{1,0:T(8,128)(2,1)S(1)}, bf16[160,2560]{1,0:T(8,128)(2,1)S(1)}, u32[]{:S(2)}, u32[]{:S(2)}) collective-permute-start(bf16[160,2560]{1,0:T(8,128)(2,1)S(1)} %bitcast.41), channel_id=1, source_target_pairs={{0,64},{64,0},{1,65},{65,1},{2,66},{66,2},{3,67},{67,3},{4,68},{68... | collective-permute-start | bytes 2457608 | tf_op jit(solution)/shard_map/ppermute | solution.py:320
  59.4 19.9 %collective-permute-start.18 = (bf16[160,2560]{1,0:T(8,128)(2,1)}, bf16[160,2560]{1,0:T(8,128)(2,1)S(1)}, u32[]{:S(2)}, u32[]{:S(2)}) collective-permute-start(bf16[160,2560]{1,0:T(8,128)(2,1)} %collective-permute-done.9.refs_3_), channel_id=1, source_target_pairs={{0,64},{64,0},{1,65},{65,1},{2,66},{66,2},{3,67},{67,3},{4,68},{68... | collective-permute-start | bytes 2457608 | tf_op jit(solution)/shard_map/ppermute | solution.py:320
  60.2 12.5 %collective-permute-start.26 = (f32[8,128]{1,0:T(8,128)S(1)}, f32[8,128]{1,0:T(8,128)S(1)}, u32[]{:S(2)}, u32[]{:S(2)}) collective-permute-start(f32[8,128]{1,0:T(8,128)S(1)} %concatenate.28), channel_id=1, source_target_pairs={{0,16},{16,0},{32,48},{48,32},{1,17},{17,1},{33,49},{49,33},{2,18}... | collective-permute-start | bytes 12296 | tf_op jit(solution)/shard_map/ppermute | solution.py:355
  71.7 3.8 %collective-permute-start.12 = (bf16[512,128]{1,0:T(8,128)(2,1)S(1)}, bf16[512,128]{1,0:T(8,128)(2,1)S(1)}, u32[]{:S(2)}, u32[]{:S(2)}) collective-permute-start(bf16[512,128]{1,0:T(8,128)(2,1)S(1)} %maximum_maximum_fusion), channel_id=1, source_target_pairs={{0,16},{16,0},{32,48},{48,32},{1,17},{17,1},{33,49},{49,33},{2,18}... | collective-permute-start | bytes 393224 | tf_op jit(solution)/shard_map/ppermute | solution.py:344
  72.7 8.1 %collective-permute-start.19 = (bf16[160,2560]{1,0:T(8,128)(2,1)S(1)}, bf16[160,2560]{1,0:T(8,128)(2,1)}, u32[]{:S(2)}, u32[]{:S(2)}) collective-permute-start(bf16[160,2560]{1,0:T(8,128)(2,1)S(1)} %bitcast.36), channel_id=1, source_target_pairs={{0,64},{64,0},{1,65},{65,1},{2,66},{66,2},{3,67},{67,3},{4,68},{68... | collective-permute-start | bytes 2457608 | tf_op jit(solution)/shard_map/ppermute | solution.py:320
  75.5 9.2 %collective-permute-start.20 = (bf16[160,2560]{1,0:T(8,128)(2,1)S(1)}, bf16[160,2560]{1,0:T(8,128)(2,1)}, u32[]{:S(2)}, u32[]{:S(2)}) collective-permute-start(bf16[160,2560]{1,0:T(8,128)(2,1)S(1)} %collective-permute-done.10.refs_5_), channel_id=1, source_target_pairs={{0,64},{64,0},{1,65},{65,1},{2,66},{66,2},{3,67},{67,3},{4,68},{68... | collective-permute-start | bytes 2457608 | tf_op jit(solution)/shard_map/ppermute | solution.py:320
  77.9 0.9 copy-start.5
  78.8 6.0 %collective-permute-start.22 = (bf16[160,2560]{1,0:T(8,128)(2,1)}, bf16[160,2560]{1,0:T(8,128)(2,1)}, u32[]{:S(2)}, u32[]{:S(2)}) collective-permute-start(bf16[160,2560]{1,0:T(8,128)(2,1)} %collective-permute-done.11.refs_7_), channel_id=1, source_target_pairs={{0,64},{64,0},{1,65},{65,1},{2,66},{66,2},{3,67},{67,3},{4,68},{68... | collective-permute-start | bytes 2457608 | tf_op jit(solution)/shard_map/ppermute | solution.py:320
  78.8 6.0 %collective-permute-start.17 = (bf16[160,2560]{1,0:T(8,128)(2,1)}, bf16[160,2560]{1,0:T(8,128)(2,1)}, u32[]{:S(2)}, u32[]{:S(2)}) collective-permute-start(bf16[160,2560]{1,0:T(8,128)(2,1)} %collective-permute-done.13.refs_2_), channel_id=1, source_target_pairs={{0,64},{64,0},{1,65},{65,1},{2,66},{66,2},{3,67},{67,3},{4,68},{68... | collective-permute-start | bytes 2457608 | tf_op jit(solution)/shard_map/ppermute | solution.py:323
  79.3 0.9 copy-start.7
  80.2 4.6 %collective-permute-start.21 = (bf16[160,2560]{1,0:T(8,128)(2,1)}, bf16[160,2560]{1,0:T(8,128)(2,1)}, u32[]{:S(2)}, u32[]{:S(2)}) collective-permute-start(bf16[160,2560]{1,0:T(8,128)(2,1)} %collective-permute-done.14.refs_6_), channel_id=1, source_target_pairs={{0,64},{64,0},{1,65},{65,1},{2,66},{66,2},{3,67},{67,3},{4,68},{68... | collective-permute-start | bytes 2457608 | tf_op jit(solution)/shard_map/ppermute | solution.py:323
  80.8 40.4 %collective-permute-start.27 = (f32[8,128]{1,0:T(8,128)S(1)}, f32[8,128]{1,0:T(8,128)S(1)}, u32[]{:S(2)}, u32[]{:S(2)}) collective-permute-start(f32[8,128]{1,0:T(8,128)S(1)} %pad_add_fusion.1), channel_id=1, source_target_pairs={{0,128},{128,0},{1,129},{129,1},{2,130},{130,2},{3,131},{131,3},{4... | collective-permute-start | bytes 12296 | tf_op jit(solution)/shard_map/ppermute | solution.py:356
  84.8 1.1 copy-start.4
  86.0 1.1 copy-start.6
  87.1 1.1 copy-start.8
  98.1 4.7 %copy-start.1 = (bf16[2560,2560]{1,0:T(8,128)(2,1)S(1)}, bf16[2560,2560]{1,0:T(8,128)(2,1)}, u32[]{:S(2)}) copy-start(bf16[2560,2560]{1,0:T(8,128)(2,1)} %get-tuple-element.101.full_ref.refs_2_) | copy-start | bytes 39321604
  118.2 12.9 %collective-permute-start.23 = (bf16[256,128]{1,0:T(8,128)(2,1)S(1)}, bf16[256,128]{1,0:T(8,128)(2,1)S(1)}, u32[]{:S(2)}, u32[]{:S(2)}) collective-permute-start(bf16[256,128]{1,0:T(8,128)(2,1)S(1)} %shard_map.83), channel_id=1, source_target_pairs={{0,144},{32,176},{1,145},{33,177},{2,146},{34,178},{3,147},{35,179... | collective-permute-start | bytes 196616 | tf_op jit(solution)/shard_map/ppermute | solution.py:369
  118.9 12.2 %collective-permute-start.24 = (bf16[256,128]{1,0:T(8,128)(2,1)S(1)}, bf16[256,128]{1,0:T(8,128)(2,1)S(1)}, u32[]{:S(2)}, u32[]{:S(2)}) collective-permute-start(bf16[256,128]{1,0:T(8,128)(2,1)S(1)} %shard_map.83), channel_id=1, source_target_pairs={{0,128},{32,160},{1,129},{33,161},{2,130},{34,162},{3,131},{35,163... | collective-permute-start | bytes 196616 | tf_op jit(solution)/shard_map/ppermute | solution.py:370
  119.6 11.5 %collective-permute-start.25 = (bf16[256,128]{1,0:T(8,128)(2,1)S(1)}, bf16[256,128]{1,0:T(8,128)(2,1)S(1)}, u32[]{:S(2)}, u32[]{:S(2)}) collective-permute-start(bf16[256,128]{1,0:T(8,128)(2,1)S(1)} %shard_map.83), channel_id=1, source_target_pairs={{0,16},{32,48},{1,17},{33,49},{2,18},{34,50},{3,19},{35,51},{4,20}... | collective-permute-start | bytes 196616 | tf_op jit(solution)/shard_map/ppermute | solution.py:371
  121.2 4.7 %copy-start.2 = (bf16[2560,2560]{1,0:T(8,128)(2,1)S(1)}, bf16[2560,2560]{1,0:T(8,128)(2,1)}, u32[]{:S(2)}) copy-start(bf16[2560,2560]{1,0:T(8,128)(2,1)} %get-tuple-element.101.full_ref.refs_2_) | copy-start | bytes 39321604
  146.6 5.4 %collective-permute-start.28 = (f32[16,128]{1,0:T(8,128)S(1)}, f32[16,128]{1,0:T(8,128)S(1)}, u32[]{:S(2)}, u32[]{:S(2)}) collective-permute-start(f32[16,128]{1,0:T(8,128)S(1)} %get-tuple-element.113), channel_id=1, source_target_pairs={{0,64},{64,0},{1,65},{65,1},{2,66},{66,2},{3,67},{67,3},{4,68},{68... | collective-permute-start | bytes 24584 | tf_op jit(solution)/shard_map/ppermute | solution.py:388
  152.0 5.6 %collective-permute-start.29 = (f32[16,128]{1,0:T(8,128)S(1)}, f32[16,128]{1,0:T(8,128)S(1)}, u32[]{:S(2)}, u32[]{:S(2)}) collective-permute-start(f32[16,128]{1,0:T(8,128)S(1)} %add.155), channel_id=1, source_target_pairs={{0,32},{32,0},{16,48},{48,16},{1,33},{33,1},{17,49},{49,17},{2,34}... | collective-permute-start | bytes 24584 | tf_op jit(solution)/shard_map/ppermute | solution.py:388
  157.7 7.6 %collective-permute-start.30 = (f32[16,128]{1,0:T(8,128)S(1)}, f32[16,128]{1,0:T(8,128)S(1)}, u32[]{:S(2)}, u32[]{:S(2)}) collective-permute-start(f32[16,128]{1,0:T(8,128)S(1)} %add.156), channel_id=1, source_target_pairs={{0,4},{4,8},{8,12},{12,0},{1,5},{5,9},{9,13},{13,1},{2,6},{6,10},{... | collective-permute-start | bytes 24584 | tf_op jit(solution)/shard_map/ppermute | solution.py:388
  159.0 6.3 %collective-permute-start.31 = (f32[16,128]{1,0:T(8,128)S(1)}, f32[16,128]{1,0:T(8,128)S(1)}, u32[]{:S(2)}, u32[]{:S(2)}) collective-permute-start(f32[16,128]{1,0:T(8,128)S(1)} %add.156), channel_id=1, source_target_pairs={{0,8},{4,12},{8,0},{12,4},{1,9},{5,13},{9,1},{13,5},{2,10},{6,14},... | collective-permute-start | bytes 24584 | tf_op jit(solution)/shard_map/ppermute | solution.py:388
  162.8 2.5 %collective-permute-start.32 = (f32[16,128]{1,0:T(8,128)S(1)}, f32[16,128]{1,0:T(8,128)S(1)}, u32[]{:S(2)}, u32[]{:S(2)}) collective-permute-start(f32[16,128]{1,0:T(8,128)S(1)} %add.156), channel_id=1, source_target_pairs={{0,12},{4,0},{8,4},{12,8},{1,13},{5,1},{9,5},{13,9},{2,14},{6,2},{... | collective-permute-start | bytes 24584 | tf_op jit(solution)/shard_map/ppermute | solution.py:388
  165.3 7.6 %collective-permute-start.33 = (f32[16,128]{1,0:T(8,128)S(1)}, f32[16,128]{1,0:T(8,128)S(1)}, u32[]{:S(2)}, u32[]{:S(2)}) collective-permute-start(f32[16,128]{1,0:T(8,128)S(1)} %add_add_fusion.2), channel_id=1, source_target_pairs={{0,1},{1,2},{2,3},{3,0},{4,5},{5,6},{6,7},{7,4},{8,9},{9,10},{10,1... | collective-permute-start | bytes 24584 | tf_op jit(solution)/shard_map/ppermute | solution.py:388
  168.0 4.9 %collective-permute-start.34 = (f32[16,128]{1,0:T(8,128)S(1)}, f32[16,128]{1,0:T(8,128)S(1)}, u32[]{:S(2)}, u32[]{:S(2)}) collective-permute-start(f32[16,128]{1,0:T(8,128)S(1)} %add_add_fusion.2), channel_id=1, source_target_pairs={{0,2},{1,3},{2,0},{3,1},{4,6},{5,7},{6,4},{7,5},{8,10},{9,11},{10,... | collective-permute-start | bytes 24584 | tf_op jit(solution)/shard_map/ppermute | solution.py:388
  169.5 3.5 %collective-permute-start.35 = (f32[16,128]{1,0:T(8,128)S(1)}, f32[16,128]{1,0:T(8,128)S(1)}, u32[]{:S(2)}, u32[]{:S(2)}) collective-permute-start(f32[16,128]{1,0:T(8,128)S(1)} %add_add_fusion.2), channel_id=1, source_target_pairs={{0,3},{1,0},{2,1},{3,2},{4,7},{5,4},{6,5},{7,6},{8,11},{9,8},{10,9... | collective-permute-start | bytes 24584 | tf_op jit(solution)/shard_map/ppermute | solution.py:388
  173.0 10.7 %collective-permute-start.36 = (f32[8,128]{1,0:T(8,128)S(1)}, f32[8,128]{1,0:T(8,128)S(1)}, u32[]{:S(2)}, u32[]{:S(2)}) collective-permute-start(f32[8,128]{1,0:T(8,128)S(1)} %slice.86), channel_id=1, source_target_pairs={{16,144},{48,176},{17,145},{49,177},{18,146},{50,178},{19,147},{51... | collective-permute-start | bytes 12296 | tf_op jit(solution)/shard_map/ppermute | solution.py:393
  177.2 7.1 %collective-permute-start.37 = (f32[256,128]{1,0:T(8,128)S(1)}, f32[256,128]{1,0:T(8,128)S(1)}, u32[]{:S(2)}, u32[]{:S(2)}) collective-permute-start(f32[256,128]{1,0:T(8,128)S(1)} %get-tuple-element.137), channel_id=1, source_target_pairs={{128,144},{160,176},{129,145},{161,177},{130,146},{162,178},{131,1... | collective-permute-start | bytes 393224 | tf_op jit(solution)/shard_map/ppermute | solution.py:382
  177.9 6.4 %collective-permute-start.38 = (f32[256,128]{1,0:T(8,128)S(1)}, f32[256,128]{1,0:T(8,128)S(1)}, u32[]{:S(2)}, u32[]{:S(2)}) collective-permute-start(f32[256,128]{1,0:T(8,128)S(1)} %get-tuple-element.137), channel_id=1, source_target_pairs={{16,144},{48,176},{17,145},{49,177},{18,146},{50,178},{19,147},{51... | collective-permute-start | bytes 393224 | tf_op jit(solution)/shard_map/ppermute | solution.py:381
  184.6 3.3 %collective-permute-start.39 = (f32[256,128]{1,0:T(8,128)S(1)}, f32[256,128]{1,0:T(8,128)S(1)}, u32[]{:S(2)}, u32[]{:S(2)}) collective-permute-start(f32[256,128]{1,0:T(8,128)S(1)} %fusion), channel_id=1, source_target_pairs={{144,0},{176,32},{208,16},{240,48},{145,1},{177,33},{209,17},{241,... | collective-permute-start | bytes 393224 | tf_op jit(solution)/shard_map/ppermute | solution.py:407
  185.3 18.4 %collective-permute-start.40 = (f32[256,128]{1,0:T(8,128)S(1)}, f32[256,128]{1,0:T(8,128)S(1)}, u32[]{:S(2)}, u32[]{:S(2)}) collective-permute-start(f32[256,128]{1,0:T(8,128)S(1)} %fusion), channel_id=1, source_target_pairs={{144,64},{176,96},{208,80},{240,112},{145,65},{177,97},{209,81},{2... | collective-permute-start | bytes 393224 | tf_op jit(solution)/shard_map/ppermute | solution.py:407
  186.6 17.1 %collective-permute-start.41 = (f32[256,128]{1,0:T(8,128)S(1)}, f32[256,128]{1,0:T(8,128)S(1)}, u32[]{:S(2)}, u32[]{:S(2)}) collective-permute-start(f32[256,128]{1,0:T(8,128)S(1)} %fusion), channel_id=1, source_target_pairs={{144,128},{176,160},{208,144},{240,176},{145,129},{177,161},{209,1... | collective-permute-start | bytes 393224 | tf_op jit(solution)/shard_map/ppermute | solution.py:407
  187.3 16.4 %collective-permute-start.42 = (f32[256,128]{1,0:T(8,128)S(1)}, f32[256,128]{1,0:T(8,128)S(1)}, u32[]{:S(2)}, u32[]{:S(2)}) collective-permute-start(f32[256,128]{1,0:T(8,128)S(1)} %fusion), channel_id=1, source_target_pairs={{144,192},{176,224},{208,208},{240,240},{145,193},{177,225},{209,2... | collective-permute-start | bytes 393224 | tf_op jit(solution)/shard_map/ppermute | solution.py:407
where the time goes:
time: 205 us
  starting transfers between devices  84.3 us (41%)
  Pallas kernels  62.5 us (30%)
  waiting for transfers between devices  37.9 us (18%)
  local copies, waits for them, and re-layouts  17.4 us (8%)
    ppermute x6, starting transfers between devices, gather_weights(): swaps = {i: lax.ppermute(v, 'c', CORE) for i, v in zip(near, ready)}  23 us
    ppermute x4, waiting for transfers between devices, on_device(): landed = landed + lax.ppermute(result, NET + ('z',), pairs)  15.7 us
    pallas_call x1, Pallas kernels, second(): call(second_body, [((HALF, 128), bf16), ((HALF, 128), f32), ((16, 128), f...  15.5 us
    pallas_call x1, Pallas kernels, student(): call(student_body, [((HALF, 128), bf16)], [ACTIVE, WIDE, NORMED, SQUARES]...  15.4 us
    ppermute x12, starting transfers between devices, gather_axis(): lax.ppermute(piece, axis, shift(4, k))  15.3 us
    ppermute x12, waiting for transfers between devices, gather_axis(): lax.ppermute(piece, axis, shift(4, k))  15.1 us
    unnamed x26, local copies, waits for them, and re-layouts  14.7 us
    ppermute x8, starting transfers between devices, on_device(): moved = [lax.ppermute(sums, axis, pairs) for axis, pairs in sends]  13.4 us
  transfers between devices with their start and end apart: 43, of which 11 were waited for; matrix products, arithmetic and copies ran while one was open for 1% of the time, Pallas kernels for 23%

commit v1 on v0

v1 whole, which is shorter than its diff:
```python
import jax
import jax.numpy as jnp
from jax import lax
from jax.experimental import pallas as pl
from jax.experimental.pallas import tpu as pltpu
from jax.sharding import Mesh, PartitionSpec as P

epsilon = 1e-06
NET = ("h", "c")
FSDP = ("z", "x", "y")
ROWS, CH, D, SHARD, PADDED = 512, 64, 2432, 38, 40
PIECE = 4 * PADDED
KDIM = 64 * PADDED
CHUNKS = ((0, 3), (3, 4), (7, 3))
ANY = pl.BlockSpec(memory_space=pl.ANY)
LIMIT_A, LIMIT_B, LIMIT_C = 18, 16, 8
HALF = ROWS // 2
VM = pl.BlockSpec(memory_space=pltpu.VMEM)
SM = pl.BlockSpec(memory_space=pltpu.SMEM)
NT = (((1,), (1,)), ((), ()))
f32, bf16 = jnp.float32, jnp.bfloat16


def call(body, outs, limit, scratch=(), smem=0, ins=0, anys=0):
    return pl.pallas_call(
        body,
        out_shape=[jax.ShapeDtypeStruct(s, t) for s, t in outs],
        in_specs=[SM] * smem + [VM] * ins + [ANY] * anys,
        out_specs=[VM] * len(outs),
        scratch_shapes=list(scratch),
        compiler_params=pltpu.CompilerParams(vmem_limit_bytes=limit * 1024 * 1024),
    )


def fetch(pieces, full, sems):
    copies = [
        pltpu.make_async_copy(ref, full.at[pl.ds(i * PIECE, PIECE), :], sems.at[i])
        for i, ref in enumerate(pieces)
    ]
    for copy in copies:
        copy.start()
    return copies


def mm(a, b):
    return jnp.dot(a, b, preferred_element_type=f32)


def mm_nt(a, b):
    return lax.dot_general(a, b, NT, preferred_element_type=f32)


def unpack(v):
    return jnp.concatenate([v[:, :CH], v[:, CH:]], axis=0)


def pack(v):
    return jnp.concatenate([v[:HALF], v[HALF:]], axis=1)


def order_tails(where_ref, tails, close_ref, en_ref, fin_ref, padded):
    core, x, y = where_ref[0], where_ref[1], where_ref[2]
    for side in range(2):
        parity = core if side == 0 else 1 - core
        for part in range(2):
            z = 2 * part + parity
            for k in range(4):
                at_k = (side * 8 + part * 4 + k) * PIECE
                tail = tails[at_k : at_k + PIECE, :]
                close_ref[at_k : at_k + PIECE, :] = tail[:, :CH]
                tail = tail.astype(f32)
                for i in range(4):
                    xs = i if part == 0 else lax.rem(x + 4 - k, 4)
                    ys = lax.rem(y + 4 - k, 4) if part == 0 else i
                    at = ((z * 4 + xs) * 4 + ys) * PADDED
                    padded[pl.ds(pl.multiple_of(at, 8), PADDED), :] = tail[
                        i * PADDED : (i + 1) * PADDED
                    ]
    for d in range(64):
        padded[d * SHARD : (d + 1) * SHARD, :] = padded[d * PADDED : d * PADDED + SHARD, :]

    def cut(i, _):
        at = pl.multiple_of(i * 128, 128)
        rows = padded[pl.ds(at, 128), :]
        en_ref[pl.ds(at, 128), :] = rows[:, :CH].astype(bf16)
        fin_ref[pl.ds(at, 128), :] = rows[:, CH:].astype(bf16)
        return 0

    lax.fori_loop(0, D // 128, cut, 0)


def forward(rows, close_ref, en_ref, fin_ref, copies, full, active, wide, normed, squares):
    def act(i, _):
        at = pl.multiple_of(i * 256, 256)
        hidden = mm_nt(rows, close_ref[pl.ds(at, 256), :])
        active[:, pl.ds(at, 256)] = jax.nn.gelu(hidden).astype(bf16)
        return 0

    lax.fori_loop(0, KDIM // 256, act, 0)
    squares[...] = jnp.zeros((ROWS, 128), f32)
    for copy in copies:
        copy.wait()

    def tile(at, size):
        for r in range(0, ROWS, HALF):
            total = mm(active[r : r + HALF, :], full[:, pl.ds(at, size)])
            total += mm_nt(rows[r : r + HALF], en_ref[pl.ds(at, size), :])
            wide[r : r + HALF, pl.ds(at, size)] = total
            part = total[:, :128] * total[:, :128]
            for lane in range(128, size, 128):
                part += total[:, lane : lane + 128] * total[:, lane : lane + 128]
            squares[r : r + HALF] += part

    def step(i, _):
        tile(pl.multiple_of(i * 768, 256), 768)
        return 0

    lax.fori_loop(0, 3, step, 0)
    tile(2304, 128)
    mean = jnp.sum(squares[...], axis=1, keepdims=True) / D
    factor = lax.rsqrt(mean + epsilon)
    squares[...] = jnp.broadcast_to(factor, (ROWS, 128))

    def scale(i, _):
        at = pl.multiple_of(i * 128, 128)
        normed[:, pl.ds(at, 128)] = (wide[:, pl.ds(at, 128)] * squares[...]).astype(bf16)
        return 0

    lax.fori_loop(0, D // 128, scale, 0)
    return mm(normed[...], fin_ref[...])


ACTIVE = pltpu.VMEM((ROWS, KDIM), bf16)
WIDE = pltpu.VMEM((ROWS, D), f32)
NORMED = pltpu.VMEM((ROWS, D), bf16)
SQUARES = pltpu.VMEM((ROWS, 128), f32)


SEMS = pltpu.SemaphoreType.DMA((16,))


def student_body(where_ref, rows_ref, *refs):
    pieces, (out_ref, full, close_ref, en_ref, fin_ref) = refs[:16], refs[16:21]
    active, wide, normed, squares, tails, padded, sems, tail_sems = refs[21:]
    small = [
        pltpu.make_async_copy(
            ref.at[:, pl.ds(D, 2 * CH)], tails.at[pl.ds(i * PIECE, PIECE), :], tail_sems.at[i]
        )
        for i, ref in enumerate(pieces)
    ]
    for copy in small:
        copy.start()
    copies = fetch(pieces, full, sems)
    for copy in small:
        copy.wait()
    order_tails(where_ref, tails, close_ref, en_ref, fin_ref, padded)
    rows = unpack(rows_ref[...])
    projected = forward(
        rows, close_ref, en_ref, fin_ref, copies, full, active, wide, normed, squares
    )
    out_ref[...] = pack((rows.astype(f32) + projected)).astype(bf16)


def student(where, rows, pieces):
    out, *tables = call(
        student_body,
        [
            ((HALF, 128), bf16),
            ((KDIM, KDIM), bf16),
            ((KDIM, CH), bf16),
            ((D, CH), bf16),
            ((D, CH), bf16),
        ],
        LIMIT_A,
        [
            ACTIVE,
            WIDE,
            NORMED,
            SQUARES,
            pltpu.VMEM((KDIM, 2 * CH), bf16),
            pltpu.VMEM((KDIM, 2 * CH), f32),
            SEMS,
            SEMS,
        ],
        1,
        1,
        16,
    )(where, rows, *pieces)
    return out, tables


def second_body(sample_ref, renoise_ref, level_ref, text_ref, full, close_ref, en_ref, fin_ref, *refs):
    rows_ref, pred_ref, sums_ref, proj_ref, squares, normed, active, wide = refs
    level = level_ref[...]
    sample = sample_ref[...].astype(f32)
    packed = ((1.0 - level) * sample + level * renoise_ref[...].astype(f32)).astype(bf16)
    rows_ref[...] = packed
    rows = unpack(packed)
    projected = forward(
        rows, close_ref, en_ref, fin_ref, (), full, active, wide, normed, squares
    )
    proj_ref[...] = projected
    judged = rows.astype(f32) + projected
    pred = packed.astype(f32) - level * pack(judged)
    pred_ref[...] = pred
    spread = jnp.abs(sample - pred)
    for p in range(4):
        part = jnp.sum(spread[p * 64 : p * 64 + 64], axis=0, keepdims=True)
        for q, cut in ((p, part[:, :CH]), (p + 4, part[:, CH:])):
            pool = jnp.sum(judged[q * 64 : q * 64 + 64], axis=0, keepdims=True)
            sums_ref[q : q + 1, :] = jnp.concatenate([pool, cut], axis=1)
    sums_ref[8:16, :] = text_ref[...]


def second(sample, renoise, level, text, tables):
    return call(
        second_body,
        [
            ((HALF, 128), bf16),
            ((HALF, 128), f32),
            ((16, 128), f32),
            ((ROWS, CH), f32),
            ((ROWS, 128), f32),
            ((ROWS, D), bf16),
        ],
        LIMIT_B,
        [ACTIVE, WIDE],
        0,
        8,
    )(sample, renoise, level, text, *tables)


def pf_body(full, en_ref, fin_ref, out_ref, ef_ref):
    def tile(i, _):
        at = pl.multiple_of(i * 256, 256)
        out_ref[pl.ds(at, 256), :] = mm(full[pl.ds(at, 256), :D], fin_ref[...])
        return 0

    lax.fori_loop(0, KDIM // 256, tile, 0)
    ef_ref[...] = lax.dot_general(
        en_ref[...], fin_ref[...], (((0,), (0,)), ((), ())), preferred_element_type=f32
    )


def proj_final(full, en, fin):
    return call(pf_body, [((KDIM, CH), f32), ((CH, CH), f32)], LIMIT_C, (), 0, 3)(full, en, fin)


def back_body(base, tiles, rows_ref, normed_ref, full, close_ref, en_ref, sum_ref, *refs):
    out_ref, slope_ref = refs
    rows = unpack(rows_ref[...])
    if base == 0:
        out_ref[...] = mm(normed_ref[...], en_ref[...])
    else:
        out_ref[...] = sum_ref[...]

    def tile(i, _):
        at = pl.multiple_of(base * 256 + i * 256, 256)
        embed = close_ref[pl.ds(at, 256), :]
        hidden = mm_nt(rows, embed)
        s = 0.7978845608028654
        square = hidden * hidden
        th = jnp.tanh(s * hidden * (1.0 + 0.044715 * square))
        slope = 0.5 * (1.0 + th) + (0.5 * s) * hidden * (1.0 - th * th) * (1.0 + 0.134145 * square)
        slope_ref[:, pl.ds(pl.multiple_of(i * 256, 256), 256)] = slope.astype(bf16)
        moved = mm_nt(normed_ref[...], full[pl.ds(at, 256), :D]) * slope
        out_ref[...] += mm(moved.astype(bf16), embed)
        return 0

    lax.fori_loop(0, tiles, tile, 0)


def back_step(chunk, rows, normed, tables, total):
    base, tiles = chunk
    full, close, en, _ = tables
    return call(
        lambda *refs: back_body(base, tiles, *refs),
        [((ROWS, CH), f32), ((ROWS, tiles * 256), bf16)],
        LIMIT_C,
        (),
        0,
        6,
    )(rows, normed, full, close, en, total)


def finish_body(sums_ref, close_ref, pf_ref, ef_ref, proj_ref, factor_ref, total_ref, *refs):
    slopes, (out_ref, carried, result) = refs[:3], refs[3:]
    high = lax.Precision.HIGHEST
    pooled = sums_ref[:8, :CH] / 4096.0
    text = sums_ref[8:16, :CH]
    pooled_norm = jnp.sqrt(jnp.sum(pooled * pooled, axis=-1, keepdims=True) + epsilon)
    text_norm = jnp.sqrt(jnp.sum(text * text, axis=-1, keepdims=True) + epsilon)
    unit_pool = pooled / pooled_norm
    unit_text = text / text_norm
    reward = jnp.sum(unit_pool * unit_text, axis=-1, keepdims=True)
    cot = (unit_text - reward * unit_pool) / pooled_norm
    direct = lax.dot_general(cot, ef_ref[...], NT, precision=high, preferred_element_type=f32)

    def rows_of(v):
        return jnp.concatenate(
            [jnp.broadcast_to(v[p : p + 1], (64, v.shape[1])) for p in range(8)], axis=0
        )

    carried[...] = lax.dot_general(
        cot, pf_ref[...], NT, precision=high, preferred_element_type=f32
    )
    result[...] = rows_of(direct)
    for (base, tiles), ref in zip(CHUNKS, slopes):

        def tile(i, _, base=base, ref=ref):
            at = pl.multiple_of(base * 256 + i * 256, 256)
            local = pl.multiple_of(i * 256, 256)
            scaled = ref[:, pl.ds(local, 256)].astype(f32) * rows_of(carried[:, pl.ds(at, 256)])
            result[...] += mm(scaled.astype(bf16), close_ref[pl.ds(at, 256), :])
            return 0

        lax.fori_loop(0, tiles, tile, 0)
    cot_rows = rows_of(cot)
    along = jnp.sum(cot_rows * proj_ref[...], axis=1, keepdims=True) / D
    out_ref[...] = pack(
        factor_ref[:, :CH] * (result[...] - along * total_ref[...]) + cot_rows
    )


def finish(sums, close, pf, ef, projected, factor, total, slopes):
    return call(
        finish_body,
        [((HALF, 128), f32)],
        LIMIT_C,
        [pltpu.VMEM((8, KDIM), f32), pltpu.VMEM((ROWS, CH), f32)],
        0,
        10,
    )(sums, close, pf, ef, projected, factor, total, *slopes)[0]


def shift(n, k):
    return [(i, (i + k) % n) for i in range(n)]


Z1 = [(0, 1), (1, 0), (2, 3), (3, 2)]
Z2 = [(0, 2), (2, 0), (1, 3), (3, 1)]
CORE = [(0, 1), (1, 0)]


def gather_axis(piece, axis):
    return [piece] + [lax.ppermute(piece, axis, shift(4, k)) for k in range(1, 4)]


def place(me, moved):
    out = jnp.zeros((4,) + moved[0].shape, moved[0].dtype)
    for k, piece in enumerate(moved):
        out = lax.dynamic_update_index_in_dim(out, piece, lax.rem(me - k + 4, 4), 0)
    return out.reshape((4 * moved[0].shape[0],) + moved[0].shape[1:])


def gather_weights(slab, exchange):
    core, z, x, y = (lax.axis_index(a) for a in ("c", "z", "x", "y"))
    swapped = lax.ppermute(slab, ("c", "z"), [(4, 1), (1, 4), (6, 3), (3, 6)])
    mine = jnp.where(core == lax.rem(z, 2), slab, swapped)
    far = lax.ppermute(mine, "z", Z2)
    part_a, part_b = jnp.where(z < 2, mine, far), jnp.where(z < 2, far, mine)
    part_a, part_b = lax.optimization_barrier((part_a, part_b))
    moved_a, moved_b = gather_axis(part_a, "x"), gather_axis(part_b, "y")
    moved_a, moved_b = lax.optimization_barrier((moved_a, moved_b))
    part_a, part_b = lax.optimization_barrier((place(x, moved_a), place(y, moved_b)))
    pieces = gather_axis(part_a, "y") + gather_axis(part_b, "x")
    extra = exchange(part_a)
    first = [0, 4, 1, 5, 3, 7]
    ready, extra = lax.optimization_barrier(([pieces[i] for i in first], extra))
    swaps = {i: lax.ppermute(v, "c", CORE) for i, v in zip(first, ready)}
    pieces = [ready[first.index(i)] if i in first else pieces[i] for i in range(8)]
    for i in (2, 6):
        swaps[i] = lax.ppermute(pieces[i], "c", CORE)
    return pieces + [swaps[i] for i in range(8)], extra


def packed_rows(block):
    flat = block.reshape(ROWS, CH)
    return jnp.concatenate([flat[:HALF], flat[HALF:]], axis=1)


def on_device(noise_in, renoise, timesteps, prompt_ids, embed_w, proj_w, final_w, text_table):
    h, core, z, x, y = (lax.axis_index(a) for a in NET + FSDP)
    parity = lax.rem(z, 2)
    slab = jnp.concatenate([proj_w[0], embed_w[0].T, final_w[0]], axis=1)
    slab = jnp.pad(slab, ((0, PADDED - SHARD), (0, 0)))


    def exchange(anchor):
        _, first, second_in, ids = lax.optimization_barrier(
            (anchor, noise_in, renoise, prompt_ids)
        )
        both = jnp.concatenate([packed_rows(first), packed_rows(second_in)], axis=0)
        other = lax.ppermute(both, "z", Z1)
        table_rows = text_table.shape[0]
        first_row = lax.axis_index(NET + FSDP) * table_rows
        offsets = ids - first_row
        matches = offsets[:, :, None] == jnp.arange(table_rows, dtype=jnp.int32)[None, None, :]
        counts = jnp.sum(matches.astype(f32), axis=1).astype(bf16)
        text = jnp.dot(counts, text_table, preferred_element_type=f32) / ids.shape[1]
        text = jnp.concatenate([text, jnp.zeros_like(text)], axis=1)
        text = text + lax.ppermute(text, "z", Z1)
        text = text + lax.ppermute(text, "h", CORE)
        return jnp.where(core == parity, both, other), text

    pieces, (both, text) = gather_weights(slab, exchange)
    noise, fresh = both[:HALF], both[HALF:]

    judge = (h == 1) & (parity == 1)
    level = timesteps.astype(f32) / 1000.0
    level = jnp.where(judge, 0.0, level)
    level = jnp.broadcast_to(level[:, None, None], (8, 64, CH))
    level = packed_rows(level)

    where = jnp.stack([core, x, y]).astype(jnp.int32)
    sample, tables = student(where, noise, pieces)
    is_student = (h == 0) & (parity == 0)
    got = [
        lax.ppermute(sample, ("h", "z"), [(0, 5), (2, 7)]),
        lax.ppermute(sample, ("h", "z"), [(0, 4), (2, 6)]),
        lax.ppermute(sample, ("h", "z"), [(0, 1), (2, 3)]),
    ]
    full, close, en, fin = tables
    pf, ef = proj_final(full, en, fin)
    got, sample, pf = lax.optimization_barrier((got, sample, pf))
    sample = jnp.where(
        is_student, sample, jnp.where(h == 0, got[2], jnp.where(parity == 1, got[0], got[1]))
    )
    rows, pred, sums, projected, factor, normed = second(
        sample, fresh, level, text, tables
    )

    real = lax.ppermute(pred, ("h", "z"), [(1, 5), (3, 7)])
    fake = lax.ppermute(pred, ("h", "z"), [(4, 5), (6, 7)])
    total = jnp.zeros((ROWS, CH), f32)
    slopes = []
    corners = [("c", CORE), ("z", Z2), (("c", "z"), [(i, i ^ 6) for i in range(8)])]
    rounds = [corners] + [[(a, shift(4, k)) for k in (1, 2, 3)] for a in "xy"]
    for chunk, sends in zip(CHUNKS, rounds):
        sums, rows = lax.optimization_barrier((sums, rows))
        moved = [lax.ppermute(sums, axis, pairs) for axis, pairs in sends]
        total, slope = back_step(chunk, rows, normed, tables, total)
        total, moved = lax.optimization_barrier((total, moved))
        slopes.append(slope)
        sums = sum(moved, sums)
    absolute = lax.ppermute(sums[:8], ("h", "z"), [(1, 5), (3, 7)])
    reward = finish(sums, close, pf, ef, projected, factor, total, slopes)
    weight = jnp.sum(absolute[:, CH:], axis=1) / (4096.0 * CH)
    weight = 1.0 / (weight + epsilon)
    weight = packed_rows(jnp.broadcast_to(weight[:, None, None], (8, 64, CH)))
    result = weight * (fake - real) - reward
    landed = 0.0
    for to_h in range(2):
        for to_c in range(2):
            pairs = [
                (9 + 4 * c + 2 * q, 8 * to_h + 4 * to_c + 2 * q + c)
                for c in range(2)
                for q in range(2)
            ]
            landed = landed + lax.ppermute(result, NET + ("z",), pairs)
    out = jnp.concatenate([landed[:, :CH], landed[:, CH:]], axis=0)
    return out.reshape(8, 64, CH)


def solution(mesh):
    cube = Mesh(mesh.devices.reshape(2, 2, 4, 4, 4), NET + FSDP)
    placed = (
        P(None, FSDP, None),
        P(None, FSDP, None),
        P(),
        P(),
        P(NET, None, FSDP),
        P(NET, FSDP, None),
        P(NET, FSDP, None),
        P(NET + FSDP, None),
    )
    return jax.shard_map(
        on_device, mesh=cube, in_specs=placed, out_specs=P(None, FSDP, None), check_vma=False
    )
```

time: 205 us -> 183 us (0.89)
  Pallas kernels: 62.5 us -> 51.9 us
  local copies, waits for them, and re-layouts: 17.4 us -> 9.79 us
  waiting for transfers between devices: 37.9 us -> 34.2 us
    ppermute x12, waiting for transfers between devices: 15.1 us -> 4.28 us  [gather_axis(): lax.ppermute(piece, axis, shift(4, k))]
    unnamed x26 -> x20, local copies, waits for them, and re-layouts: 14.7 us -> 6.21 us
    pallas_call x4 -> x3, Pallas kernels: 34.3 us -> 25.9 us  [the longest x1 16.9 us: student(): call(student_body, [((HALF, 128), bf16), ((KDIM, KDIM), bf16), ((KDIM, CH...]
    ppermute x1, waiting for transfers between devices: 0.01 us -> 4.71 us  [on_device(): lax.ppermute(sample, ('h', 'z'), [(0, 1), (2, 3)])]
    ppermute x8 -> x9, starting transfers between devices: 13.4 us -> 10.8 us  [on_device(): moved = [lax.ppermute(sums, axis, pairs) for axis, pairs in sends]]
    ppermute x2, waiting for transfers between devices: 0.01 us -> 2.16 us  [gather_weights(): swaps[i] = lax.ppermute(pieces[i], 'c', CORE)]
    pallas_call x1, Pallas kernels: 15.5 us -> 13.3 us  [second(): call(second_body, [((HALF, 128), bf16), ((HALF, 128), f32), ((16, 128), f...]
    pallas_call x4 -> x3, Pallas kernels: 12.7 us -> 12.7 us  [back_step(): call(lambda *refs: back_body(base, tiles, *refs), [((ROWS, CH), f32), ((R...]
  transfers between devices with their start and end apart: 43 -> 44, of which waited for: 11 -> 10; matrix products, arithmetic and copies ran while one was open for 1% -> 2% of each run, Pallas kernels for 23% -> 12%
where the time goes in v1:
time: 183 us; the launch traced here: 182 us
  starting transfers between devices  84 us (46%)
  Pallas kernels  51.9 us (28%)
  waiting for transfers between devices  34.2 us (19%)
  local copies, waits for them, and re-layouts  9.79 us (5%)
    ppermute x6, starting transfers between devices, gather_weights(): swaps = {i: lax.ppermute(v, 'c', CORE) for i, v in zip(first, ready)}  20.7 us
    ppermute x12, starting transfers between devices, gather_axis(): lax.ppermute(piece, axis, shift(4, k))  17.1 us
    pallas_call x1, Pallas kernels, student(): call(student_body, [((HALF, 128), bf16), ((KDIM, KDIM), bf16), ((KDIM, CH...  16.9 us
    ppermute x4, waiting for transfers between devices, on_device(): landed = landed + lax.ppermute(result, NET + ('z',), pairs)  14.2 us
    pallas_call x1, Pallas kernels, second(): call(second_body, [((HALF, 128), bf16), ((HALF, 128), f32), ((16, 128), f...  13.3 us
    pallas_call x3, Pallas kernels, back_step(): call(lambda *refs: back_body(base, tiles, *refs), [((ROWS, CH), f32), ((R...  12.7 us
    ppermute x9, starting transfers between devices, on_device(): moved = [lax.ppermute(sums, axis, pairs) for axis, pairs in sends]  10.8 us
    ppermute x1, starting transfers between devices, exchange(): text = text + lax.ppermute(text, 'h', CORE)  8.7 us
  transfers between devices with their start and end apart: 44, of which 10 were waited for; matrix products, arithmetic and copies ran while one was open for 2% of the time, Pallas kernels for 12%

profile of v1, /device:TPU:35, one launch (start us, length us, event | category | flops | bytes accessed | tf_op | source)
XLA Modules:
  0.0 182.3 jit_solution(2489112355290518474)
XLA Ops:
  0.0 1.0 concatenate.24
  1.1 0.7 collective-permute-start
  1.8 3.1 %collective-permute-start.1 = (bf16[40,2560]{1,0:T(8,128)(2,1)S(1)}, bf16[40,2560]{1,0:T(8,128)(2,1)S(1)}, u32[]{:S(2)}, u32[]{:S(2)}) collective-permute-start(bf16[40,2560]{1,0:T(8,128)(2,1)S(1)} %broadcast_select_fusion), channel_id=1, source_target_pairs={{0,32},{32,0},{16,48},{48,16},{1,33},{33,1},{17,49},{49,17},{2,34}... | collective-permute-start | bytes 614408 | tf_op jit(solution)/shard_map/ppermute | solution.py:360
  4.9 4.9 %collective-permute-done.1 = bf16[40,2560]{1,0:T(8,128)(2,1)S(1)} collective-permute-done((bf16[40,2560]{1,0:T(8,128)(2,1)S(1)}, bf16[40,2560]{1,0:T(8,128)(2,1)S(1)}, u32[]{:S(2)}, u32[]{:S(2)}) %collective-permute-start.1) | collective-permute-done | bytes 204832 | tf_op jit(solution)/shard_map/ppermute | solution.py:360
  9.8 1.3 collective-permute-start.2
  11.1 0.8 collective-permute-start.3
  12.0 1.9 %collective-permute-start.4 = (bf16[40,2560]{1,0:T(8,128)(2,1)S(1)}, bf16[40,2560]{1,0:T(8,128)(2,1)S(1)}, u32[]{:S(2)}, u32[]{:S(2)}) collective-permute-start(bf16[40,2560]{1,0:T(8,128)(2,1)S(1)} %get-tuple-element.72), channel_id=1, source_target_pairs={{0,12},{4,0},{8,4},{12,8},{1,13},{5,1},{9,5},{13,9},{2,14},{6,2},{... | collective-permute-start | bytes 614408 | tf_op jit(solution)/shard_map/ppermute | solution.py:346
  13.8 1.3 collective-permute-start.5
  15.1 2.6 %collective-permute-start.6 = (bf16[40,2560]{1,0:T(8,128)(2,1)S(1)}, bf16[40,2560]{1,0:T(8,128)(2,1)S(1)}, u32[]{:S(2)}, u32[]{:S(2)}) collective-permute-start(bf16[40,2560]{1,0:T(8,128)(2,1)S(1)} %get-tuple-element.76), channel_id=1, source_target_pairs={{0,2},{1,3},{2,0},{3,1},{4,6},{5,7},{6,4},{7,5},{8,10},{9,11},{10,... | collective-permute-start | bytes 614408 | tf_op jit(solution)/shard_map/ppermute | solution.py:346
  17.8 1.1 collective-permute-start.7
  18.8 0.9 collective-permute-done.5
  19.7 3.4 %collective-permute-done.6 = bf16[40,2560]{1,0:T(8,128)(2,1)S(1)} collective-permute-done((bf16[40,2560]{1,0:T(8,128)(2,1)S(1)}, bf16[40,2560]{1,0:T(8,128)(2,1)S(1)}, u32[]{:S(2)}, u32[]{:S(2)}) %collective-permute-start.6) | collective-permute-done | bytes 204832 | tf_op jit(solution)/shard_map/ppermute | solution.py:346
  23.4 1.9 %collective-permute-start.10 = (bf16[160,2560]{1,0:T(8,128)(2,1)S(1)}, bf16[160,2560]{1,0:T(8,128)(2,1)S(1)}, u32[]{:S(2)}, u32[]{:S(2)}) collective-permute-start(bf16[160,2560]{1,0:T(8,128)(2,1)S(1)} %bitcast.38), channel_id=1, source_target_pairs={{0,3},{1,0},{2,1},{3,2},{4,7},{5,4},{6,5},{7,6},{8,11},{9,8},{10,9... | collective-permute-start | bytes 2457608 | tf_op jit(solution)/shard_map/ppermute | solution.py:346
  25.3 1.4 collective-permute-start.11
  27.2 7.8 %collective-permute-start.13 = (f32[8,128]{1,0:T(8,128)S(1)}, f32[8,128]{1,0:T(8,128)S(1)}, u32[]{:S(2)}, u32[]{:S(2)}) collective-permute-start(f32[8,128]{1,0:T(8,128)S(1)} %concatenate.28), channel_id=1, source_target_pairs={{0,16},{16,0},{32,48},{48,32},{1,17},{17,1},{33,49},{49,33},{2,18}... | collective-permute-start | bytes 12296 | tf_op jit(solution)/shard_map/ppermute | solution.py:402
  35.0 0.9 fusion.5
  35.9 0.3 collective-permute-done.13
  36.2 8.7 %collective-permute-start.14 = (f32[8,128]{1,0:T(8,128)S(1)}, f32[8,128]{1,0:T(8,128)S(1)}, u32[]{:S(2)}, u32[]{:S(2)}) collective-permute-start(f32[8,128]{1,0:T(8,128)S(1)} %pad_add_fusion.1), channel_id=1, source_target_pairs={{0,128},{128,0},{1,129},{129,1},{2,130},{130,2},{3,131},{131,3},{4... | collective-permute-start | bytes 12296 | tf_op jit(solution)/shard_map/ppermute | solution.py:403
  45.0 0.9 collective-permute-done.14
  45.9 1.9 %collective-permute-start.12 = (bf16[512,128]{1,0:T(8,128)(2,1)S(1)}, bf16[512,128]{1,0:T(8,128)(2,1)S(1)}, u32[]{:S(2)}, u32[]{:S(2)}) collective-permute-start(bf16[512,128]{1,0:T(8,128)(2,1)S(1)} %maximum_maximum_fusion), channel_id=1, source_target_pairs={{0,16},{16,0},{32,48},{48,32},{1,17},{17,1},{33,49},{49,33},{2,18}... | collective-permute-start | bytes 393224 | tf_op jit(solution)/shard_map/ppermute | solution.py:394
  47.7 2.8 %collective-permute-done.12 = bf16[512,128]{1,0:T(8,128)(2,1)S(1)} collective-permute-done((bf16[512,128]{1,0:T(8,128)(2,1)S(1)}, bf16[512,128]{1,0:T(8,128)(2,1)S(1)}, u32[]{:S(2)}, u32[]{:S(2)}) %collective-permute-start.12) | collective-permute-done | bytes 131104 | tf_op jit(solution)/shard_map/ppermute | solution.py:394
  50.5 3.2 %collective-permute-start.15 = (bf16[160,2560]{1,0:T(8,128)(2,1)S(1)}, bf16[160,2560]{1,0:T(8,128)(2,1)}, u32[]{:S(2)}, u32[]{:S(2)}) collective-permute-start(bf16[160,2560]{1,0:T(8,128)(2,1)S(1)} %bitcast.40), channel_id=1, source_target_pairs={{0,2},{1,3},{2,0},{3,1},{4,6},{5,7},{6,4},{7,5},{8,10},{9,11},{10,... | collective-permute-start | bytes 2457608 | tf_op jit(solution)/shard_map/ppermute | solution.py:346
  53.8 1.6 collective-permute-start.16
  55.5 8.1 %collective-permute-start.17 = (bf16[160,2560]{1,0:T(8,128)(2,1)S(1)}, bf16[160,2560]{1,0:T(8,128)(2,1)S(1)}, u32[]{:S(2)}, u32[]{:S(2)}) collective-permute-start(bf16[160,2560]{1,0:T(8,128)(2,1)S(1)} %bitcast.41), channel_id=1, source_target_pairs={{0,64},{64,0},{1,65},{65,1},{2,66},{66,2},{3,67},{67,3},{4,68},{68... | collective-permute-start | bytes 2457608 | tf_op jit(solution)/shard_map/ppermute | solution.py:370
  63.6 0.3 collective-permute-start.18
  63.9 0.2 collective-permute-start.20
  64.1 8.9 %collective-permute-start.21 = (bf16[160,2560]{1,0:T(8,128)(2,1)S(1)}, bf16[160,2560]{1,0:T(8,128)(2,1)}, u32[]{:S(2)}, u32[]{:S(2)}) collective-permute-start(bf16[160,2560]{1,0:T(8,128)(2,1)S(1)} %bitcast.36), channel_id=1, source_target_pairs={{0,64},{64,0},{1,65},{65,1},{2,66},{66,2},{3,67},{67,3},{4,68},{68... | collective-permute-start | bytes 2457608 | tf_op jit(solution)/shard_map/ppermute | solution.py:370
  73.0 3.2 %collective-permute-start.22 = (bf16[160,2560]{1,0:T(8,128)(2,1)}, bf16[160,2560]{1,0:T(8,128)(2,1)}, u32[]{:S(2)}, u32[]{:S(2)}) collective-permute-start(bf16[160,2560]{1,0:T(8,128)(2,1)} %collective-permute-done.9.refs_5_), channel_id=1, source_target_pairs={{0,64},{64,0},{1,65},{65,1},{2,66},{66,2},{3,67},{67,3},{4,68},{68... | collective-permute-start | bytes 2457608 | tf_op jit(solution)/shard_map/ppermute | solution.py:370
  76.2 0.9 copy-done.1
  77.2 0.9 copy-done.3
  78.1 0.5 collective-permute-start.19
  78.6 0.9 copy-done.5
  80.0 1.0 collective-permute-done.19.refs_10_
  81.0 1.2 collective-permute-done.23.refs_14_
  82.2 1.1 copy-done.2
  83.3 1.1 copy-done.4
  84.5 1.1 copy-done.6
  85.6 16.9 %shard_map.82 = (bf16[256,128]{1,0:T(8,128)(2,1)S(1)}, bf16[2560,2560]{1,0:T(8,128)(2,1)S(1)}, bf16[2560,64]{1,0:T(8,128)(2,1)S(1)}, bf16[2432,64]{1,0:T(8,128)(2,1)S(1)}, bf16[2432,64]{1,0:T(8,128)(2,1)S(1)}) custom-call(s32[3]{0:T(128)S(1)} %pad_add_fusion.where_ref, bf16[256,128]{1,0:T(8,128)(2,1)S(1)} %get-tuple-element.140.rows_ref, ...), custom_call_target="tpu_custom_call" | custom-call | tf_op jit(solution)/shard_map/pallas_call | solution.py:165
  102.5 0.7 collective-permute-start.25
  103.1 0.7 collective-permute-start.26
  103.8 1.3 collective-permute-start.27
  105.4 5.1 %shard_map.83 = (f32[2560,64]{1,0:T(8,128)S(1)}, f32[64,64]{1,0:T(8,128)S(1)}) custom-call(bf16[2560,2560]{1,0:T(8,128)(2,1)S(1)} %get-tuple-element.93.full.refs_2_, bf16[2432,64]{1,0:T(8,128)(2,1)S(1)} %get-tuple-element.94.en_ref.refs_4_, bf16[2432,64]{1,0:T(8,128)(2,1)S(1)} %get-tuple-element.95.fin_ref), custom_call_target="tpu_custom_call" | custom-call | tf_op jit(solution)/shard_map/pallas_call | solution.py:246
  110.6 4.7 %collective-permute-done.27 = bf16[256,128]{1,0:T(8,128)(2,1)S(1)} collective-permute-done((bf16[256,128]{1,0:T(8,128)(2,1)S(1)}, bf16[256,128]{1,0:T(8,128)(2,1)S(1)}, u32[]{:S(2)}, u32[]{:S(2)}) %collective-permute-start.27) | collective-permute-done | bytes 65568 | tf_op jit(solution)/shard_map/ppermute | solution.py:421
  115.3 13.3 %shard_map.84 = (bf16[256,128]{1,0:T(8,128)(2,1)S(1)}, f32[256,128]{1,0:T(8,128)S(1)}, f32[16,128]{1,0:T(8,128)S(1)}, f32[512,64]{1,0:T(8,128)S(1)}, f32[512,128...) custom-call(bf16[256,128]{1,0:T(8,128)(2,1)S(1)} %select_select_fusion.sample_ref, ...), custom_call_target="tpu_custom_call" | custom-call | tf_op jit(solution)/shard_map/pallas_call | solution.py:216
  128.6 1.2 collective-permute-start.28
  129.9 2.3 %collective-permute-start.29 = (f32[16,128]{1,0:T(8,128)S(1)}, f32[16,128]{1,0:T(8,128)S(1)}, u32[]{:S(2)}, u32[]{:S(2)}) collective-permute-start(f32[16,128]{1,0:T(8,128)S(1)} %get-tuple-element.105), channel_id=1, source_target_pairs={{0,32},{32,0},{16,48},{48,16},{1,33},{33,1},{17,49},{49,17},{2,34}... | collective-permute-start | bytes 24584 | tf_op jit(solution)/shard_map/ppermute | solution.py:441
  132.2 0.3 collective-permute-start.30
  132.5 4.3 %shard_map.85 = (f32[512,64]{1,0:T(8,128)S(1)}, bf16[512,768]{1,0:T(8,128)(2,1)S(1)}) custom-call(bf16[256,128]{1,0:T(8,128)(2,1)S(1)} %get-tuple-element.120.refs_0_, bf16[512,2432]{1,0:T(8,128)(2,1)S(1)} %get-tuple-element.107.refs_1_, bf16[2560,2560]{1,0:T(8,128)(2,1)S(1)} %get-tuple-element.93.full.refs_2_, ...), custom_call_target="tpu_custom_call" | custom-call | tf_op jit(solution)/shard_map/pallas_call | solution.py:276
  137.0 2.9 %collective-permute-start.32 = (f32[16,128]{1,0:T(8,128)S(1)}, f32[16,128]{1,0:T(8,128)S(1)}, u32[]{:S(2)}, u32[]{:S(2)}) collective-permute-start(f32[16,128]{1,0:T(8,128)S(1)} %add_add_fusion.3), channel_id=1, source_target_pairs={{0,8},{4,12},{8,0},{12,4},{1,9},{5,13},{9,1},{13,5},{2,10},{6,14},... | collective-permute-start | bytes 24584 | tf_op jit(solution)/shard_map/ppermute | solution.py:441
  139.9 0.9 collective-permute-start.33
  140.8 4.8 %shard_map.86 = (f32[512,64]{1,0:T(8,128)S(1)}, bf16[512,1024]{1,0:T(8,128)(2,1)S(1)}) custom-call(bf16[256,128]{1,0:T(8,128)(2,1)S(1)} %get-tuple-element.120.refs_0_, bf16[512,2432]{1,0:T(8,128)(2,1)S(1)} %get-tuple-element.107.refs_1_, bf16[2560,2560]{1,0:T(8,128)(2,1)S(1)} %get-tuple-element.93.full.refs_2_, ...), custom_call_target="tpu_custom_call" | custom-call | tf_op jit(solution)/shard_map/pallas_call | solution.py:276
  145.7 2.1 %collective-permute-start.35 = (f32[16,128]{1,0:T(8,128)S(1)}, f32[16,128]{1,0:T(8,128)S(1)}, u32[]{:S(2)}, u32[]{:S(2)}) collective-permute-start(f32[16,128]{1,0:T(8,128)S(1)} %add_add_fusion.2), channel_id=1, source_target_pairs={{0,2},{1,3},{2,0},{3,1},{4,6},{5,7},{6,4},{7,5},{8,10},{9,11},{10,... | collective-permute-start | bytes 24584 | tf_op jit(solution)/shard_map/ppermute | solution.py:441
  147.8 0.9 collective-permute-start.36
  148.7 3.6 %shard_map.87 = (f32[512,64]{1,0:T(8,128)S(1)}, bf16[512,768]{1,0:T(8,128)(2,1)S(1)}) custom-call(bf16[256,128]{1,0:T(8,128)(2,1)S(1)} %get-tuple-element.120.refs_0_, bf16[512,2432]{1,0:T(8,128)(2,1)S(1)} %get-tuple-element.107.refs_1_, bf16[2560,2560]{1,0:T(8,128)(2,1)S(1)} %get-tuple-element.93.full.refs_2_, ...), custom_call_target="tpu_custom_call" | custom-call | tf_op jit(solution)/shard_map/pallas_call | solution.py:276
  152.3 4.2 %collective-permute-start.37 = (f32[8,128]{1,0:T(8,128)S(1)}, f32[8,128]{1,0:T(8,128)S(1)}, u32[]{:S(2)}, u32[]{:S(2)}) collective-permute-start(f32[8,128]{1,0:T(8,128)S(1)} %slice.84), channel_id=1, source_target_pairs={{16,144},{48,176},{17,145},{49,177},{18,146},{50,178},{19,147},{51... | collective-permute-start | bytes 12296 | tf_op jit(solution)/shard_map/ppermute | solution.py:446
  156.5 0.7 collective-permute-start.38
  157.2 1.9 %collective-permute-start.39 = (f32[256,128]{1,0:T(8,128)S(1)}, f32[256,128]{1,0:T(8,128)S(1)}, u32[]{:S(2)}, u32[]{:S(2)}) collective-permute-start(f32[256,128]{1,0:T(8,128)S(1)} %get-tuple-element.126), channel_id=1, source_target_pairs={{16,144},{48,176},{17,145},{49,177},{18,146},{50,178},{19,147},{51... | collective-permute-start | bytes 393224 | tf_op jit(solution)/shard_map/ppermute | solution.py:433
  159.1 3.9 %shard_map.88 = f32[256,128]{1,0:T(8,128)S(1)} custom-call(f32[16,128]{1,0:T(8,128)S(1)} %add_add_fusion.1.sums_ref, bf16[2560,64]{1,0:T(8,128)(2,1)S(1)} %get-tuple-element.102.close_ref.refs_3_, f32[2560,64]{1,0:T(8,128)S(1)} %get-tuple-element.127.pf_ref, f32[64,64]{1,0:T(8,128)S(1)} %get-tuple-element.128.ef_ref, ...), custom_call_target="tpu_custom_call" | custom-call | tf_op jit(solution)/shard_map/pallas_call | solution.py:326
  163.9 0.7 collective-permute-start.40
  164.6 1.3 collective-permute-start.41
  165.9 0.7 collective-permute-start.42
  166.6 0.7 collective-permute-start.43
  167.3 14.1 %collective-permute-done.41 = f32[256,128]{1,0:T(8,128)S(1)} collective-permute-done((f32[256,128]{1,0:T(8,128)S(1)}, f32[256,128]{1,0:T(8,128)S(1)}, u32[]{:S(2)}, u32[]{:S(2)}) %collective-permute-start.41) | collective-permute-done | bytes 131104 | tf_op jit(solution)/shard_map/ppermute | solution.py:460
  181.5 0.7 pad_maximum_fusion
  (105 shorter events, 3.1 us)
Async XLA Ops:
  0.0 27.0 %copy-start = (bf16[193,64]{0,1:T(8,128)(2,1)S(1)}, bf16[193,64]{0,1:T(8,128)(2,1)}, u32[]{:S(2)}) copy-start(bf16[193,64]{0,1:T(8,128)(2,1)} %param.15) | copy-start | bytes 74116
  1.1 0.7 collective-permute-start
  1.8 8.0 %collective-permute-start.1 = (bf16[40,2560]{1,0:T(8,128)(2,1)S(1)}, bf16[40,2560]{1,0:T(8,128)(2,1)S(1)}, u32[]{:S(2)}, u32[]{:S(2)}) collective-permute-start(bf16[40,2560]{1,0:T(8,128)(2,1)S(1)} %broadcast_select_fusion), channel_id=1, source_target_pairs={{0,32},{32,0},{16,48},{48,16},{1,33},{33,1},{17,49},{49,17},{2,34}... | collective-permute-start | bytes 614408 | tf_op jit(solution)/shard_map/ppermute | solution.py:360
  9.8 7.9 %collective-permute-start.2 = (bf16[40,2560]{1,0:T(8,128)(2,1)S(1)}, bf16[40,2560]{1,0:T(8,128)(2,1)S(1)}, u32[]{:S(2)}, u32[]{:S(2)}) collective-permute-start(bf16[40,2560]{1,0:T(8,128)(2,1)S(1)} %get-tuple-element.72), channel_id=1, source_target_pairs={{0,4},{4,8},{8,12},{12,0},{1,5},{5,9},{9,13},{13,1},{2,6},{6,10},{... | collective-permute-start | bytes 614408 | tf_op jit(solution)/shard_map/ppermute | solution.py:346
  11.1 7.7 %collective-permute-start.3 = (bf16[40,2560]{1,0:T(8,128)(2,1)S(1)}, bf16[40,2560]{1,0:T(8,128)(2,1)S(1)}, u32[]{:S(2)}, u32[]{:S(2)}) collective-permute-start(bf16[40,2560]{1,0:T(8,128)(2,1)S(1)} %get-tuple-element.72), channel_id=1, source_target_pairs={{0,8},{4,12},{8,0},{12,4},{1,9},{5,13},{9,1},{13,5},{2,10},{6,14},... | collective-permute-start | bytes 614408 | tf_op jit(solution)/shard_map/ppermute | solution.py:346
  12.0 6.9 %collective-permute-start.4 = (bf16[40,2560]{1,0:T(8,128)(2,1)S(1)}, bf16[40,2560]{1,0:T(8,128)(2,1)S(1)}, u32[]{:S(2)}, u32[]{:S(2)}) collective-permute-start(bf16[40,2560]{1,0:T(8,128)(2,1)S(1)} %get-tuple-element.72), channel_id=1, source_target_pairs={{0,12},{4,0},{8,4},{12,8},{1,13},{5,1},{9,5},{13,9},{2,14},{6,2},{... | collective-permute-start | bytes 614408 | tf_op jit(solution)/shard_map/ppermute | solution.py:346
  13.8 5.9 %collective-permute-start.5 = (bf16[40,2560]{1,0:T(8,128)(2,1)S(1)}, bf16[40,2560]{1,0:T(8,128)(2,1)S(1)}, u32[]{:S(2)}, u32[]{:S(2)}) collective-permute-start(bf16[40,2560]{1,0:T(8,128)(2,1)S(1)} %get-tuple-element.76), channel_id=1, source_target_pairs={{0,1},{1,2},{2,3},{3,0},{4,5},{5,6},{6,7},{7,4},{8,9},{9,10},{10,1... | collective-permute-start | bytes 614408 | tf_op jit(solution)/shard_map/ppermute | solution.py:346
  15.1 8.0 %collective-permute-start.6 = (bf16[40,2560]{1,0:T(8,128)(2,1)S(1)}, bf16[40,2560]{1,0:T(8,128)(2,1)S(1)}, u32[]{:S(2)}, u32[]{:S(2)}) collective-permute-start(bf16[40,2560]{1,0:T(8,128)(2,1)S(1)} %get-tuple-element.76), channel_id=1, source_target_pairs={{0,2},{1,3},{2,0},{3,1},{4,6},{5,7},{6,4},{7,5},{8,10},{9,11},{10,... | collective-permute-start | bytes 614408 | tf_op jit(solution)/shard_map/ppermute | solution.py:346
  17.8 5.3 %collective-permute-start.7 = (bf16[40,2560]{1,0:T(8,128)(2,1)S(1)}, bf16[40,2560]{1,0:T(8,128)(2,1)S(1)}, u32[]{:S(2)}, u32[]{:S(2)}) collective-permute-start(bf16[40,2560]{1,0:T(8,128)(2,1)S(1)} %get-tuple-element.76), channel_id=1, source_target_pairs={{0,3},{1,0},{2,1},{3,2},{4,7},{5,4},{6,5},{7,6},{8,11},{9,8},{10,9... | collective-permute-start | bytes 614408 | tf_op jit(solution)/shard_map/ppermute | solution.py:346
  18.8 8.0 %copy-start.8 = (s32[8,77]{1,0:T(8,128)S(1)}, s32[8,77]{1,0:T(8,128)}, u32[]{:S(2)}) copy-start(s32[8,77]{1,0:T(8,128)} %param.11) | copy-start | bytes 7396
  18.8 16.1 %copy-start.7 = (bf16[8,64,64]{2,1,0:T(8,128)(2,1)S(1)}, bf16[8,64,64]{2,1,0:T(8,128)(2,1)}, u32[]{:S(2)}) copy-start(bf16[8,64,64]{2,1,0:T(8,128)(2,1)} %param.8) | copy-start | bytes 196612
  23.2 56.3 %copy-start.9 = (s32[8]{0:T(128)S(1)}, s32[8]{0:T(128)}, u32[]{:S(2)}) copy-start(s32[8]{0:T(128)} %param.10) | copy-start | bytes 100
  23.4 30.4 %collective-permute-start.10 = (bf16[160,2560]{1,0:T(8,128)(2,1)S(1)}, bf16[160,2560]{1,0:T(8,128)(2,1)S(1)}, u32[]{:S(2)}, u32[]{:S(2)}) collective-permute-start(bf16[160,2560]{1,0:T(8,128)(2,1)S(1)} %bitcast.38), channel_id=1, source_target_pairs={{0,3},{1,0},{2,1},{3,2},{4,7},{5,4},{6,5},{7,6},{8,11},{9,8},{10,9... | collective-permute-start | bytes 2457608 | tf_op jit(solution)/shard_map/ppermute | solution.py:346
  25.3 30.2 %collective-permute-start.8 = (bf16[160,2560]{1,0:T(8,128)(2,1)S(1)}, bf16[160,2560]{1,0:T(8,128)(2,1)S(1)}, u32[]{:S(2)}, u32[]{:S(2)}) collective-permute-start(bf16[160,2560]{1,0:T(8,128)(2,1)S(1)} %bitcast.39), channel_id=1, source_target_pairs={{0,1},{1,2},{2,3},{3,0},{4,5},{5,6},{6,7},{7,4},{8,9},{9,10},{10,1... | collective-permute-start | bytes 2457608 | tf_op jit(solution)/shard_map/ppermute | solution.py:346
  25.3 30.2 %collective-permute-start.11 = (bf16[160,2560]{1,0:T(8,128)(2,1)S(1)}, bf16[160,2560]{1,0:T(8,128)(2,1)}, u32[]{:S(2)}, u32[]{:S(2)}) collective-permute-start(bf16[160,2560]{1,0:T(8,128)(2,1)S(1)} %bitcast.33), channel_id=1, source_target_pairs={{0,12},{4,0},{8,4},{12,8},{1,13},{5,1},{9,5},{13,9},{2,14},{6,2},{... | collective-permute-start | bytes 2457608 | tf_op jit(solution)/shard_map/ppermute | solution.py:346
  26.8 28.7 %collective-permute-start.9 = (bf16[160,2560]{1,0:T(8,128)(2,1)S(1)}, bf16[160,2560]{1,0:T(8,128)(2,1)}, u32[]{:S(2)}, u32[]{:S(2)}) collective-permute-start(bf16[160,2560]{1,0:T(8,128)(2,1)S(1)} %bitcast.34), channel_id=1, source_target_pairs={{0,4},{4,8},{8,12},{12,0},{1,5},{5,9},{9,13},{13,1},{2,6},{6,10},{... | collective-permute-start | bytes 2457608 | tf_op jit(solution)/shard_map/ppermute | solution.py:346
  27.2 9.0 %collective-permute-start.13 = (f32[8,128]{1,0:T(8,128)S(1)}, f32[8,128]{1,0:T(8,128)S(1)}, u32[]{:S(2)}, u32[]{:S(2)}) collective-permute-start(f32[8,128]{1,0:T(8,128)S(1)} %concatenate.28), channel_id=1, source_target_pairs={{0,16},{16,0},{32,48},{48,32},{1,17},{17,1},{33,49},{49,33},{2,18}... | collective-permute-start | bytes 12296 | tf_op jit(solution)/shard_map/ppermute | solution.py:402
  36.2 9.7 %collective-permute-start.14 = (f32[8,128]{1,0:T(8,128)S(1)}, f32[8,128]{1,0:T(8,128)S(1)}, u32[]{:S(2)}, u32[]{:S(2)}) collective-permute-start(f32[8,128]{1,0:T(8,128)S(1)} %pad_add_fusion.1), channel_id=1, source_target_pairs={{0,128},{128,0},{1,129},{129,1},{2,130},{130,2},{3,131},{131,3},{4... | collective-permute-start | bytes 12296 | tf_op jit(solution)/shard_map/ppermute | solution.py:403
  45.9 4.6 %collective-permute-start.12 = (bf16[512,128]{1,0:T(8,128)(2,1)S(1)}, bf16[512,128]{1,0:T(8,128)(2,1)S(1)}, u32[]{:S(2)}, u32[]{:S(2)}) collective-permute-start(bf16[512,128]{1,0:T(8,128)(2,1)S(1)} %maximum_maximum_fusion), channel_id=1, source_target_pairs={{0,16},{16,0},{32,48},{48,32},{1,17},{17,1},{33,49},{49,33},{2,18}... | collective-permute-start | bytes 393224 | tf_op jit(solution)/shard_map/ppermute | solution.py:394
  50.5 13.6 %collective-permute-start.15 = (bf16[160,2560]{1,0:T(8,128)(2,1)S(1)}, bf16[160,2560]{1,0:T(8,128)(2,1)}, u32[]{:S(2)}, u32[]{:S(2)}) collective-permute-start(bf16[160,2560]{1,0:T(8,128)(2,1)S(1)} %bitcast.40), channel_id=1, source_target_pairs={{0,2},{1,3},{2,0},{3,1},{4,6},{5,7},{6,4},{7,5},{8,10},{9,11},{10,... | collective-permute-start | bytes 2457608 | tf_op jit(solution)/shard_map/ppermute | solution.py:346
  53.8 19.2 %collective-permute-start.16 = (bf16[160,2560]{1,0:T(8,128)(2,1)S(1)}, bf16[160,2560]{1,0:T(8,128)(2,1)}, u32[]{:S(2)}, u32[]{:S(2)}) collective-permute-start(bf16[160,2560]{1,0:T(8,128)(2,1)S(1)} %bitcast.35), channel_id=1, source_target_pairs={{0,8},{4,12},{8,0},{12,4},{1,9},{5,13},{9,1},{13,5},{2,10},{6,14},... | collective-permute-start | bytes 2457608 | tf_op jit(solution)/shard_map/ppermute | solution.py:346
  55.5 20.7 %collective-permute-start.17 = (bf16[160,2560]{1,0:T(8,128)(2,1)S(1)}, bf16[160,2560]{1,0:T(8,128)(2,1)S(1)}, u32[]{:S(2)}, u32[]{:S(2)}) collective-permute-start(bf16[160,2560]{1,0:T(8,128)(2,1)S(1)} %bitcast.41), channel_id=1, source_target_pairs={{0,64},{64,0},{1,65},{65,1},{2,66},{66,2},{3,67},{67,3},{4,68},{68... | collective-permute-start | bytes 2457608 | tf_op jit(solution)/shard_map/ppermute | solution.py:370
  63.6 13.6 %collective-permute-start.18 = (bf16[160,2560]{1,0:T(8,128)(2,1)S(1)}, bf16[160,2560]{1,0:T(8,128)(2,1)S(1)}, u32[]{:S(2)}, u32[]{:S(2)}) collective-permute-start(bf16[160,2560]{1,0:T(8,128)(2,1)S(1)} %collective-permute-done.8.refs_1_), channel_id=1, source_target_pairs={{0,64},{64,0},{1,65},{65,1},{2,66},{66,2},{3,67},{67,3},{4,68},{68... | collective-permute-start | bytes 2457608 | tf_op jit(solution)/shard_map/ppermute | solution.py:370
  63.9 14.7 %collective-permute-start.20 = (bf16[160,2560]{1,0:T(8,128)(2,1)S(1)}, bf16[160,2560]{1,0:T(8,128)(2,1)S(1)}, u32[]{:S(2)}, u32[]{:S(2)}) collective-permute-start(bf16[160,2560]{1,0:T(8,128)(2,1)S(1)} %collective-permute-done.10.refs_3_), channel_id=1, source_target_pairs={{0,64},{64,0},{1,65},{65,1},{2,66},{66,2},{3,67},{67,3},{4,68},{68... | collective-permute-start | bytes 2457608 | tf_op jit(solution)/shard_map/ppermute | solution.py:370
  64.1 15.9 %collective-permute-start.21 = (bf16[160,2560]{1,0:T(8,128)(2,1)S(1)}, bf16[160,2560]{1,0:T(8,128)(2,1)}, u32[]{:S(2)}, u32[]{:S(2)}) collective-permute-start(bf16[160,2560]{1,0:T(8,128)(2,1)S(1)} %bitcast.36), channel_id=1, source_target_pairs={{0,64},{64,0},{1,65},{65,1},{2,66},{66,2},{3,67},{67,3},{4,68},{68... | collective-permute-start | bytes 2457608 | tf_op jit(solution)/shard_map/ppermute | solution.py:370
  73.0 7.0 %collective-permute-start.22 = (bf16[160,2560]{1,0:T(8,128)(2,1)}, bf16[160,2560]{1,0:T(8,128)(2,1)}, u32[]{:S(2)}, u32[]{:S(2)}) collective-permute-start(bf16[160,2560]{1,0:T(8,128)(2,1)} %collective-permute-done.9.refs_5_), channel_id=1, source_target_pairs={{0,64},{64,0},{1,65},{65,1},{2,66},{66,2},{3,67},{67,3},{4,68},{68... | collective-permute-start | bytes 2457608 | tf_op jit(solution)/shard_map/ppermute | solution.py:370
  76.2 0.9 copy-start.1
  77.1 2.9 %collective-permute-start.24 = (bf16[160,2560]{1,0:T(8,128)(2,1)}, bf16[160,2560]{1,0:T(8,128)(2,1)}, u32[]{:S(2)}, u32[]{:S(2)}) collective-permute-start(bf16[160,2560]{1,0:T(8,128)(2,1)} %collective-permute-done.11.refs_7_), channel_id=1, source_target_pairs={{0,64},{64,0},{1,65},{65,1},{2,66},{66,2},{3,67},{67,3},{4,68},{68... | collective-permute-start | bytes 2457608 | tf_op jit(solution)/shard_map/ppermute | solution.py:370
  77.2 0.9 copy-start.3
  78.1 2.9 %collective-permute-start.19 = (bf16[160,2560]{1,0:T(8,128)(2,1)}, bf16[160,2560]{1,0:T(8,128)(2,1)}, u32[]{:S(2)}, u32[]{:S(2)}) collective-permute-start(bf16[160,2560]{1,0:T(8,128)(2,1)} %collective-permute-done.15.refs_2_), channel_id=1, source_target_pairs={{0,64},{64,0},{1,65},{65,1},{2,66},{66,2},{3,67},{67,3},{4,68},{68... | collective-permute-start | bytes 2457608 | tf_op jit(solution)/shard_map/ppermute | solution.py:373
  78.6 0.9 copy-start.5
  79.5 2.7 %collective-permute-start.23 = (bf16[160,2560]{1,0:T(8,128)(2,1)}, bf16[160,2560]{1,0:T(8,128)(2,1)}, u32[]{:S(2)}, u32[]{:S(2)}) collective-permute-start(bf16[160,2560]{1,0:T(8,128)(2,1)} %collective-permute-done.16.refs_6_), channel_id=1, source_target_pairs={{0,64},{64,0},{1,65},{65,1},{2,66},{66,2},{3,67},{67,3},{4,68},{68... | collective-permute-start | bytes 2457608 | tf_op jit(solution)/shard_map/ppermute | solution.py:373
  82.2 1.1 copy-start.2
  83.3 1.1 copy-start.4
  84.5 1.1 copy-start.6
  102.5 8.1 %collective-permute-start.25 = (bf16[256,128]{1,0:T(8,128)(2,1)S(1)}, bf16[256,128]{1,0:T(8,128)(2,1)S(1)}, u32[]{:S(2)}, u32[]{:S(2)}) collective-permute-start(bf16[256,128]{1,0:T(8,128)(2,1)S(1)} %get-tuple-element.97), channel_id=1, source_target_pairs={{0,144},{32,176},{1,145},{33,177},{2,146},{34,178},{3,147},{35,179... | collective-permute-start | bytes 196616 | tf_op jit(solution)/shard_map/ppermute | solution.py:419
  103.1 7.4 %collective-permute-start.26 = (bf16[256,128]{1,0:T(8,128)(2,1)S(1)}, bf16[256,128]{1,0:T(8,128)(2,1)S(1)}, u32[]{:S(2)}, u32[]{:S(2)}) collective-permute-start(bf16[256,128]{1,0:T(8,128)(2,1)S(1)} %get-tuple-element.97), channel_id=1, source_target_pairs={{0,128},{32,160},{1,129},{33,161},{2,130},{34,162},{3,131},{35,163... | collective-permute-start | bytes 196616 | tf_op jit(solution)/shard_map/ppermute | solution.py:420
  103.8 11.5 %collective-permute-start.27 = (bf16[256,128]{1,0:T(8,128)(2,1)S(1)}, bf16[256,128]{1,0:T(8,128)(2,1)S(1)}, u32[]{:S(2)}, u32[]{:S(2)}) collective-permute-start(bf16[256,128]{1,0:T(8,128)(2,1)S(1)} %get-tuple-element.97), channel_id=1, source_target_pairs={{0,16},{32,48},{1,17},{33,49},{2,18},{34,50},{3,19},{35,51},{4,20}... | collective-permute-start | bytes 196616 | tf_op jit(solution)/shard_map/ppermute | solution.py:421
  128.6 8.2 %collective-permute-start.28 = (f32[16,128]{1,0:T(8,128)S(1)}, f32[16,128]{1,0:T(8,128)S(1)}, u32[]{:S(2)}, u32[]{:S(2)}) collective-permute-start(f32[16,128]{1,0:T(8,128)S(1)} %get-tuple-element.105), channel_id=1, source_target_pairs={{0,64},{64,0},{1,65},{65,1},{2,66},{66,2},{3,67},{67,3},{4,68},{68... | collective-permute-start | bytes 24584 | tf_op jit(solution)/shard_map/ppermute | solution.py:441
  129.9 7.0 %collective-permute-start.29 = (f32[16,128]{1,0:T(8,128)S(1)}, f32[16,128]{1,0:T(8,128)S(1)}, u32[]{:S(2)}, u32[]{:S(2)}) collective-permute-start(f32[16,128]{1,0:T(8,128)S(1)} %get-tuple-element.105), channel_id=1, source_target_pairs={{0,32},{32,0},{16,48},{48,16},{1,33},{33,1},{17,49},{49,17},{2,34}... | collective-permute-start | bytes 24584 | tf_op jit(solution)/shard_map/ppermute | solution.py:441
  132.2 4.7 %collective-permute-start.30 = (f32[16,128]{1,0:T(8,128)S(1)}, f32[16,128]{1,0:T(8,128)S(1)}, u32[]{:S(2)}, u32[]{:S(2)}) collective-permute-start(f32[16,128]{1,0:T(8,128)S(1)} %get-tuple-element.105), channel_id=1, source_target_pairs={{0,96},{16,112},{32,64},{48,80},{64,32},{80,48},{96,0},{112,16},{1... | collective-permute-start | bytes 24584 | tf_op jit(solution)/shard_map/ppermute | solution.py:441
  136.9 8.6 %collective-permute-start.31 = (f32[16,128]{1,0:T(8,128)S(1)}, f32[16,128]{1,0:T(8,128)S(1)}, u32[]{:S(2)}, u32[]{:S(2)}) collective-permute-start(f32[16,128]{1,0:T(8,128)S(1)} %add_add_fusion.3), channel_id=1, source_target_pairs={{0,4},{4,8},{8,12},{12,0},{1,5},{5,9},{9,13},{13,1},{2,6},{6,10},{... | collective-permute-start | bytes 24584 | tf_op jit(solution)/shard_map/ppermute | solution.py:441
  137.0 8.6 %collective-permute-start.32 = (f32[16,128]{1,0:T(8,128)S(1)}, f32[16,128]{1,0:T(8,128)S(1)}, u32[]{:S(2)}, u32[]{:S(2)}) collective-permute-start(f32[16,128]{1,0:T(8,128)S(1)} %add_add_fusion.3), channel_id=1, source_target_pairs={{0,8},{4,12},{8,0},{12,4},{1,9},{5,13},{9,1},{13,5},{2,10},{6,14},... | collective-permute-start | bytes 24584 | tf_op jit(solution)/shard_map/ppermute | solution.py:441
  139.9 5.6 %collective-permute-start.33 = (f32[16,128]{1,0:T(8,128)S(1)}, f32[16,128]{1,0:T(8,128)S(1)}, u32[]{:S(2)}, u32[]{:S(2)}) collective-permute-start(f32[16,128]{1,0:T(8,128)S(1)} %add_add_fusion.3), channel_id=1, source_target_pairs={{0,12},{4,0},{8,4},{12,8},{1,13},{5,1},{9,5},{13,9},{2,14},{6,2},{... | collective-permute-start | bytes 24584 | tf_op jit(solution)/shard_map/ppermute | solution.py:441
  145.6 6.7 %collective-permute-start.34 = (f32[16,128]{1,0:T(8,128)S(1)}, f32[16,128]{1,0:T(8,128)S(1)}, u32[]{:S(2)}, u32[]{:S(2)}) collective-permute-start(f32[16,128]{1,0:T(8,128)S(1)} %add_add_fusion.2), channel_id=1, source_target_pairs={{0,1},{1,2},{2,3},{3,0},{4,5},{5,6},{6,7},{7,4},{8,9},{9,10},{10,1... | collective-permute-start | bytes 24584 | tf_op jit(solution)/shard_map/ppermute | solution.py:441
  145.7 6.6 %collective-permute-start.35 = (f32[16,128]{1,0:T(8,128)S(1)}, f32[16,128]{1,0:T(8,128)S(1)}, u32[]{:S(2)}, u32[]{:S(2)}) collective-permute-start(f32[16,128]{1,0:T(8,128)S(1)} %add_add_fusion.2), channel_id=1, source_target_pairs={{0,2},{1,3},{2,0},{3,1},{4,6},{5,7},{6,4},{7,5},{8,10},{9,11},{10,... | collective-permute-start | bytes 24584 | tf_op jit(solution)/shard_map/ppermute | solution.py:441
  147.8 4.5 %collective-permute-start.36 = (f32[16,128]{1,0:T(8,128)S(1)}, f32[16,128]{1,0:T(8,128)S(1)}, u32[]{:S(2)}, u32[]{:S(2)}) collective-permute-start(f32[16,128]{1,0:T(8,128)S(1)} %add_add_fusion.2), channel_id=1, source_target_pairs={{0,3},{1,0},{2,1},{3,2},{4,7},{5,4},{6,5},{7,6},{8,11},{9,8},{10,9... | collective-permute-start | bytes 24584 | tf_op jit(solution)/shard_map/ppermute | solution.py:441
  152.3 10.7 %collective-permute-start.37 = (f32[8,128]{1,0:T(8,128)S(1)}, f32[8,128]{1,0:T(8,128)S(1)}, u32[]{:S(2)}, u32[]{:S(2)}) collective-permute-start(f32[8,128]{1,0:T(8,128)S(1)} %slice.84), channel_id=1, source_target_pairs={{16,144},{48,176},{17,145},{49,177},{18,146},{50,178},{19,147},{51... | collective-permute-start | bytes 12296 | tf_op jit(solution)/shard_map/ppermute | solution.py:446
  156.5 7.1 %collective-permute-start.38 = (f32[256,128]{1,0:T(8,128)S(1)}, f32[256,128]{1,0:T(8,128)S(1)}, u32[]{:S(2)}, u32[]{:S(2)}) collective-permute-start(f32[256,128]{1,0:T(8,128)S(1)} %get-tuple-element.126), channel_id=1, source_target_pairs={{128,144},{160,176},{129,145},{161,177},{130,146},{162,178},{131,1... | collective-permute-start | bytes 393224 | tf_op jit(solution)/shard_map/ppermute | solution.py:434
  157.2 6.4 %collective-permute-start.39 = (f32[256,128]{1,0:T(8,128)S(1)}, f32[256,128]{1,0:T(8,128)S(1)}, u32[]{:S(2)}, u32[]{:S(2)}) collective-permute-start(f32[256,128]{1,0:T(8,128)S(1)} %get-tuple-element.126), channel_id=1, source_target_pairs={{16,144},{48,176},{17,145},{49,177},{18,146},{50,178},{19,147},{51... | collective-permute-start | bytes 393224 | tf_op jit(solution)/shard_map/ppermute | solution.py:433
  163.9 3.3 %collective-permute-start.40 = (f32[256,128]{1,0:T(8,128)S(1)}, f32[256,128]{1,0:T(8,128)S(1)}, u32[]{:S(2)}, u32[]{:S(2)}) collective-permute-start(f32[256,128]{1,0:T(8,128)S(1)} %fusion), channel_id=1, source_target_pairs={{144,0},{176,32},{208,16},{240,48},{145,1},{177,33},{209,17},{241,... | collective-permute-start | bytes 393224 | tf_op jit(solution)/shard_map/ppermute | solution.py:460
  164.6 16.8 %collective-permute-start.41 = (f32[256,128]{1,0:T(8,128)S(1)}, f32[256,128]{1,0:T(8,128)S(1)}, u32[]{:S(2)}, u32[]{:S(2)}) collective-permute-start(f32[256,128]{1,0:T(8,128)S(1)} %fusion), channel_id=1, source_target_pairs={{144,64},{176,96},{208,80},{240,112},{145,65},{177,97},{209,81},{2... | collective-permute-start | bytes 393224 | tf_op jit(solution)/shard_map/ppermute | solution.py:460
  165.9 15.5 %collective-permute-start.42 = (f32[256,128]{1,0:T(8,128)S(1)}, f32[256,128]{1,0:T(8,128)S(1)}, u32[]{:S(2)}, u32[]{:S(2)}) collective-permute-start(f32[256,128]{1,0:T(8,128)S(1)} %fusion), channel_id=1, source_target_pairs={{144,128},{176,160},{208,144},{240,176},{145,129},{177,161},{209,1... | collective-permute-start | bytes 393224 | tf_op jit(solution)/shard_map/ppermute | solution.py:460
  166.6 14.8 %collective-permute-start.43 = (f32[256,128]{1,0:T(8,128)S(1)}, f32[256,128]{1,0:T(8,128)S(1)}, u32[]{:S(2)}, u32[]{:S(2)}) collective-permute-start(f32[256,128]{1,0:T(8,128)S(1)} %fusion), channel_id=1, source_target_pairs={{144,192},{176,224},{208,208},{240,240},{145,193},{177,225},{209,2... | collective-permute-start | bytes 393224 | tf_op jit(solution)/shard_map/ppermute | solution.py:460

commit v2 on v1

--- a/solution.py
+++ b/solution.py
@@ -89,7 +89,7 @@
     lax.fori_loop(0, D // 128, cut, 0)
 
 
-def forward(rows, close_ref, en_ref, fin_ref, copies, full, active, wide, normed, squares):
+def activate(rows, close_ref, active):
     def act(i, _):
         at = pl.multiple_of(i * 256, 256)
         hidden = mm_nt(rows, close_ref[pl.ds(at, 256), :])
@@ -97,9 +97,10 @@
         return 0
 
     lax.fori_loop(0, KDIM // 256, act, 0)
+
+
+def forward(rows, en_ref, fin_ref, full, active, wide, normed, squares):
     squares[...] = jnp.zeros((ROWS, 128), f32)
-    for copy in copies:
-        copy.wait()
 
     def tile(at, size):
         for r in range(0, ROWS, HALF):
@@ -154,11 +155,24 @@
     for copy in small:
         copy.wait()
     order_tails(where_ref, tails, close_ref, en_ref, fin_ref, padded)
-    rows = unpack(rows_ref[...])
-    projected = forward(
-        rows, close_ref, en_ref, fin_ref, copies, full, active, wide, normed, squares
-    )
-    out_ref[...] = pack((rows.astype(f32) + projected)).astype(bf16)
+    mine = where_ref[3] == 1
+
+    @pl.when(mine)
+    def _():
+        activate(unpack(rows_ref[...]), close_ref, active)
+
+    for copy in copies:
+        copy.wait()
+
+    @pl.when(mine)
+    def _():
+        rows = unpack(rows_ref[...])
+        projected = forward(rows, en_ref, fin_ref, full, active, wide, normed, squares)
+        out_ref[...] = pack((rows.astype(f32) + projected)).astype(bf16)
+
+    @pl.when(jnp.logical_not(mine))
+    def _():
+        out_ref[...] = jnp.zeros((HALF, 128), bf16)
 
 
 def student(where, rows, pieces):
@@ -196,9 +210,8 @@
     packed = ((1.0 - level) * sample + level * renoise_ref[...].astype(f32)).astype(bf16)
     rows_ref[...] = packed
     rows = unpack(packed)
-    projected = forward(
-        rows, close_ref, en_ref, fin_ref, (), full, active, wide, normed, squares
-    )
+    activate(rows, close_ref, active)
+    projected = forward(rows, en_ref, fin_ref, full, active, wide, normed, squares)
     proj_ref[...] = projected
     judged = rows.astype(f32) + projected
     pred = packed.astype(f32) - level * pack(judged)
@@ -412,9 +425,9 @@
     level = jnp.broadcast_to(level[:, None, None], (8, 64, CH))
     level = packed_rows(level)
 
-    where = jnp.stack([core, x, y]).astype(jnp.int32)
+    is_student = (h == 0) & (parity == 0)
+    where = jnp.stack([core, x, y, is_student.astype(jnp.int32)]).astype(jnp.int32)
     sample, tables = student(where, noise, pieces)
-    is_student = (h == 0) & (parity == 0)
     got = [
         lax.ppermute(sample, ("h", "z"), [(0, 5), (2, 7)]),
         lax.ppermute(sample, ("h", "z"), [(0, 4), (2, 6)]),

time: 183 us -> 177 us (0.967)
  Pallas kernels: 51.9 us -> 39.4 us
  waiting for transfers between devices: 34.2 us -> 41.5 us
    pallas_call x1, Pallas kernels: 16.9 us -> 4.35 us  [student(): call(student_body, [((HALF, 128), bf16), ((KDIM, KDIM), bf16), ((KDIM, CH...]
    ppermute x1, waiting for transfers between devices: 4.71 us -> 12.3 us  [on_device(): lax.ppermute(sample, ('h', 'z'), [(0, 1), (2, 3)])]
  transfers between devices with their start and end apart: 44 -> 44, of which waited for: 10 -> 11; matrix products, arithmetic and copies ran while one was open for 2% -> 2% of each run, Pallas kernels for 12% -> 12%
where the time goes in v2:
time: 177 us; the launch traced here: 176 us
  starting transfers between devices  83.4 us (47%)
  waiting for transfers between devices  41.5 us (23%)
  Pallas kernels  39.4 us (22%)
  local copies, waits for them, and re-layouts  9.78 us (6%)
    ppermute x6, starting transfers between devices, gather_weights(): swaps = {i: lax.ppermute(v, 'c', CORE) for i, v in zip(first, ready)}  20.7 us
    ppermute x12, starting transfers between devices, gather_axis(): lax.ppermute(piece, axis, shift(4, k))  17.1 us
    ppermute x4, waiting for transfers between devices, on_device(): landed = landed + lax.ppermute(result, NET + ('z',), pairs)  13.7 us
    pallas_call x1, Pallas kernels, second(): call(second_body, [((HALF, 128), bf16), ((HALF, 128), f32), ((16, 128), f...  13.3 us
    pallas_call x3, Pallas kernels, back_step(): call(lambda *refs: back_body(base, tiles, *refs), [((ROWS, CH), f32), ((R...  12.7 us
    ppermute x1, waiting for transfers between devices, on_device(): lax.ppermute(sample, ('h', 'z'), [(0, 1), (2, 3)])  12.3 us
    ppermute x9, starting transfers between devices, on_device(): moved = [lax.ppermute(sums, axis, pairs) for axis, pairs in sends]  10.4 us
    ppermute x1, starting transfers between devices, exchange(): text = text + lax.ppermute(text, 'h', CORE)  8.7 us
  transfers between devices with their start and end apart: 44, of which 11 were waited for; matrix products, arithmetic and copies ran while one was open for 2% of the time, Pallas kernels for 12%

profile of v2, /device:TPU:35, one launch (start us, length us, event | category | flops | bytes accessed | tf_op | source)
XLA Modules:
  0.0 176.5 jit_solution(17558059636498812946)
XLA Ops:
  0.0 1.0 concatenate.24
  1.1 0.7 collective-permute-start
  1.8 3.1 %collective-permute-start.1 = (bf16[40,2560]{1,0:T(8,128)(2,1)S(1)}, bf16[40,2560]{1,0:T(8,128)(2,1)S(1)}, u32[]{:S(2)}, u32[]{:S(2)}) collective-permute-start(bf16[40,2560]{1,0:T(8,128)(2,1)S(1)} %broadcast_select_fusion), channel_id=1, source_target_pairs={{0,32},{32,0},{16,48},{48,16},{1,33},{33,1},{17,49},{49,17},{2,34}... | collective-permute-start | bytes 614408 | tf_op jit(solution)/shard_map/ppermute | solution.py:373
  4.9 4.9 %collective-permute-done.1 = bf16[40,2560]{1,0:T(8,128)(2,1)S(1)} collective-permute-done((bf16[40,2560]{1,0:T(8,128)(2,1)S(1)}, bf16[40,2560]{1,0:T(8,128)(2,1)S(1)}, u32[]{:S(2)}, u32[]{:S(2)}) %collective-permute-start.1) | collective-permute-done | bytes 204832 | tf_op jit(solution)/shard_map/ppermute | solution.py:373
  9.8 1.3 collective-permute-start.2
  11.1 0.8 collective-permute-start.3
  12.0 1.9 %collective-permute-start.4 = (bf16[40,2560]{1,0:T(8,128)(2,1)S(1)}, bf16[40,2560]{1,0:T(8,128)(2,1)S(1)}, u32[]{:S(2)}, u32[]{:S(2)}) collective-permute-start(bf16[40,2560]{1,0:T(8,128)(2,1)S(1)} %get-tuple-element.72), channel_id=1, source_target_pairs={{0,12},{4,0},{8,4},{12,8},{1,13},{5,1},{9,5},{13,9},{2,14},{6,2},{... | collective-permute-start | bytes 614408 | tf_op jit(solution)/shard_map/ppermute | solution.py:359
  13.8 1.3 collective-permute-start.5
  15.1 2.6 %collective-permute-start.6 = (bf16[40,2560]{1,0:T(8,128)(2,1)S(1)}, bf16[40,2560]{1,0:T(8,128)(2,1)S(1)}, u32[]{:S(2)}, u32[]{:S(2)}) collective-permute-start(bf16[40,2560]{1,0:T(8,128)(2,1)S(1)} %get-tuple-element.76), channel_id=1, source_target_pairs={{0,2},{1,3},{2,0},{3,1},{4,6},{5,7},{6,4},{7,5},{8,10},{9,11},{10,... | collective-permute-start | bytes 614408 | tf_op jit(solution)/shard_map/ppermute | solution.py:359
  17.8 1.1 collective-permute-start.7
  18.8 0.9 collective-permute-done.5
  19.7 3.4 %collective-permute-done.6 = bf16[40,2560]{1,0:T(8,128)(2,1)S(1)} collective-permute-done((bf16[40,2560]{1,0:T(8,128)(2,1)S(1)}, bf16[40,2560]{1,0:T(8,128)(2,1)S(1)}, u32[]{:S(2)}, u32[]{:S(2)}) %collective-permute-start.6) | collective-permute-done | bytes 204832 | tf_op jit(solution)/shard_map/ppermute | solution.py:359
  23.4 1.9 %collective-permute-start.10 = (bf16[160,2560]{1,0:T(8,128)(2,1)S(1)}, bf16[160,2560]{1,0:T(8,128)(2,1)S(1)}, u32[]{:S(2)}, u32[]{:S(2)}) collective-permute-start(bf16[160,2560]{1,0:T(8,128)(2,1)S(1)} %bitcast.39), channel_id=1, source_target_pairs={{0,3},{1,0},{2,1},{3,2},{4,7},{5,4},{6,5},{7,6},{8,11},{9,8},{10,9... | collective-permute-start | bytes 2457608 | tf_op jit(solution)/shard_map/ppermute | solution.py:359
  25.3 1.4 collective-permute-start.11
  27.2 7.8 %collective-permute-start.13 = (f32[8,128]{1,0:T(8,128)S(1)}, f32[8,128]{1,0:T(8,128)S(1)}, u32[]{:S(2)}, u32[]{:S(2)}) collective-permute-start(f32[8,128]{1,0:T(8,128)S(1)} %concatenate.28), channel_id=1, source_target_pairs={{0,16},{16,0},{32,48},{48,32},{1,17},{17,1},{33,49},{49,33},{2,18}... | collective-permute-start | bytes 12296 | tf_op jit(solution)/shard_map/ppermute | solution.py:415
  35.0 0.9 fusion.5
  35.9 0.3 collective-permute-done.13
  36.2 8.7 %collective-permute-start.14 = (f32[8,128]{1,0:T(8,128)S(1)}, f32[8,128]{1,0:T(8,128)S(1)}, u32[]{:S(2)}, u32[]{:S(2)}) collective-permute-start(f32[8,128]{1,0:T(8,128)S(1)} %pad_add_fusion.1), channel_id=1, source_target_pairs={{0,128},{128,0},{1,129},{129,1},{2,130},{130,2},{3,131},{131,3},{4... | collective-permute-start | bytes 12296 | tf_op jit(solution)/shard_map/ppermute | solution.py:416
  45.0 0.9 collective-permute-done.14
  45.9 1.9 %collective-permute-start.12 = (bf16[512,128]{1,0:T(8,128)(2,1)S(1)}, bf16[512,128]{1,0:T(8,128)(2,1)S(1)}, u32[]{:S(2)}, u32[]{:S(2)}) collective-permute-start(bf16[512,128]{1,0:T(8,128)(2,1)S(1)} %maximum_maximum_fusion), channel_id=1, source_target_pairs={{0,16},{16,0},{32,48},{48,32},{1,17},{17,1},{33,49},{49,33},{2,18}... | collective-permute-start | bytes 393224 | tf_op jit(solution)/shard_map/ppermute | solution.py:407
  47.7 2.8 %collective-permute-done.12 = bf16[512,128]{1,0:T(8,128)(2,1)S(1)} collective-permute-done((bf16[512,128]{1,0:T(8,128)(2,1)S(1)}, bf16[512,128]{1,0:T(8,128)(2,1)S(1)}, u32[]{:S(2)}, u32[]{:S(2)}) %collective-permute-start.12) | collective-permute-done | bytes 131104 | tf_op jit(solution)/shard_map/ppermute | solution.py:407
  50.5 3.2 %collective-permute-start.15 = (bf16[160,2560]{1,0:T(8,128)(2,1)S(1)}, bf16[160,2560]{1,0:T(8,128)(2,1)}, u32[]{:S(2)}, u32[]{:S(2)}) collective-permute-start(bf16[160,2560]{1,0:T(8,128)(2,1)S(1)} %bitcast.41), channel_id=1, source_target_pairs={{0,2},{1,3},{2,0},{3,1},{4,6},{5,7},{6,4},{7,5},{8,10},{9,11},{10,... | collective-permute-start | bytes 2457608 | tf_op jit(solution)/shard_map/ppermute | solution.py:359
  53.8 1.6 collective-permute-start.16
  55.5 8.1 %collective-permute-start.17 = (bf16[160,2560]{1,0:T(8,128)(2,1)S(1)}, bf16[160,2560]{1,0:T(8,128)(2,1)S(1)}, u32[]{:S(2)}, u32[]{:S(2)}) collective-permute-start(bf16[160,2560]{1,0:T(8,128)(2,1)S(1)} %bitcast.42), channel_id=1, source_target_pairs={{0,64},{64,0},{1,65},{65,1},{2,66},{66,2},{3,67},{67,3},{4,68},{68... | collective-permute-start | bytes 2457608 | tf_op jit(solution)/shard_map/ppermute | solution.py:383
  63.6 0.3 collective-permute-start.18
  63.9 0.2 collective-permute-start.20
  64.1 8.9 %collective-permute-start.21 = (bf16[160,2560]{1,0:T(8,128)(2,1)S(1)}, bf16[160,2560]{1,0:T(8,128)(2,1)}, u32[]{:S(2)}, u32[]{:S(2)}) collective-permute-start(bf16[160,2560]{1,0:T(8,128)(2,1)S(1)} %bitcast.37), channel_id=1, source_target_pairs={{0,64},{64,0},{1,65},{65,1},{2,66},{66,2},{3,67},{67,3},{4,68},{68... | collective-permute-start | bytes 2457608 | tf_op jit(solution)/shard_map/ppermute | solution.py:383
  73.0 3.2 %collective-permute-start.22 = (bf16[160,2560]{1,0:T(8,128)(2,1)}, bf16[160,2560]{1,0:T(8,128)(2,1)}, u32[]{:S(2)}, u32[]{:S(2)}) collective-permute-start(bf16[160,2560]{1,0:T(8,128)(2,1)} %collective-permute-done.9.refs_5_), channel_id=1, source_target_pairs={{0,64},{64,0},{1,65},{65,1},{2,66},{66,2},{3,67},{67,3},{4,68},{68... | collective-permute-start | bytes 2457608 | tf_op jit(solution)/shard_map/ppermute | solution.py:383
  76.2 0.9 copy-done.1
  77.2 0.9 copy-done.3
  78.1 0.5 collective-permute-start.19
  78.6 0.9 copy-done.5
  80.0 1.0 collective-permute-done.19.refs_10_
  81.0 1.2 collective-permute-done.23.refs_14_
  82.2 1.1 copy-done.2
  83.3 1.1 copy-done.4
  84.5 1.1 copy-done.6
  85.6 4.4 %shard_map.82 = (bf16[256,128]{1,0:T(8,128)(2,1)S(1)}, bf16[2560,2560]{1,0:T(8,128)(2,1)S(1)}, bf16[2560,64]{1,0:T(8,128)(2,1)S(1)}, bf16[2432,64]{1,0:T(8,128)(2,1)S(1)}, bf16[2432,64]{1,0:T(8,128)(2,1)S(1)}) custom-call(s32[4]{0:T(128)S(1)} %pad_add_fusion.where_ref, bf16[256,128]{1,0:T(8,128)(2,1)S(1)} %get-tuple-element.140.rows_ref, ...), custom_call_target="tpu_custom_call" | custom-call | tf_op jit(solution)/shard_map/pallas_call | solution.py:179
  90.0 0.7 collective-permute-start.25
  90.6 0.7 collective-permute-start.26
  91.3 1.3 collective-permute-start.27
  92.9 5.2 %shard_map.83 = (f32[2560,64]{1,0:T(8,128)S(1)}, f32[64,64]{1,0:T(8,128)S(1)}) custom-call(bf16[2560,2560]{1,0:T(8,128)(2,1)S(1)} %get-tuple-element.93.full.refs_2_, bf16[2432,64]{1,0:T(8,128)(2,1)S(1)} %get-tuple-element.94.en_ref.refs_4_, bf16[2432,64]{1,0:T(8,128)(2,1)S(1)} %get-tuple-element.95.fin_ref), custom_call_target="tpu_custom_call" | custom-call | tf_op jit(solution)/shard_map/pallas_call | solution.py:259
  98.1 12.3 %collective-permute-done.27 = bf16[256,128]{1,0:T(8,128)(2,1)S(1)} collective-permute-done((bf16[256,128]{1,0:T(8,128)(2,1)S(1)}, bf16[256,128]{1,0:T(8,128)(2,1)S(1)}, u32[]{:S(2)}, u32[]{:S(2)}) %collective-permute-start.27) | collective-permute-done | bytes 65568 | tf_op jit(solution)/shard_map/ppermute | solution.py:434
  110.4 13.3 %shard_map.84 = (bf16[256,128]{1,0:T(8,128)(2,1)S(1)}, f32[256,128]{1,0:T(8,128)S(1)}, f32[16,128]{1,0:T(8,128)S(1)}, f32[512,64]{1,0:T(8,128)S(1)}, f32[512,128...) custom-call(bf16[256,128]{1,0:T(8,128)(2,1)S(1)} %select_select_fusion.sample_ref, ...), custom_call_target="tpu_custom_call" | custom-call | tf_op jit(solution)/shard_map/pallas_call | solution.py:229
  123.8 1.0 collective-permute-start.28
  124.7 1.6 collective-permute-start.29
  126.3 1.0 collective-permute-start.30
  127.4 4.3 %shard_map.85 = (f32[512,64]{1,0:T(8,128)S(1)}, bf16[512,768]{1,0:T(8,128)(2,1)S(1)}) custom-call(bf16[256,128]{1,0:T(8,128)(2,1)S(1)} %get-tuple-element.120.refs_0_, bf16[512,2432]{1,0:T(8,128)(2,1)S(1)} %get-tuple-element.107.refs_1_, bf16[2560,2560]{1,0:T(8,128)(2,1)S(1)} %get-tuple-element.93.full.refs_2_, ...), custom_call_target="tpu_custom_call" | custom-call | tf_op jit(solution)/shard_map/pallas_call | solution.py:289
  131.8 2.9 %collective-permute-start.32 = (f32[16,128]{1,0:T(8,128)S(1)}, f32[16,128]{1,0:T(8,128)S(1)}, u32[]{:S(2)}, u32[]{:S(2)}) collective-permute-start(f32[16,128]{1,0:T(8,128)S(1)} %add_add_fusion.3), channel_id=1, source_target_pairs={{0,8},{4,12},{8,0},{12,4},{1,9},{5,13},{9,1},{13,5},{2,10},{6,14},... | collective-permute-start | bytes 24584 | tf_op jit(solution)/shard_map/ppermute | solution.py:454
  134.8 0.8 collective-permute-start.33
  135.6 4.8 %shard_map.86 = (f32[512,64]{1,0:T(8,128)S(1)}, bf16[512,1024]{1,0:T(8,128)(2,1)S(1)}) custom-call(bf16[256,128]{1,0:T(8,128)(2,1)S(1)} %get-tuple-element.120.refs_0_, bf16[512,2432]{1,0:T(8,128)(2,1)S(1)} %get-tuple-element.107.refs_1_, bf16[2560,2560]{1,0:T(8,128)(2,1)S(1)} %get-tuple-element.93.full.refs_2_, ...), custom_call_target="tpu_custom_call" | custom-call | tf_op jit(solution)/shard_map/pallas_call | solution.py:289
  140.5 2.3 %collective-permute-start.35 = (f32[16,128]{1,0:T(8,128)S(1)}, f32[16,128]{1,0:T(8,128)S(1)}, u32[]{:S(2)}, u32[]{:S(2)}) collective-permute-start(f32[16,128]{1,0:T(8,128)S(1)} %add_add_fusion.2), channel_id=1, source_target_pairs={{0,2},{1,3},{2,0},{3,1},{4,6},{5,7},{6,4},{7,5},{8,10},{9,11},{10,... | collective-permute-start | bytes 24584 | tf_op jit(solution)/shard_map/ppermute | solution.py:454
  142.8 0.6 collective-permute-start.36
  143.3 3.6 %shard_map.87 = (f32[512,64]{1,0:T(8,128)S(1)}, bf16[512,768]{1,0:T(8,128)(2,1)S(1)}) custom-call(bf16[256,128]{1,0:T(8,128)(2,1)S(1)} %get-tuple-element.120.refs_0_, bf16[512,2432]{1,0:T(8,128)(2,1)S(1)} %get-tuple-element.107.refs_1_, bf16[2560,2560]{1,0:T(8,128)(2,1)S(1)} %get-tuple-element.93.full.refs_2_, ...), custom_call_target="tpu_custom_call" | custom-call | tf_op jit(solution)/shard_map/pallas_call | solution.py:289
  147.0 4.1 %collective-permute-start.37 = (f32[8,128]{1,0:T(8,128)S(1)}, f32[8,128]{1,0:T(8,128)S(1)}, u32[]{:S(2)}, u32[]{:S(2)}) collective-permute-start(f32[8,128]{1,0:T(8,128)S(1)} %slice.84), channel_id=1, source_target_pairs={{16,144},{48,176},{17,145},{49,177},{18,146},{50,178},{19,147},{51... | collective-permute-start | bytes 12296 | tf_op jit(solution)/shard_map/ppermute | solution.py:459
  151.1 0.7 collective-permute-start.38
  151.7 1.9 %collective-permute-start.39 = (f32[256,128]{1,0:T(8,128)S(1)}, f32[256,128]{1,0:T(8,128)S(1)}, u32[]{:S(2)}, u32[]{:S(2)}) collective-permute-start(f32[256,128]{1,0:T(8,128)S(1)} %get-tuple-element.126), channel_id=1, source_target_pairs={{16,144},{48,176},{17,145},{49,177},{18,146},{50,178},{19,147},{51... | collective-permute-start | bytes 393224 | tf_op jit(solution)/shard_map/ppermute | solution.py:446
  153.7 3.9 %shard_map.88 = f32[256,128]{1,0:T(8,128)S(1)} custom-call(f32[16,128]{1,0:T(8,128)S(1)} %add_add_fusion.1.sums_ref, bf16[2560,64]{1,0:T(8,128)(2,1)S(1)} %get-tuple-element.102.close_ref.refs_3_, f32[2560,64]{1,0:T(8,128)S(1)} %get-tuple-element.127.pf_ref, f32[64,64]{1,0:T(8,128)S(1)} %get-tuple-element.128.ef_ref, ...), custom_call_target="tpu_custom_call" | custom-call | tf_op jit(solution)/shard_map/pallas_call | solution.py:339
  158.6 0.7 collective-permute-start.40
  159.3 1.3 collective-permute-start.41
  160.6 0.7 collective-permute-start.42
  161.3 0.7 collective-permute-start.43
  162.0 13.7 %collective-permute-done.41 = f32[256,128]{1,0:T(8,128)S(1)} collective-permute-done((f32[256,128]{1,0:T(8,128)S(1)}, f32[256,128]{1,0:T(8,128)S(1)}, u32[]{:S(2)}, u32[]{:S(2)}) %collective-permute-start.41) | collective-permute-done | bytes 131104 | tf_op jit(solution)/shard_map/ppermute | solution.py:473
  175.8 0.7 pad_maximum_fusion
  (105 shorter events, 3.3 us)
Async XLA Ops:
  0.0 27.0 %copy-start = (bf16[193,64]{0,1:T(8,128)(2,1)S(1)}, bf16[193,64]{0,1:T(8,128)(2,1)}, u32[]{:S(2)}) copy-start(bf16[193,64]{0,1:T(8,128)(2,1)} %param.15) | copy-start | bytes 74116
  1.1 0.7 collective-permute-start
  1.8 8.0 %collective-permute-start.1 = (bf16[40,2560]{1,0:T(8,128)(2,1)S(1)}, bf16[40,2560]{1,0:T(8,128)(2,1)S(1)}, u32[]{:S(2)}, u32[]{:S(2)}) collective-permute-start(bf16[40,2560]{1,0:T(8,128)(2,1)S(1)} %broadcast_select_fusion), channel_id=1, source_target_pairs={{0,32},{32,0},{16,48},{48,16},{1,33},{33,1},{17,49},{49,17},{2,34}... | collective-permute-start | bytes 614408 | tf_op jit(solution)/shard_map/ppermute | solution.py:373
  9.8 7.9 %collective-permute-start.2 = (bf16[40,2560]{1,0:T(8,128)(2,1)S(1)}, bf16[40,2560]{1,0:T(8,128)(2,1)S(1)}, u32[]{:S(2)}, u32[]{:S(2)}) collective-permute-start(bf16[40,2560]{1,0:T(8,128)(2,1)S(1)} %get-tuple-element.72), channel_id=1, source_target_pairs={{0,4},{4,8},{8,12},{12,0},{1,5},{5,9},{9,13},{13,1},{2,6},{6,10},{... | collective-permute-start | bytes 614408 | tf_op jit(solution)/shard_map/ppermute | solution.py:359
  11.1 7.7 %collective-permute-start.3 = (bf16[40,2560]{1,0:T(8,128)(2,1)S(1)}, bf16[40,2560]{1,0:T(8,128)(2,1)S(1)}, u32[]{:S(2)}, u32[]{:S(2)}) collective-permute-start(bf16[40,2560]{1,0:T(8,128)(2,1)S(1)} %get-tuple-element.72), channel_id=1, source_target_pairs={{0,8},{4,12},{8,0},{12,4},{1,9},{5,13},{9,1},{13,5},{2,10},{6,14},... | collective-permute-start | bytes 614408 | tf_op jit(solution)/shard_map/ppermute | solution.py:359
  12.0 6.9 %collective-permute-start.4 = (bf16[40,2560]{1,0:T(8,128)(2,1)S(1)}, bf16[40,2560]{1,0:T(8,128)(2,1)S(1)}, u32[]{:S(2)}, u32[]{:S(2)}) collective-permute-start(bf16[40,2560]{1,0:T(8,128)(2,1)S(1)} %get-tuple-element.72), channel_id=1, source_target_pairs={{0,12},{4,0},{8,4},{12,8},{1,13},{5,1},{9,5},{13,9},{2,14},{6,2},{... | collective-permute-start | bytes 614408 | tf_op jit(solution)/shard_map/ppermute | solution.py:359
  13.8 5.9 %collective-permute-start.5 = (bf16[40,2560]{1,0:T(8,128)(2,1)S(1)}, bf16[40,2560]{1,0:T(8,128)(2,1)S(1)}, u32[]{:S(2)}, u32[]{:S(2)}) collective-permute-start(bf16[40,2560]{1,0:T(8,128)(2,1)S(1)} %get-tuple-element.76), channel_id=1, source_target_pairs={{0,1},{1,2},{2,3},{3,0},{4,5},{5,6},{6,7},{7,4},{8,9},{9,10},{10,1... | collective-permute-start | bytes 614408 | tf_op jit(solution)/shard_map/ppermute | solution.py:359
  15.1 8.0 %collective-permute-start.6 = (bf16[40,2560]{1,0:T(8,128)(2,1)S(1)}, bf16[40,2560]{1,0:T(8,128)(2,1)S(1)}, u32[]{:S(2)}, u32[]{:S(2)}) collective-permute-start(bf16[40,2560]{1,0:T(8,128)(2,1)S(1)} %get-tuple-element.76), channel_id=1, source_target_pairs={{0,2},{1,3},{2,0},{3,1},{4,6},{5,7},{6,4},{7,5},{8,10},{9,11},{10,... | collective-permute-start | bytes 614408 | tf_op jit(solution)/shard_map/ppermute | solution.py:359
  17.8 5.3 %collective-permute-start.7 = (bf16[40,2560]{1,0:T(8,128)(2,1)S(1)}, bf16[40,2560]{1,0:T(8,128)(2,1)S(1)}, u32[]{:S(2)}, u32[]{:S(2)}) collective-permute-start(bf16[40,2560]{1,0:T(8,128)(2,1)S(1)} %get-tuple-element.76), channel_id=1, source_target_pairs={{0,3},{1,0},{2,1},{3,2},{4,7},{5,4},{6,5},{7,6},{8,11},{9,8},{10,9... | collective-permute-start | bytes 614408 | tf_op jit(solution)/shard_map/ppermute | solution.py:359
  18.8 8.0 %copy-start.8 = (s32[8,77]{1,0:T(8,128)S(1)}, s32[8,77]{1,0:T(8,128)}, u32[]{:S(2)}) copy-start(s32[8,77]{1,0:T(8,128)} %param.11) | copy-start | bytes 7396
  18.8 16.1 %copy-start.7 = (bf16[8,64,64]{2,1,0:T(8,128)(2,1)S(1)}, bf16[8,64,64]{2,1,0:T(8,128)(2,1)}, u32[]{:S(2)}) copy-start(bf16[8,64,64]{2,1,0:T(8,128)(2,1)} %param.8) | copy-start | bytes 196612
  23.2 56.3 %copy-start.9 = (s32[8]{0:T(128)S(1)}, s32[8]{0:T(128)}, u32[]{:S(2)}) copy-start(s32[8]{0:T(128)} %param.10) | copy-start | bytes 100
  23.4 30.4 %collective-permute-start.10 = (bf16[160,2560]{1,0:T(8,128)(2,1)S(1)}, bf16[160,2560]{1,0:T(8,128)(2,1)S(1)}, u32[]{:S(2)}, u32[]{:S(2)}) collective-permute-start(bf16[160,2560]{1,0:T(8,128)(2,1)S(1)} %bitcast.39), channel_id=1, source_target_pairs={{0,3},{1,0},{2,1},{3,2},{4,7},{5,4},{6,5},{7,6},{8,11},{9,8},{10,9... | collective-permute-start | bytes 2457608 | tf_op jit(solution)/shard_map/ppermute | solution.py:359
  25.3 30.2 %collective-permute-start.8 = (bf16[160,2560]{1,0:T(8,128)(2,1)S(1)}, bf16[160,2560]{1,0:T(8,128)(2,1)S(1)}, u32[]{:S(2)}, u32[]{:S(2)}) collective-permute-start(bf16[160,2560]{1,0:T(8,128)(2,1)S(1)} %bitcast.40), channel_id=1, source_target_pairs={{0,1},{1,2},{2,3},{3,0},{4,5},{5,6},{6,7},{7,4},{8,9},{9,10},{10,1... | collective-permute-start | bytes 2457608 | tf_op jit(solution)/shard_map/ppermute | solution.py:359
  25.3 30.2 %collective-permute-start.11 = (bf16[160,2560]{1,0:T(8,128)(2,1)S(1)}, bf16[160,2560]{1,0:T(8,128)(2,1)}, u32[]{:S(2)}, u32[]{:S(2)}) collective-permute-start(bf16[160,2560]{1,0:T(8,128)(2,1)S(1)} %bitcast.34), channel_id=1, source_target_pairs={{0,12},{4,0},{8,4},{12,8},{1,13},{5,1},{9,5},{13,9},{2,14},{6,2},{... | collective-permute-start | bytes 2457608 | tf_op jit(solution)/shard_map/ppermute | solution.py:359
  26.8 28.7 %collective-permute-start.9 = (bf16[160,2560]{1,0:T(8,128)(2,1)S(1)}, bf16[160,2560]{1,0:T(8,128)(2,1)}, u32[]{:S(2)}, u32[]{:S(2)}) collective-permute-start(bf16[160,2560]{1,0:T(8,128)(2,1)S(1)} %bitcast.35), channel_id=1, source_target_pairs={{0,4},{4,8},{8,12},{12,0},{1,5},{5,9},{9,13},{13,1},{2,6},{6,10},{... | collective-permute-start | bytes 2457608 | tf_op jit(solution)/shard_map/ppermute | solution.py:359
  27.2 9.0 %collective-permute-start.13 = (f32[8,128]{1,0:T(8,128)S(1)}, f32[8,128]{1,0:T(8,128)S(1)}, u32[]{:S(2)}, u32[]{:S(2)}) collective-permute-start(f32[8,128]{1,0:T(8,128)S(1)} %concatenate.28), channel_id=1, source_target_pairs={{0,16},{16,0},{32,48},{48,32},{1,17},{17,1},{33,49},{49,33},{2,18}... | collective-permute-start | bytes 12296 | tf_op jit(solution)/shard_map/ppermute | solution.py:415
  36.2 9.7 %collective-permute-start.14 = (f32[8,128]{1,0:T(8,128)S(1)}, f32[8,128]{1,0:T(8,128)S(1)}, u32[]{:S(2)}, u32[]{:S(2)}) collective-permute-start(f32[8,128]{1,0:T(8,128)S(1)} %pad_add_fusion.1), channel_id=1, source_target_pairs={{0,128},{128,0},{1,129},{129,1},{2,130},{130,2},{3,131},{131,3},{4... | collective-permute-start | bytes 12296 | tf_op jit(solution)/shard_map/ppermute | solution.py:416
  45.9 4.6 %collective-permute-start.12 = (bf16[512,128]{1,0:T(8,128)(2,1)S(1)}, bf16[512,128]{1,0:T(8,128)(2,1)S(1)}, u32[]{:S(2)}, u32[]{:S(2)}) collective-permute-start(bf16[512,128]{1,0:T(8,128)(2,1)S(1)} %maximum_maximum_fusion), channel_id=1, source_target_pairs={{0,16},{16,0},{32,48},{48,32},{1,17},{17,1},{33,49},{49,33},{2,18}... | collective-permute-start | bytes 393224 | tf_op jit(solution)/shard_map/ppermute | solution.py:407
  50.5 13.6 %collective-permute-start.15 = (bf16[160,2560]{1,0:T(8,128)(2,1)S(1)}, bf16[160,2560]{1,0:T(8,128)(2,1)}, u32[]{:S(2)}, u32[]{:S(2)}) collective-permute-start(bf16[160,2560]{1,0:T(8,128)(2,1)S(1)} %bitcast.41), channel_id=1, source_target_pairs={{0,2},{1,3},{2,0},{3,1},{4,6},{5,7},{6,4},{7,5},{8,10},{9,11},{10,... | collective-permute-start | bytes 2457608 | tf_op jit(solution)/shard_map/ppermute | solution.py:359
  53.8 19.2 %collective-permute-start.16 = (bf16[160,2560]{1,0:T(8,128)(2,1)S(1)}, bf16[160,2560]{1,0:T(8,128)(2,1)}, u32[]{:S(2)}, u32[]{:S(2)}) collective-permute-start(bf16[160,2560]{1,0:T(8,128)(2,1)S(1)} %bitcast.36), channel_id=1, source_target_pairs={{0,8},{4,12},{8,0},{12,4},{1,9},{5,13},{9,1},{13,5},{2,10},{6,14},... | collective-permute-start | bytes 2457608 | tf_op jit(solution)/shard_map/ppermute | solution.py:359
  55.5 20.7 %collective-permute-start.17 = (bf16[160,2560]{1,0:T(8,128)(2,1)S(1)}, bf16[160,2560]{1,0:T(8,128)(2,1)S(1)}, u32[]{:S(2)}, u32[]{:S(2)}) collective-permute-start(bf16[160,2560]{1,0:T(8,128)(2,1)S(1)} %bitcast.42), channel_id=1, source_target_pairs={{0,64},{64,0},{1,65},{65,1},{2,66},{66,2},{3,67},{67,3},{4,68},{68... | collective-permute-start | bytes 2457608 | tf_op jit(solution)/shard_map/ppermute | solution.py:383
  63.6 13.6 %collective-permute-start.18 = (bf16[160,2560]{1,0:T(8,128)(2,1)S(1)}, bf16[160,2560]{1,0:T(8,128)(2,1)S(1)}, u32[]{:S(2)}, u32[]{:S(2)}) collective-permute-start(bf16[160,2560]{1,0:T(8,128)(2,1)S(1)} %collective-permute-done.8.refs_1_), channel_id=1, source_target_pairs={{0,64},{64,0},{1,65},{65,1},{2,66},{66,2},{3,67},{67,3},{4,68},{68... | collective-permute-start | bytes 2457608 | tf_op jit(solution)/shard_map/ppermute | solution.py:383
  63.9 14.7 %collective-permute-start.20 = (bf16[160,2560]{1,0:T(8,128)(2,1)S(1)}, bf16[160,2560]{1,0:T(8,128)(2,1)S(1)}, u32[]{:S(2)}, u32[]{:S(2)}) collective-permute-start(bf16[160,2560]{1,0:T(8,128)(2,1)S(1)} %collective-permute-done.10.refs_3_), channel_id=1, source_target_pairs={{0,64},{64,0},{1,65},{65,1},{2,66},{66,2},{3,67},{67,3},{4,68},{68... | collective-permute-start | bytes 2457608 | tf_op jit(solution)/shard_map/ppermute | solution.py:383
  64.1 15.9 %collective-permute-start.21 = (bf16[160,2560]{1,0:T(8,128)(2,1)S(1)}, bf16[160,2560]{1,0:T(8,128)(2,1)}, u32[]{:S(2)}, u32[]{:S(2)}) collective-permute-start(bf16[160,2560]{1,0:T(8,128)(2,1)S(1)} %bitcast.37), channel_id=1, source_target_pairs={{0,64},{64,0},{1,65},{65,1},{2,66},{66,2},{3,67},{67,3},{4,68},{68... | collective-permute-start | bytes 2457608 | tf_op jit(solution)/shard_map/ppermute | solution.py:383
  73.0 7.0 %collective-permute-start.22 = (bf16[160,2560]{1,0:T(8,128)(2,1)}, bf16[160,2560]{1,0:T(8,128)(2,1)}, u32[]{:S(2)}, u32[]{:S(2)}) collective-permute-start(bf16[160,2560]{1,0:T(8,128)(2,1)} %collective-permute-done.9.refs_5_), channel_id=1, source_target_pairs={{0,64},{64,0},{1,65},{65,1},{2,66},{66,2},{3,67},{67,3},{4,68},{68... | collective-permute-start | bytes 2457608 | tf_op jit(solution)/shard_map/ppermute | solution.py:383
  76.2 0.9 copy-start.1
  77.1 2.9 %collective-permute-start.24 = (bf16[160,2560]{1,0:T(8,128)(2,1)}, bf16[160,2560]{1,0:T(8,128)(2,1)}, u32[]{:S(2)}, u32[]{:S(2)}) collective-permute-start(bf16[160,2560]{1,0:T(8,128)(2,1)} %collective-permute-done.11.refs_7_), channel_id=1, source_target_pairs={{0,64},{64,0},{1,65},{65,1},{2,66},{66,2},{3,67},{67,3},{4,68},{68... | collective-permute-start | bytes 2457608 | tf_op jit(solution)/shard_map/ppermute | solution.py:383
  77.2 0.9 copy-start.3
  78.1 2.9 %collective-permute-start.19 = (bf16[160,2560]{1,0:T(8,128)(2,1)}, bf16[160,2560]{1,0:T(8,128)(2,1)}, u32[]{:S(2)}, u32[]{:S(2)}) collective-permute-start(bf16[160,2560]{1,0:T(8,128)(2,1)} %collective-permute-done.15.refs_2_), channel_id=1, source_target_pairs={{0,64},{64,0},{1,65},{65,1},{2,66},{66,2},{3,67},{67,3},{4,68},{68... | collective-permute-start | bytes 2457608 | tf_op jit(solution)/shard_map/ppermute | solution.py:386
  78.6 0.9 copy-start.5
  79.5 2.7 %collective-permute-start.23 = (bf16[160,2560]{1,0:T(8,128)(2,1)}, bf16[160,2560]{1,0:T(8,128)(2,1)}, u32[]{:S(2)}, u32[]{:S(2)}) collective-permute-start(bf16[160,2560]{1,0:T(8,128)(2,1)} %collective-permute-done.16.refs_6_), channel_id=1, source_target_pairs={{0,64},{64,0},{1,65},{65,1},{2,66},{66,2},{3,67},{67,3},{4,68},{68... | collective-permute-start | bytes 2457608 | tf_op jit(solution)/shard_map/ppermute | solution.py:386
  82.2 1.1 copy-start.2
  83.3 1.1 copy-start.4
  84.5 1.1 copy-start.6
  90.0 8.1 %collective-permute-start.25 = (bf16[256,128]{1,0:T(8,128)(2,1)S(1)}, bf16[256,128]{1,0:T(8,128)(2,1)S(1)}, u32[]{:S(2)}, u32[]{:S(2)}) collective-permute-start(bf16[256,128]{1,0:T(8,128)(2,1)S(1)} %get-tuple-element.97), channel_id=1, source_target_pairs={{0,144},{32,176},{1,145},{33,177},{2,146},{34,178},{3,147},{35,179... | collective-permute-start | bytes 196616 | tf_op jit(solution)/shard_map/ppermute | solution.py:432
  90.6 7.5 %collective-permute-start.26 = (bf16[256,128]{1,0:T(8,128)(2,1)S(1)}, bf16[256,128]{1,0:T(8,128)(2,1)S(1)}, u32[]{:S(2)}, u32[]{:S(2)}) collective-permute-start(bf16[256,128]{1,0:T(8,128)(2,1)S(1)} %get-tuple-element.97), channel_id=1, source_target_pairs={{0,128},{32,160},{1,129},{33,161},{2,130},{34,162},{3,131},{35,163... | collective-permute-start | bytes 196616 | tf_op jit(solution)/shard_map/ppermute | solution.py:433
  91.3 19.1 %collective-permute-start.27 = (bf16[256,128]{1,0:T(8,128)(2,1)S(1)}, bf16[256,128]{1,0:T(8,128)(2,1)S(1)}, u32[]{:S(2)}, u32[]{:S(2)}) collective-permute-start(bf16[256,128]{1,0:T(8,128)(2,1)S(1)} %get-tuple-element.97), channel_id=1, source_target_pairs={{0,16},{32,48},{1,17},{33,49},{2,18},{34,50},{3,19},{35,51},{4,20}... | collective-permute-start | bytes 196616 | tf_op jit(solution)/shard_map/ppermute | solution.py:434
  123.8 8.0 %collective-permute-start.28 = (f32[16,128]{1,0:T(8,128)S(1)}, f32[16,128]{1,0:T(8,128)S(1)}, u32[]{:S(2)}, u32[]{:S(2)}) collective-permute-start(f32[16,128]{1,0:T(8,128)S(1)} %get-tuple-element.105), channel_id=1, source_target_pairs={{0,64},{64,0},{1,65},{65,1},{2,66},{66,2},{3,67},{67,3},{4,68},{68... | collective-permute-start | bytes 24584 | tf_op jit(solution)/shard_map/ppermute | solution.py:454
  124.7 7.0 %collective-permute-start.29 = (f32[16,128]{1,0:T(8,128)S(1)}, f32[16,128]{1,0:T(8,128)S(1)}, u32[]{:S(2)}, u32[]{:S(2)}) collective-permute-start(f32[16,128]{1,0:T(8,128)S(1)} %get-tuple-element.105), channel_id=1, source_target_pairs={{0,32},{32,0},{16,48},{48,16},{1,33},{33,1},{17,49},{49,17},{2,34}... | collective-permute-start | bytes 24584 | tf_op jit(solution)/shard_map/ppermute | solution.py:454
  126.3 5.4 %collective-permute-start.30 = (f32[16,128]{1,0:T(8,128)S(1)}, f32[16,128]{1,0:T(8,128)S(1)}, u32[]{:S(2)}, u32[]{:S(2)}) collective-permute-start(f32[16,128]{1,0:T(8,128)S(1)} %get-tuple-element.105), channel_id=1, source_target_pairs={{0,96},{16,112},{32,64},{48,80},{64,32},{80,48},{96,0},{112,16},{1... | collective-permute-start | bytes 24584 | tf_op jit(solution)/shard_map/ppermute | solution.py:454
  131.8 8.6 %collective-permute-start.31 = (f32[16,128]{1,0:T(8,128)S(1)}, f32[16,128]{1,0:T(8,128)S(1)}, u32[]{:S(2)}, u32[]{:S(2)}) collective-permute-start(f32[16,128]{1,0:T(8,128)S(1)} %add_add_fusion.3), channel_id=1, source_target_pairs={{0,4},{4,8},{8,12},{12,0},{1,5},{5,9},{9,13},{13,1},{2,6},{6,10},{... | collective-permute-start | bytes 24584 | tf_op jit(solution)/shard_map/ppermute | solution.py:454
  131.8 8.5 %collective-permute-start.32 = (f32[16,128]{1,0:T(8,128)S(1)}, f32[16,128]{1,0:T(8,128)S(1)}, u32[]{:S(2)}, u32[]{:S(2)}) collective-permute-start(f32[16,128]{1,0:T(8,128)S(1)} %add_add_fusion.3), channel_id=1, source_target_pairs={{0,8},{4,12},{8,0},{12,4},{1,9},{5,13},{9,1},{13,5},{2,10},{6,14},... | collective-permute-start | bytes 24584 | tf_op jit(solution)/shard_map/ppermute | solution.py:454
  134.8 5.6 %collective-permute-start.33 = (f32[16,128]{1,0:T(8,128)S(1)}, f32[16,128]{1,0:T(8,128)S(1)}, u32[]{:S(2)}, u32[]{:S(2)}) collective-permute-start(f32[16,128]{1,0:T(8,128)S(1)} %add_add_fusion.3), channel_id=1, source_target_pairs={{0,12},{4,0},{8,4},{12,8},{1,13},{5,1},{9,5},{13,9},{2,14},{6,2},{... | collective-permute-start | bytes 24584 | tf_op jit(solution)/shard_map/ppermute | solution.py:454
  140.4 6.6 %collective-permute-start.34 = (f32[16,128]{1,0:T(8,128)S(1)}, f32[16,128]{1,0:T(8,128)S(1)}, u32[]{:S(2)}, u32[]{:S(2)}) collective-permute-start(f32[16,128]{1,0:T(8,128)S(1)} %add_add_fusion.2), channel_id=1, source_target_pairs={{0,1},{1,2},{2,3},{3,0},{4,5},{5,6},{6,7},{7,4},{8,9},{9,10},{10,1... | collective-permute-start | bytes 24584 | tf_op jit(solution)/shard_map/ppermute | solution.py:454
  140.5 6.5 %collective-permute-start.35 = (f32[16,128]{1,0:T(8,128)S(1)}, f32[16,128]{1,0:T(8,128)S(1)}, u32[]{:S(2)}, u32[]{:S(2)}) collective-permute-start(f32[16,128]{1,0:T(8,128)S(1)} %add_add_fusion.2), channel_id=1, source_target_pairs={{0,2},{1,3},{2,0},{3,1},{4,6},{5,7},{6,4},{7,5},{8,10},{9,11},{10,... | collective-permute-start | bytes 24584 | tf_op jit(solution)/shard_map/ppermute | solution.py:454
  142.8 4.2 %collective-permute-start.36 = (f32[16,128]{1,0:T(8,128)S(1)}, f32[16,128]{1,0:T(8,128)S(1)}, u32[]{:S(2)}, u32[]{:S(2)}) collective-permute-start(f32[16,128]{1,0:T(8,128)S(1)} %add_add_fusion.2), channel_id=1, source_target_pairs={{0,3},{1,0},{2,1},{3,2},{4,7},{5,4},{6,5},{7,6},{8,11},{9,8},{10,9... | collective-permute-start | bytes 24584 | tf_op jit(solution)/shard_map/ppermute | solution.py:454
  147.0 10.6 %collective-permute-start.37 = (f32[8,128]{1,0:T(8,128)S(1)}, f32[8,128]{1,0:T(8,128)S(1)}, u32[]{:S(2)}, u32[]{:S(2)}) collective-permute-start(f32[8,128]{1,0:T(8,128)S(1)} %slice.84), channel_id=1, source_target_pairs={{16,144},{48,176},{17,145},{49,177},{18,146},{50,178},{19,147},{51... | collective-permute-start | bytes 12296 | tf_op jit(solution)/shard_map/ppermute | solution.py:459
  151.1 7.1 %collective-permute-start.38 = (f32[256,128]{1,0:T(8,128)S(1)}, f32[256,128]{1,0:T(8,128)S(1)}, u32[]{:S(2)}, u32[]{:S(2)}) collective-permute-start(f32[256,128]{1,0:T(8,128)S(1)} %get-tuple-element.126), channel_id=1, source_target_pairs={{128,144},{160,176},{129,145},{161,177},{130,146},{162,178},{131,1... | collective-permute-start | bytes 393224 | tf_op jit(solution)/shard_map/ppermute | solution.py:447
  151.7 6.6 %collective-permute-start.39 = (f32[256,128]{1,0:T(8,128)S(1)}, f32[256,128]{1,0:T(8,128)S(1)}, u32[]{:S(2)}, u32[]{:S(2)}) collective-permute-start(f32[256,128]{1,0:T(8,128)S(1)} %get-tuple-element.126), channel_id=1, source_target_pairs={{16,144},{48,176},{17,145},{49,177},{18,146},{50,178},{19,147},{51... | collective-permute-start | bytes 393224 | tf_op jit(solution)/shard_map/ppermute | solution.py:446
  158.6 3.3 %collective-permute-start.40 = (f32[256,128]{1,0:T(8,128)S(1)}, f32[256,128]{1,0:T(8,128)S(1)}, u32[]{:S(2)}, u32[]{:S(2)}) collective-permute-start(f32[256,128]{1,0:T(8,128)S(1)} %fusion), channel_id=1, source_target_pairs={{144,0},{176,32},{208,16},{240,48},{145,1},{177,33},{209,17},{241,... | collective-permute-start | bytes 393224 | tf_op jit(solution)/shard_map/ppermute | solution.py:473
  159.3 16.3 %collective-permute-start.41 = (f32[256,128]{1,0:T(8,128)S(1)}, f32[256,128]{1,0:T(8,128)S(1)}, u32[]{:S(2)}, u32[]{:S(2)}) collective-permute-start(f32[256,128]{1,0:T(8,128)S(1)} %fusion), channel_id=1, source_target_pairs={{144,64},{176,96},{208,80},{240,112},{145,65},{177,97},{209,81},{2... | collective-permute-start | bytes 393224 | tf_op jit(solution)/shard_map/ppermute | solution.py:473
  160.6 15.0 %collective-permute-start.42 = (f32[256,128]{1,0:T(8,128)S(1)}, f32[256,128]{1,0:T(8,128)S(1)}, u32[]{:S(2)}, u32[]{:S(2)}) collective-permute-start(f32[256,128]{1,0:T(8,128)S(1)} %fusion), channel_id=1, source_target_pairs={{144,128},{176,160},{208,144},{240,176},{145,129},{177,161},{209,1... | collective-permute-start | bytes 393224 | tf_op jit(solution)/shard_map/ppermute | solution.py:473
  161.3 14.4 %collective-permute-start.43 = (f32[256,128]{1,0:T(8,128)S(1)}, f32[256,128]{1,0:T(8,128)S(1)}, u32[]{:S(2)}, u32[]{:S(2)}) collective-permute-start(f32[256,128]{1,0:T(8,128)S(1)} %fusion), channel_id=1, source_target_pairs={{144,192},{176,224},{208,208},{240,240},{145,193},{177,225},{209,2... | collective-permute-start | bytes 393224 | tf_op jit(solution)/shard_map/ppermute | solution.py:473

commit v3 on v2

--- a/solution.py
+++ b/solution.py
@@ -404,7 +404,7 @@
             (anchor, noise_in, renoise, prompt_ids)
         )
         both = jnp.concatenate([packed_rows(first), packed_rows(second_in)], axis=0)
-        other = lax.ppermute(both, "z", Z1)
+        other = lax.ppermute(both, ("c", "z"), [(5, 4), (7, 6), (0, 1), (2, 3)])
         table_rows = text_table.shape[0]
         first_row = lax.axis_index(NET + FSDP) * table_rows
         offsets = ids - first_row

time: 177 us -> 179 us (1.011)
  starting transfers between devices: 83.4 us -> 85.8 us
    ppermute x1, starting transfers between devices: 1.86 us -> 3.76 us  [exchange(): other = lax.ppermute(both, ('c', 'z'), [(5, 4), (7, 6), (0, 1), (2, 3)])]
  transfers between devices with their start and end apart: 44 -> 44, of which waited for: 11 -> 10; matrix products, arithmetic and copies ran while one was open for 2% -> 2% of each run, Pallas kernels for 12% -> 12%
where the time goes in v3:
time: 179 us; the launch traced here: 178 us
  starting transfers between devices  85.8 us (48%)
  waiting for transfers between devices  40.6 us (23%)
  Pallas kernels  39.4 us (22%)
  local copies, waits for them, and re-layouts  9.79 us (5%)
    ppermute x6, starting transfers between devices, gather_weights(): swaps = {i: lax.ppermute(v, 'c', CORE) for i, v in zip(first, ready)}  21.1 us
    ppermute x12, starting transfers between devices, gather_axis(): lax.ppermute(piece, axis, shift(4, k))  17.4 us
    ppermute x4, waiting for transfers between devices, on_device(): landed = landed + lax.ppermute(result, NET + ('z',), pairs)  14 us
    pallas_call x1, Pallas kernels, second(): call(second_body, [((HALF, 128), bf16), ((HALF, 128), f32), ((16, 128), f...  13.3 us
    pallas_call x3, Pallas kernels, back_step(): call(lambda *refs: back_body(base, tiles, *refs), [((ROWS, CH), f32), ((R...  12.7 us
    ppermute x1, waiting for transfers between devices, on_device(): lax.ppermute(sample, ('h', 'z'), [(0, 1), (2, 3)])  12.2 us
    ppermute x9, starting transfers between devices, on_device(): moved = [lax.ppermute(sums, axis, pairs) for axis, pairs in sends]  10.5 us
    ppermute x1, starting transfers between devices, exchange(): text = text + lax.ppermute(text, 'h', CORE)  8.7 us
  transfers between devices with their start and end apart: 44, of which 10 were waited for; matrix products, arithmetic and copies ran while one was open for 2% of the time, Pallas kernels for 12%

profile of v3, /device:TPU:35, one launch (start us, length us, event | category | flops | bytes accessed | tf_op | source)
XLA Modules:
  0.0 178.0 jit_solution(12643574583613554452)
XLA Ops:
  0.0 1.0 concatenate.24
  1.1 0.7 collective-permute-start
  1.8 3.1 %collective-permute-start.1 = (bf16[40,2560]{1,0:T(8,128)(2,1)S(1)}, bf16[40,2560]{1,0:T(8,128)(2,1)S(1)}, u32[]{:S(2)}, u32[]{:S(2)}) collective-permute-start(bf16[40,2560]{1,0:T(8,128)(2,1)S(1)} %broadcast_select_fusion), channel_id=1, source_target_pairs={{0,32},{32,0},{16,48},{48,16},{1,33},{33,1},{17,49},{49,17},{2,34}... | collective-permute-start | bytes 614408 | tf_op jit(solution)/shard_map/ppermute | solution.py:373
  4.9 4.9 %collective-permute-done.1 = bf16[40,2560]{1,0:T(8,128)(2,1)S(1)} collective-permute-done((bf16[40,2560]{1,0:T(8,128)(2,1)S(1)}, bf16[40,2560]{1,0:T(8,128)(2,1)S(1)}, u32[]{:S(2)}, u32[]{:S(2)}) %collective-permute-start.1) | collective-permute-done | bytes 204832 | tf_op jit(solution)/shard_map/ppermute | solution.py:373
  9.8 1.3 collective-permute-start.2
  11.1 0.8 collective-permute-start.3
  12.0 1.9 %collective-permute-start.4 = (bf16[40,2560]{1,0:T(8,128)(2,1)S(1)}, bf16[40,2560]{1,0:T(8,128)(2,1)S(1)}, u32[]{:S(2)}, u32[]{:S(2)}) collective-permute-start(bf16[40,2560]{1,0:T(8,128)(2,1)S(1)} %get-tuple-element.72), channel_id=1, source_target_pairs={{0,12},{4,0},{8,4},{12,8},{1,13},{5,1},{9,5},{13,9},{2,14},{6,2},{... | collective-permute-start | bytes 614408 | tf_op jit(solution)/shard_map/ppermute | solution.py:359
  13.8 1.3 collective-permute-start.5
  15.1 2.6 %collective-permute-start.6 = (bf16[40,2560]{1,0:T(8,128)(2,1)S(1)}, bf16[40,2560]{1,0:T(8,128)(2,1)S(1)}, u32[]{:S(2)}, u32[]{:S(2)}) collective-permute-start(bf16[40,2560]{1,0:T(8,128)(2,1)S(1)} %get-tuple-element.76), channel_id=1, source_target_pairs={{0,2},{1,3},{2,0},{3,1},{4,6},{5,7},{6,4},{7,5},{8,10},{9,11},{10,... | collective-permute-start | bytes 614408 | tf_op jit(solution)/shard_map/ppermute | solution.py:359
  17.8 1.1 collective-permute-start.7
  18.8 0.9 collective-permute-done.5
  19.7 3.4 %collective-permute-done.6 = bf16[40,2560]{1,0:T(8,128)(2,1)S(1)} collective-permute-done((bf16[40,2560]{1,0:T(8,128)(2,1)S(1)}, bf16[40,2560]{1,0:T(8,128)(2,1)S(1)}, u32[]{:S(2)}, u32[]{:S(2)}) %collective-permute-start.6) | collective-permute-done | bytes 204832 | tf_op jit(solution)/shard_map/ppermute | solution.py:359
  23.4 1.9 %collective-permute-start.10 = (bf16[160,2560]{1,0:T(8,128)(2,1)S(1)}, bf16[160,2560]{1,0:T(8,128)(2,1)S(1)}, u32[]{:S(2)}, u32[]{:S(2)}) collective-permute-start(bf16[160,2560]{1,0:T(8,128)(2,1)S(1)} %bitcast.39), channel_id=1, source_target_pairs={{0,3},{1,0},{2,1},{3,2},{4,7},{5,4},{6,5},{7,6},{8,11},{9,8},{10,9... | collective-permute-start | bytes 2457608 | tf_op jit(solution)/shard_map/ppermute | solution.py:359
  25.3 1.4 collective-permute-start.11
  27.2 7.8 %collective-permute-start.13 = (f32[8,128]{1,0:T(8,128)S(1)}, f32[8,128]{1,0:T(8,128)S(1)}, u32[]{:S(2)}, u32[]{:S(2)}) collective-permute-start(f32[8,128]{1,0:T(8,128)S(1)} %concatenate.28), channel_id=1, source_target_pairs={{0,16},{16,0},{32,48},{48,32},{1,17},{17,1},{33,49},{49,33},{2,18}... | collective-permute-start | bytes 12296 | tf_op jit(solution)/shard_map/ppermute | solution.py:415
  35.0 0.9 fusion.5
  35.9 0.3 collective-permute-done.13
  36.2 8.7 %collective-permute-start.14 = (f32[8,128]{1,0:T(8,128)S(1)}, f32[8,128]{1,0:T(8,128)S(1)}, u32[]{:S(2)}, u32[]{:S(2)}) collective-permute-start(f32[8,128]{1,0:T(8,128)S(1)} %pad_add_fusion.1), channel_id=1, source_target_pairs={{0,128},{128,0},{1,129},{129,1},{2,130},{130,2},{3,131},{131,3},{4... | collective-permute-start | bytes 12296 | tf_op jit(solution)/shard_map/ppermute | solution.py:416
  45.0 0.9 collective-permute-done.14
  45.9 3.8 %collective-permute-start.12 = (bf16[512,128]{1,0:T(8,128)(2,1)S(1)}, bf16[512,128]{1,0:T(8,128)(2,1)S(1)}, u32[]{:S(2)}, u32[]{:S(2)}) collective-permute-start(bf16[512,128]{1,0:T(8,128)(2,1)S(1)} %maximum_maximum_fusion), channel_id=1, source_target_pairs={{80,64},{112,96},{0,16},{32,48},{81,65},{113,97},{1,17},{33,49},{8... | collective-permute-start | bytes 393224 | tf_op jit(solution)/shard_map/ppermute | solution.py:407
  49.7 1.9 %collective-permute-done.12 = bf16[512,128]{1,0:T(8,128)(2,1)S(1)} collective-permute-done((bf16[512,128]{1,0:T(8,128)(2,1)S(1)}, bf16[512,128]{1,0:T(8,128)(2,1)S(1)}, u32[]{:S(2)}, u32[]{:S(2)}) %collective-permute-start.12) | collective-permute-done | bytes 131104 | tf_op jit(solution)/shard_map/ppermute | solution.py:407
  51.6 3.2 %collective-permute-start.15 = (bf16[160,2560]{1,0:T(8,128)(2,1)S(1)}, bf16[160,2560]{1,0:T(8,128)(2,1)}, u32[]{:S(2)}, u32[]{:S(2)}) collective-permute-start(bf16[160,2560]{1,0:T(8,128)(2,1)S(1)} %bitcast.41), channel_id=1, source_target_pairs={{0,2},{1,3},{2,0},{3,1},{4,6},{5,7},{6,4},{7,5},{8,10},{9,11},{10,... | collective-permute-start | bytes 2457608 | tf_op jit(solution)/shard_map/ppermute | solution.py:359
  54.9 1.9 %collective-permute-start.16 = (bf16[160,2560]{1,0:T(8,128)(2,1)S(1)}, bf16[160,2560]{1,0:T(8,128)(2,1)}, u32[]{:S(2)}, u32[]{:S(2)}) collective-permute-start(bf16[160,2560]{1,0:T(8,128)(2,1)S(1)} %bitcast.36), channel_id=1, source_target_pairs={{0,8},{4,12},{8,0},{12,4},{1,9},{5,13},{9,1},{13,5},{2,10},{6,14},... | collective-permute-start | bytes 2457608 | tf_op jit(solution)/shard_map/ppermute | solution.py:359
  56.8 8.7 %collective-permute-start.17 = (bf16[160,2560]{1,0:T(8,128)(2,1)S(1)}, bf16[160,2560]{1,0:T(8,128)(2,1)S(1)}, u32[]{:S(2)}, u32[]{:S(2)}) collective-permute-start(bf16[160,2560]{1,0:T(8,128)(2,1)S(1)} %bitcast.42), channel_id=1, source_target_pairs={{0,64},{64,0},{1,65},{65,1},{2,66},{66,2},{3,67},{67,3},{4,68},{68... | collective-permute-start | bytes 2457608 | tf_op jit(solution)/shard_map/ppermute | solution.py:383
  65.5 0.3 collective-permute-start.18
  66.0 8.8 %collective-permute-start.21 = (bf16[160,2560]{1,0:T(8,128)(2,1)S(1)}, bf16[160,2560]{1,0:T(8,128)(2,1)}, u32[]{:S(2)}, u32[]{:S(2)}) collective-permute-start(bf16[160,2560]{1,0:T(8,128)(2,1)S(1)} %bitcast.37), channel_id=1, source_target_pairs={{0,64},{64,0},{1,65},{65,1},{2,66},{66,2},{3,67},{67,3},{4,68},{68... | collective-permute-start | bytes 2457608 | tf_op jit(solution)/shard_map/ppermute | solution.py:383
  74.7 3.1 %collective-permute-start.22 = (bf16[160,2560]{1,0:T(8,128)(2,1)}, bf16[160,2560]{1,0:T(8,128)(2,1)}, u32[]{:S(2)}, u32[]{:S(2)}) collective-permute-start(bf16[160,2560]{1,0:T(8,128)(2,1)} %collective-permute-done.9.refs_5_), channel_id=1, source_target_pairs={{0,64},{64,0},{1,65},{65,1},{2,66},{66,2},{3,67},{67,3},{4,68},{68... | collective-permute-start | bytes 2457608 | tf_op jit(solution)/shard_map/ppermute | solution.py:383
  77.9 0.9 copy-done.1
  78.8 0.9 copy-done.3
  79.7 0.5 collective-permute-start.19
  80.2 0.9 copy-done.5
  81.7 1.0 collective-permute-done.19.refs_10_
  82.6 1.2 collective-permute-done.23.refs_14_
  83.8 1.1 copy-done.2
  85.0 1.1 copy-done.4
  86.1 1.1 copy-done.6
  87.2 4.4 %shard_map.82 = (bf16[256,128]{1,0:T(8,128)(2,1)S(1)}, bf16[2560,2560]{1,0:T(8,128)(2,1)S(1)}, bf16[2560,64]{1,0:T(8,128)(2,1)S(1)}, bf16[2432,64]{1,0:T(8,128)(2,1)S(1)}, bf16[2432,64]{1,0:T(8,128)(2,1)S(1)}) custom-call(s32[4]{0:T(128)S(1)} %pad_add_fusion.where_ref, bf16[256,128]{1,0:T(8,128)(2,1)S(1)} %get-tuple-element.140.rows_ref, ...), custom_call_target="tpu_custom_call" | custom-call | tf_op jit(solution)/shard_map/pallas_call | solution.py:179
  91.6 0.7 collective-permute-start.25
  92.3 0.7 collective-permute-start.26
  93.0 1.3 collective-permute-start.27
  94.6 5.1 %shard_map.83 = (f32[2560,64]{1,0:T(8,128)S(1)}, f32[64,64]{1,0:T(8,128)S(1)}) custom-call(bf16[2560,2560]{1,0:T(8,128)(2,1)S(1)} %get-tuple-element.93.full.refs_2_, bf16[2432,64]{1,0:T(8,128)(2,1)S(1)} %get-tuple-element.94.en_ref.refs_4_, bf16[2432,64]{1,0:T(8,128)(2,1)S(1)} %get-tuple-element.95.fin_ref), custom_call_target="tpu_custom_call" | custom-call | tf_op jit(solution)/shard_map/pallas_call | solution.py:259
  99.7 12.2 %collective-permute-done.27 = bf16[256,128]{1,0:T(8,128)(2,1)S(1)} collective-permute-done((bf16[256,128]{1,0:T(8,128)(2,1)S(1)}, bf16[256,128]{1,0:T(8,128)(2,1)S(1)}, u32[]{:S(2)}, u32[]{:S(2)}) %collective-permute-start.27) | collective-permute-done | bytes 65568 | tf_op jit(solution)/shard_map/ppermute | solution.py:434
  111.9 13.3 %shard_map.84 = (bf16[256,128]{1,0:T(8,128)(2,1)S(1)}, f32[256,128]{1,0:T(8,128)S(1)}, f32[16,128]{1,0:T(8,128)S(1)}, f32[512,64]{1,0:T(8,128)S(1)}, f32[512,128...) custom-call(bf16[256,128]{1,0:T(8,128)(2,1)S(1)} %select_select_fusion.sample_ref, ...), custom_call_target="tpu_custom_call" | custom-call | tf_op jit(solution)/shard_map/pallas_call | solution.py:229
  125.2 1.0 collective-permute-start.28
  126.2 1.5 collective-permute-start.29
  127.7 1.1 collective-permute-start.30
  128.9 4.3 %shard_map.85 = (f32[512,64]{1,0:T(8,128)S(1)}, bf16[512,768]{1,0:T(8,128)(2,1)S(1)}) custom-call(bf16[256,128]{1,0:T(8,128)(2,1)S(1)} %get-tuple-element.120.refs_0_, bf16[512,2432]{1,0:T(8,128)(2,1)S(1)} %get-tuple-element.107.refs_1_, bf16[2560,2560]{1,0:T(8,128)(2,1)S(1)} %get-tuple-element.93.full.refs_2_, ...), custom_call_target="tpu_custom_call" | custom-call | tf_op jit(solution)/shard_map/pallas_call | solution.py:289
  133.2 0.3 collective-permute-start.31
  133.6 2.7 %collective-permute-start.32 = (f32[16,128]{1,0:T(8,128)S(1)}, f32[16,128]{1,0:T(8,128)S(1)}, u32[]{:S(2)}, u32[]{:S(2)}) collective-permute-start(f32[16,128]{1,0:T(8,128)S(1)} %add_add_fusion.3), channel_id=1, source_target_pairs={{0,8},{4,12},{8,0},{12,4},{1,9},{5,13},{9,1},{13,5},{2,10},{6,14},... | collective-permute-start | bytes 24584 | tf_op jit(solution)/shard_map/ppermute | solution.py:454
  136.2 0.9 collective-permute-start.33
  137.1 4.8 %shard_map.86 = (f32[512,64]{1,0:T(8,128)S(1)}, bf16[512,1024]{1,0:T(8,128)(2,1)S(1)}) custom-call(bf16[256,128]{1,0:T(8,128)(2,1)S(1)} %get-tuple-element.120.refs_0_, bf16[512,2432]{1,0:T(8,128)(2,1)S(1)} %get-tuple-element.107.refs_1_, bf16[2560,2560]{1,0:T(8,128)(2,1)S(1)} %get-tuple-element.93.full.refs_2_, ...), custom_call_target="tpu_custom_call" | custom-call | tf_op jit(solution)/shard_map/pallas_call | solution.py:289
  142.0 2.2 %collective-permute-start.35 = (f32[16,128]{1,0:T(8,128)S(1)}, f32[16,128]{1,0:T(8,128)S(1)}, u32[]{:S(2)}, u32[]{:S(2)}) collective-permute-start(f32[16,128]{1,0:T(8,128)S(1)} %add_add_fusion.2), channel_id=1, source_target_pairs={{0,2},{1,3},{2,0},{3,1},{4,6},{5,7},{6,4},{7,5},{8,10},{9,11},{10,... | collective-permute-start | bytes 24584 | tf_op jit(solution)/shard_map/ppermute | solution.py:454
  144.3 0.6 collective-permute-start.36
  144.9 3.6 %shard_map.87 = (f32[512,64]{1,0:T(8,128)S(1)}, bf16[512,768]{1,0:T(8,128)(2,1)S(1)}) custom-call(bf16[256,128]{1,0:T(8,128)(2,1)S(1)} %get-tuple-element.120.refs_0_, bf16[512,2432]{1,0:T(8,128)(2,1)S(1)} %get-tuple-element.107.refs_1_, bf16[2560,2560]{1,0:T(8,128)(2,1)S(1)} %get-tuple-element.93.full.refs_2_, ...), custom_call_target="tpu_custom_call" | custom-call | tf_op jit(solution)/shard_map/pallas_call | solution.py:289
  148.6 3.8 %collective-permute-start.37 = (f32[8,128]{1,0:T(8,128)S(1)}, f32[8,128]{1,0:T(8,128)S(1)}, u32[]{:S(2)}, u32[]{:S(2)}) collective-permute-start(f32[8,128]{1,0:T(8,128)S(1)} %slice.84), channel_id=1, source_target_pairs={{16,144},{48,176},{17,145},{49,177},{18,146},{50,178},{19,147},{51... | collective-permute-start | bytes 12296 | tf_op jit(solution)/shard_map/ppermute | solution.py:459
  152.4 0.7 collective-permute-start.38
  153.1 1.9 %collective-permute-start.39 = (f32[256,128]{1,0:T(8,128)S(1)}, f32[256,128]{1,0:T(8,128)S(1)}, u32[]{:S(2)}, u32[]{:S(2)}) collective-permute-start(f32[256,128]{1,0:T(8,128)S(1)} %get-tuple-element.126), channel_id=1, source_target_pairs={{16,144},{48,176},{17,145},{49,177},{18,146},{50,178},{19,147},{51... | collective-permute-start | bytes 393224 | tf_op jit(solution)/shard_map/ppermute | solution.py:446
  155.0 3.9 %shard_map.88 = f32[256,128]{1,0:T(8,128)S(1)} custom-call(f32[16,128]{1,0:T(8,128)S(1)} %add_add_fusion.1.sums_ref, bf16[2560,64]{1,0:T(8,128)(2,1)S(1)} %get-tuple-element.102.close_ref.refs_3_, f32[2560,64]{1,0:T(8,128)S(1)} %get-tuple-element.127.pf_ref, f32[64,64]{1,0:T(8,128)S(1)} %get-tuple-element.128.ef_ref, ...), custom_call_target="tpu_custom_call" | custom-call | tf_op jit(solution)/shard_map/pallas_call | solution.py:339
  159.8 0.7 collective-permute-start.40
  160.5 1.3 collective-permute-start.41
  161.8 0.7 collective-permute-start.42
  162.5 0.7 collective-permute-start.43
  163.2 14.0 %collective-permute-done.41 = f32[256,128]{1,0:T(8,128)S(1)} collective-permute-done((f32[256,128]{1,0:T(8,128)S(1)}, f32[256,128]{1,0:T(8,128)S(1)}, u32[]{:S(2)}, u32[]{:S(2)}) %collective-permute-start.41) | collective-permute-done | bytes 131104 | tf_op jit(solution)/shard_map/ppermute | solution.py:473
  177.3 0.7 pad_maximum_fusion
  (105 shorter events, 3.3 us)
Async XLA Ops:
  0.0 27.0 %copy-start = (bf16[193,64]{0,1:T(8,128)(2,1)S(1)}, bf16[193,64]{0,1:T(8,128)(2,1)}, u32[]{:S(2)}) copy-start(bf16[193,64]{0,1:T(8,128)(2,1)} %param.15) | copy-start | bytes 74116
  1.1 0.7 collective-permute-start
  1.8 8.0 %collective-permute-start.1 = (bf16[40,2560]{1,0:T(8,128)(2,1)S(1)}, bf16[40,2560]{1,0:T(8,128)(2,1)S(1)}, u32[]{:S(2)}, u32[]{:S(2)}) collective-permute-start(bf16[40,2560]{1,0:T(8,128)(2,1)S(1)} %broadcast_select_fusion), channel_id=1, source_target_pairs={{0,32},{32,0},{16,48},{48,16},{1,33},{33,1},{17,49},{49,17},{2,34}... | collective-permute-start | bytes 614408 | tf_op jit(solution)/shard_map/ppermute | solution.py:373
  9.8 7.9 %collective-permute-start.2 = (bf16[40,2560]{1,0:T(8,128)(2,1)S(1)}, bf16[40,2560]{1,0:T(8,128)(2,1)S(1)}, u32[]{:S(2)}, u32[]{:S(2)}) collective-permute-start(bf16[40,2560]{1,0:T(8,128)(2,1)S(1)} %get-tuple-element.72), channel_id=1, source_target_pairs={{0,4},{4,8},{8,12},{12,0},{1,5},{5,9},{9,13},{13,1},{2,6},{6,10},{... | collective-permute-start | bytes 614408 | tf_op jit(solution)/shard_map/ppermute | solution.py:359
  11.1 7.7 %collective-permute-start.3 = (bf16[40,2560]{1,0:T(8,128)(2,1)S(1)}, bf16[40,2560]{1,0:T(8,128)(2,1)S(1)}, u32[]{:S(2)}, u32[]{:S(2)}) collective-permute-start(bf16[40,2560]{1,0:T(8,128)(2,1)S(1)} %get-tuple-element.72), channel_id=1, source_target_pairs={{0,8},{4,12},{8,0},{12,4},{1,9},{5,13},{9,1},{13,5},{2,10},{6,14},... | collective-permute-start | bytes 614408 | tf_op jit(solution)/shard_map/ppermute | solution.py:359
  12.0 6.9 %collective-permute-start.4 = (bf16[40,2560]{1,0:T(8,128)(2,1)S(1)}, bf16[40,2560]{1,0:T(8,128)(2,1)S(1)}, u32[]{:S(2)}, u32[]{:S(2)}) collective-permute-start(bf16[40,2560]{1,0:T(8,128)(2,1)S(1)} %get-tuple-element.72), channel_id=1, source_target_pairs={{0,12},{4,0},{8,4},{12,8},{1,13},{5,1},{9,5},{13,9},{2,14},{6,2},{... | collective-permute-start | bytes 614408 | tf_op jit(solution)/shard_map/ppermute | solution.py:359
  13.8 5.9 %collective-permute-start.5 = (bf16[40,2560]{1,0:T(8,128)(2,1)S(1)}, bf16[40,2560]{1,0:T(8,128)(2,1)S(1)}, u32[]{:S(2)}, u32[]{:S(2)}) collective-permute-start(bf16[40,2560]{1,0:T(8,128)(2,1)S(1)} %get-tuple-element.76), channel_id=1, source_target_pairs={{0,1},{1,2},{2,3},{3,0},{4,5},{5,6},{6,7},{7,4},{8,9},{9,10},{10,1... | collective-permute-start | bytes 614408 | tf_op jit(solution)/shard_map/ppermute | solution.py:359
  15.1 8.0 %collective-permute-start.6 = (bf16[40,2560]{1,0:T(8,128)(2,1)S(1)}, bf16[40,2560]{1,0:T(8,128)(2,1)S(1)}, u32[]{:S(2)}, u32[]{:S(2)}) collective-permute-start(bf16[40,2560]{1,0:T(8,128)(2,1)S(1)} %get-tuple-element.76), channel_id=1, source_target_pairs={{0,2},{1,3},{2,0},{3,1},{4,6},{5,7},{6,4},{7,5},{8,10},{9,11},{10,... | collective-permute-start | bytes 614408 | tf_op jit(solution)/shard_map/ppermute | solution.py:359
  17.8 5.3 %collective-permute-start.7 = (bf16[40,2560]{1,0:T(8,128)(2,1)S(1)}, bf16[40,2560]{1,0:T(8,128)(2,1)S(1)}, u32[]{:S(2)}, u32[]{:S(2)}) collective-permute-start(bf16[40,2560]{1,0:T(8,128)(2,1)S(1)} %get-tuple-element.76), channel_id=1, source_target_pairs={{0,3},{1,0},{2,1},{3,2},{4,7},{5,4},{6,5},{7,6},{8,11},{9,8},{10,9... | collective-permute-start | bytes 614408 | tf_op jit(solution)/shard_map/ppermute | solution.py:359
  18.8 8.0 %copy-start.8 = (s32[8,77]{1,0:T(8,128)S(1)}, s32[8,77]{1,0:T(8,128)}, u32[]{:S(2)}) copy-start(s32[8,77]{1,0:T(8,128)} %param.11) | copy-start | bytes 7396
  18.8 16.1 %copy-start.7 = (bf16[8,64,64]{2,1,0:T(8,128)(2,1)S(1)}, bf16[8,64,64]{2,1,0:T(8,128)(2,1)}, u32[]{:S(2)}) copy-start(bf16[8,64,64]{2,1,0:T(8,128)(2,1)} %param.8) | copy-start | bytes 196612
  23.2 57.9 %copy-start.9 = (s32[8]{0:T(128)S(1)}, s32[8]{0:T(128)}, u32[]{:S(2)}) copy-start(s32[8]{0:T(128)} %param.10) | copy-start | bytes 100
  23.4 31.5 %collective-permute-start.10 = (bf16[160,2560]{1,0:T(8,128)(2,1)S(1)}, bf16[160,2560]{1,0:T(8,128)(2,1)S(1)}, u32[]{:S(2)}, u32[]{:S(2)}) collective-permute-start(bf16[160,2560]{1,0:T(8,128)(2,1)S(1)} %bitcast.39), channel_id=1, source_target_pairs={{0,3},{1,0},{2,1},{3,2},{4,7},{5,4},{6,5},{7,6},{8,11},{9,8},{10,9... | collective-permute-start | bytes 2457608 | tf_op jit(solution)/shard_map/ppermute | solution.py:359
  25.3 31.5 %collective-permute-start.8 = (bf16[160,2560]{1,0:T(8,128)(2,1)S(1)}, bf16[160,2560]{1,0:T(8,128)(2,1)S(1)}, u32[]{:S(2)}, u32[]{:S(2)}) collective-permute-start(bf16[160,2560]{1,0:T(8,128)(2,1)S(1)} %bitcast.40), channel_id=1, source_target_pairs={{0,1},{1,2},{2,3},{3,0},{4,5},{5,6},{6,7},{7,4},{8,9},{9,10},{10,1... | collective-permute-start | bytes 2457608 | tf_op jit(solution)/shard_map/ppermute | solution.py:359
  25.3 31.5 %collective-permute-start.11 = (bf16[160,2560]{1,0:T(8,128)(2,1)S(1)}, bf16[160,2560]{1,0:T(8,128)(2,1)}, u32[]{:S(2)}, u32[]{:S(2)}) collective-permute-start(bf16[160,2560]{1,0:T(8,128)(2,1)S(1)} %bitcast.34), channel_id=1, source_target_pairs={{0,12},{4,0},{8,4},{12,8},{1,13},{5,1},{9,5},{13,9},{2,14},{6,2},{... | collective-permute-start | bytes 2457608 | tf_op jit(solution)/shard_map/ppermute | solution.py:359
  26.8 30.0 %collective-permute-start.9 = (bf16[160,2560]{1,0:T(8,128)(2,1)S(1)}, bf16[160,2560]{1,0:T(8,128)(2,1)}, u32[]{:S(2)}, u32[]{:S(2)}) collective-permute-start(bf16[160,2560]{1,0:T(8,128)(2,1)S(1)} %bitcast.35), channel_id=1, source_target_pairs={{0,4},{4,8},{8,12},{12,0},{1,5},{5,9},{9,13},{13,1},{2,6},{6,10},{... | collective-permute-start | bytes 2457608 | tf_op jit(solution)/shard_map/ppermute | solution.py:359
  27.2 9.0 %collective-permute-start.13 = (f32[8,128]{1,0:T(8,128)S(1)}, f32[8,128]{1,0:T(8,128)S(1)}, u32[]{:S(2)}, u32[]{:S(2)}) collective-permute-start(f32[8,128]{1,0:T(8,128)S(1)} %concatenate.28), channel_id=1, source_target_pairs={{0,16},{16,0},{32,48},{48,32},{1,17},{17,1},{33,49},{49,33},{2,18}... | collective-permute-start | bytes 12296 | tf_op jit(solution)/shard_map/ppermute | solution.py:415
  36.2 9.7 %collective-permute-start.14 = (f32[8,128]{1,0:T(8,128)S(1)}, f32[8,128]{1,0:T(8,128)S(1)}, u32[]{:S(2)}, u32[]{:S(2)}) collective-permute-start(f32[8,128]{1,0:T(8,128)S(1)} %pad_add_fusion.1), channel_id=1, source_target_pairs={{0,128},{128,0},{1,129},{129,1},{2,130},{130,2},{3,131},{131,3},{4... | collective-permute-start | bytes 12296 | tf_op jit(solution)/shard_map/ppermute | solution.py:416
  45.9 5.7 %collective-permute-start.12 = (bf16[512,128]{1,0:T(8,128)(2,1)S(1)}, bf16[512,128]{1,0:T(8,128)(2,1)S(1)}, u32[]{:S(2)}, u32[]{:S(2)}) collective-permute-start(bf16[512,128]{1,0:T(8,128)(2,1)S(1)} %maximum_maximum_fusion), channel_id=1, source_target_pairs={{80,64},{112,96},{0,16},{32,48},{81,65},{113,97},{1,17},{33,49},{8... | collective-permute-start | bytes 393224 | tf_op jit(solution)/shard_map/ppermute | solution.py:407
  51.6 14.4 %collective-permute-start.15 = (bf16[160,2560]{1,0:T(8,128)(2,1)S(1)}, bf16[160,2560]{1,0:T(8,128)(2,1)}, u32[]{:S(2)}, u32[]{:S(2)}) collective-permute-start(bf16[160,2560]{1,0:T(8,128)(2,1)S(1)} %bitcast.41), channel_id=1, source_target_pairs={{0,2},{1,3},{2,0},{3,1},{4,6},{5,7},{6,4},{7,5},{8,10},{9,11},{10,... | collective-permute-start | bytes 2457608 | tf_op jit(solution)/shard_map/ppermute | solution.py:359
  54.9 19.8 %collective-permute-start.16 = (bf16[160,2560]{1,0:T(8,128)(2,1)S(1)}, bf16[160,2560]{1,0:T(8,128)(2,1)}, u32[]{:S(2)}, u32[]{:S(2)}) collective-permute-start(bf16[160,2560]{1,0:T(8,128)(2,1)S(1)} %bitcast.36), channel_id=1, source_target_pairs={{0,8},{4,12},{8,0},{12,4},{1,9},{5,13},{9,1},{13,5},{2,10},{6,14},... | collective-permute-start | bytes 2457608 | tf_op jit(solution)/shard_map/ppermute | solution.py:359
  56.8 21.1 %collective-permute-start.17 = (bf16[160,2560]{1,0:T(8,128)(2,1)S(1)}, bf16[160,2560]{1,0:T(8,128)(2,1)S(1)}, u32[]{:S(2)}, u32[]{:S(2)}) collective-permute-start(bf16[160,2560]{1,0:T(8,128)(2,1)S(1)} %bitcast.42), channel_id=1, source_target_pairs={{0,64},{64,0},{1,65},{65,1},{2,66},{66,2},{3,67},{67,3},{4,68},{68... | collective-permute-start | bytes 2457608 | tf_op jit(solution)/shard_map/ppermute | solution.py:383
  65.5 13.3 %collective-permute-start.18 = (bf16[160,2560]{1,0:T(8,128)(2,1)S(1)}, bf16[160,2560]{1,0:T(8,128)(2,1)S(1)}, u32[]{:S(2)}, u32[]{:S(2)}) collective-permute-start(bf16[160,2560]{1,0:T(8,128)(2,1)S(1)} %collective-permute-done.8.refs_1_), channel_id=1, source_target_pairs={{0,64},{64,0},{1,65},{65,1},{2,66},{66,2},{3,67},{67,3},{4,68},{68... | collective-permute-start | bytes 2457608 | tf_op jit(solution)/shard_map/ppermute | solution.py:383
  65.8 14.5 %collective-permute-start.20 = (bf16[160,2560]{1,0:T(8,128)(2,1)S(1)}, bf16[160,2560]{1,0:T(8,128)(2,1)S(1)}, u32[]{:S(2)}, u32[]{:S(2)}) collective-permute-start(bf16[160,2560]{1,0:T(8,128)(2,1)S(1)} %collective-permute-done.10.refs_3_), channel_id=1, source_target_pairs={{0,64},{64,0},{1,65},{65,1},{2,66},{66,2},{3,67},{67,3},{4,68},{68... | collective-permute-start | bytes 2457608 | tf_op jit(solution)/shard_map/ppermute | solution.py:383
  66.0 15.6 %collective-permute-start.21 = (bf16[160,2560]{1,0:T(8,128)(2,1)S(1)}, bf16[160,2560]{1,0:T(8,128)(2,1)}, u32[]{:S(2)}, u32[]{:S(2)}) collective-permute-start(bf16[160,2560]{1,0:T(8,128)(2,1)S(1)} %bitcast.37), channel_id=1, source_target_pairs={{0,64},{64,0},{1,65},{65,1},{2,66},{66,2},{3,67},{67,3},{4,68},{68... | collective-permute-start | bytes 2457608 | tf_op jit(solution)/shard_map/ppermute | solution.py:383
  74.7 6.9 %collective-permute-start.22 = (bf16[160,2560]{1,0:T(8,128)(2,1)}, bf16[160,2560]{1,0:T(8,128)(2,1)}, u32[]{:S(2)}, u32[]{:S(2)}) collective-permute-start(bf16[160,2560]{1,0:T(8,128)(2,1)} %collective-permute-done.9.refs_5_), channel_id=1, source_target_pairs={{0,64},{64,0},{1,65},{65,1},{2,66},{66,2},{3,67},{67,3},{4,68},{68... | collective-permute-start | bytes 2457608 | tf_op jit(solution)/shard_map/ppermute | solution.py:383
  77.9 0.9 copy-start.1
  78.8 2.9 %collective-permute-start.24 = (bf16[160,2560]{1,0:T(8,128)(2,1)}, bf16[160,2560]{1,0:T(8,128)(2,1)}, u32[]{:S(2)}, u32[]{:S(2)}) collective-permute-start(bf16[160,2560]{1,0:T(8,128)(2,1)} %collective-permute-done.11.refs_7_), channel_id=1, source_target_pairs={{0,64},{64,0},{1,65},{65,1},{2,66},{66,2},{3,67},{67,3},{4,68},{68... | collective-permute-start | bytes 2457608 | tf_op jit(solution)/shard_map/ppermute | solution.py:383
  78.8 0.9 copy-start.3
  79.7 2.9 %collective-permute-start.19 = (bf16[160,2560]{1,0:T(8,128)(2,1)}, bf16[160,2560]{1,0:T(8,128)(2,1)}, u32[]{:S(2)}, u32[]{:S(2)}) collective-permute-start(bf16[160,2560]{1,0:T(8,128)(2,1)} %collective-permute-done.15.refs_2_), channel_id=1, source_target_pairs={{0,64},{64,0},{1,65},{65,1},{2,66},{66,2},{3,67},{67,3},{4,68},{68... | collective-permute-start | bytes 2457608 | tf_op jit(solution)/shard_map/ppermute | solution.py:386
  80.2 0.9 copy-start.5
  81.1 2.7 %collective-permute-start.23 = (bf16[160,2560]{1,0:T(8,128)(2,1)}, bf16[160,2560]{1,0:T(8,128)(2,1)}, u32[]{:S(2)}, u32[]{:S(2)}) collective-permute-start(bf16[160,2560]{1,0:T(8,128)(2,1)} %collective-permute-done.16.refs_6_), channel_id=1, source_target_pairs={{0,64},{64,0},{1,65},{65,1},{2,66},{66,2},{3,67},{67,3},{4,68},{68... | collective-permute-start | bytes 2457608 | tf_op jit(solution)/shard_map/ppermute | solution.py:386
  83.8 1.1 copy-start.2
  85.0 1.1 copy-start.4
  86.1 1.1 copy-start.6
  91.6 8.1 %collective-permute-start.25 = (bf16[256,128]{1,0:T(8,128)(2,1)S(1)}, bf16[256,128]{1,0:T(8,128)(2,1)S(1)}, u32[]{:S(2)}, u32[]{:S(2)}) collective-permute-start(bf16[256,128]{1,0:T(8,128)(2,1)S(1)} %get-tuple-element.97), channel_id=1, source_target_pairs={{0,144},{32,176},{1,145},{33,177},{2,146},{34,178},{3,147},{35,179... | collective-permute-start | bytes 196616 | tf_op jit(solution)/shard_map/ppermute | solution.py:432
  92.3 7.4 %collective-permute-start.26 = (bf16[256,128]{1,0:T(8,128)(2,1)S(1)}, bf16[256,128]{1,0:T(8,128)(2,1)S(1)}, u32[]{:S(2)}, u32[]{:S(2)}) collective-permute-start(bf16[256,128]{1,0:T(8,128)(2,1)S(1)} %get-tuple-element.97), channel_id=1, source_target_pairs={{0,128},{32,160},{1,129},{33,161},{2,130},{34,162},{3,131},{35,163... | collective-permute-start | bytes 196616 | tf_op jit(solution)/shard_map/ppermute | solution.py:433
  93.0 18.9 %collective-permute-start.27 = (bf16[256,128]{1,0:T(8,128)(2,1)S(1)}, bf16[256,128]{1,0:T(8,128)(2,1)S(1)}, u32[]{:S(2)}, u32[]{:S(2)}) collective-permute-start(bf16[256,128]{1,0:T(8,128)(2,1)S(1)} %get-tuple-element.97), channel_id=1, source_target_pairs={{0,16},{32,48},{1,17},{33,49},{2,18},{34,50},{3,19},{35,51},{4,20}... | collective-permute-start | bytes 196616 | tf_op jit(solution)/shard_map/ppermute | solution.py:434
  125.2 8.0 %collective-permute-start.28 = (f32[16,128]{1,0:T(8,128)S(1)}, f32[16,128]{1,0:T(8,128)S(1)}, u32[]{:S(2)}, u32[]{:S(2)}) collective-permute-start(f32[16,128]{1,0:T(8,128)S(1)} %get-tuple-element.105), channel_id=1, source_target_pairs={{0,64},{64,0},{1,65},{65,1},{2,66},{66,2},{3,67},{67,3},{4,68},{68... | collective-permute-start | bytes 24584 | tf_op jit(solution)/shard_map/ppermute | solution.py:454
  126.2 7.0 %collective-permute-start.29 = (f32[16,128]{1,0:T(8,128)S(1)}, f32[16,128]{1,0:T(8,128)S(1)}, u32[]{:S(2)}, u32[]{:S(2)}) collective-permute-start(f32[16,128]{1,0:T(8,128)S(1)} %get-tuple-element.105), channel_id=1, source_target_pairs={{0,32},{32,0},{16,48},{48,16},{1,33},{33,1},{17,49},{49,17},{2,34}... | collective-permute-start | bytes 24584 | tf_op jit(solution)/shard_map/ppermute | solution.py:454
  127.7 5.5 %collective-permute-start.30 = (f32[16,128]{1,0:T(8,128)S(1)}, f32[16,128]{1,0:T(8,128)S(1)}, u32[]{:S(2)}, u32[]{:S(2)}) collective-permute-start(f32[16,128]{1,0:T(8,128)S(1)} %get-tuple-element.105), channel_id=1, source_target_pairs={{0,96},{16,112},{32,64},{48,80},{64,32},{80,48},{96,0},{112,16},{1... | collective-permute-start | bytes 24584 | tf_op jit(solution)/shard_map/ppermute | solution.py:454
  133.2 8.7 %collective-permute-start.31 = (f32[16,128]{1,0:T(8,128)S(1)}, f32[16,128]{1,0:T(8,128)S(1)}, u32[]{:S(2)}, u32[]{:S(2)}) collective-permute-start(f32[16,128]{1,0:T(8,128)S(1)} %add_add_fusion.3), channel_id=1, source_target_pairs={{0,4},{4,8},{8,12},{12,0},{1,5},{5,9},{9,13},{13,1},{2,6},{6,10},{... | collective-permute-start | bytes 24584 | tf_op jit(solution)/shard_map/ppermute | solution.py:454
  133.6 8.4 %collective-permute-start.32 = (f32[16,128]{1,0:T(8,128)S(1)}, f32[16,128]{1,0:T(8,128)S(1)}, u32[]{:S(2)}, u32[]{:S(2)}) collective-permute-start(f32[16,128]{1,0:T(8,128)S(1)} %add_add_fusion.3), channel_id=1, source_target_pairs={{0,8},{4,12},{8,0},{12,4},{1,9},{5,13},{9,1},{13,5},{2,10},{6,14},... | collective-permute-start | bytes 24584 | tf_op jit(solution)/shard_map/ppermute | solution.py:454
  136.2 5.7 %collective-permute-start.33 = (f32[16,128]{1,0:T(8,128)S(1)}, f32[16,128]{1,0:T(8,128)S(1)}, u32[]{:S(2)}, u32[]{:S(2)}) collective-permute-start(f32[16,128]{1,0:T(8,128)S(1)} %add_add_fusion.3), channel_id=1, source_target_pairs={{0,12},{4,0},{8,4},{12,8},{1,13},{5,1},{9,5},{13,9},{2,14},{6,2},{... | collective-permute-start | bytes 24584 | tf_op jit(solution)/shard_map/ppermute | solution.py:454
  142.0 6.6 %collective-permute-start.34 = (f32[16,128]{1,0:T(8,128)S(1)}, f32[16,128]{1,0:T(8,128)S(1)}, u32[]{:S(2)}, u32[]{:S(2)}) collective-permute-start(f32[16,128]{1,0:T(8,128)S(1)} %add_add_fusion.2), channel_id=1, source_target_pairs={{0,1},{1,2},{2,3},{3,0},{4,5},{5,6},{6,7},{7,4},{8,9},{9,10},{10,1... | collective-permute-start | bytes 24584 | tf_op jit(solution)/shard_map/ppermute | solution.py:454
  142.0 6.5 %collective-permute-start.35 = (f32[16,128]{1,0:T(8,128)S(1)}, f32[16,128]{1,0:T(8,128)S(1)}, u32[]{:S(2)}, u32[]{:S(2)}) collective-permute-start(f32[16,128]{1,0:T(8,128)S(1)} %add_add_fusion.2), channel_id=1, source_target_pairs={{0,2},{1,3},{2,0},{3,1},{4,6},{5,7},{6,4},{7,5},{8,10},{9,11},{10,... | collective-permute-start | bytes 24584 | tf_op jit(solution)/shard_map/ppermute | solution.py:454
  144.3 4.2 %collective-permute-start.36 = (f32[16,128]{1,0:T(8,128)S(1)}, f32[16,128]{1,0:T(8,128)S(1)}, u32[]{:S(2)}, u32[]{:S(2)}) collective-permute-start(f32[16,128]{1,0:T(8,128)S(1)} %add_add_fusion.2), channel_id=1, source_target_pairs={{0,3},{1,0},{2,1},{3,2},{4,7},{5,4},{6,5},{7,6},{8,11},{9,8},{10,9... | collective-permute-start | bytes 24584 | tf_op jit(solution)/shard_map/ppermute | solution.py:454
  148.6 10.3 %collective-permute-start.37 = (f32[8,128]{1,0:T(8,128)S(1)}, f32[8,128]{1,0:T(8,128)S(1)}, u32[]{:S(2)}, u32[]{:S(2)}) collective-permute-start(f32[8,128]{1,0:T(8,128)S(1)} %slice.84), channel_id=1, source_target_pairs={{16,144},{48,176},{17,145},{49,177},{18,146},{50,178},{19,147},{51... | collective-permute-start | bytes 12296 | tf_op jit(solution)/shard_map/ppermute | solution.py:459
  152.4 7.1 %collective-permute-start.38 = (f32[256,128]{1,0:T(8,128)S(1)}, f32[256,128]{1,0:T(8,128)S(1)}, u32[]{:S(2)}, u32[]{:S(2)}) collective-permute-start(f32[256,128]{1,0:T(8,128)S(1)} %get-tuple-element.126), channel_id=1, source_target_pairs={{128,144},{160,176},{129,145},{161,177},{130,146},{162,178},{131,1... | collective-permute-start | bytes 393224 | tf_op jit(solution)/shard_map/ppermute | solution.py:447
  153.1 6.4 %collective-permute-start.39 = (f32[256,128]{1,0:T(8,128)S(1)}, f32[256,128]{1,0:T(8,128)S(1)}, u32[]{:S(2)}, u32[]{:S(2)}) collective-permute-start(f32[256,128]{1,0:T(8,128)S(1)} %get-tuple-element.126), channel_id=1, source_target_pairs={{16,144},{48,176},{17,145},{49,177},{18,146},{50,178},{19,147},{51... | collective-permute-start | bytes 393224 | tf_op jit(solution)/shard_map/ppermute | solution.py:446
  159.8 3.3 %collective-permute-start.40 = (f32[256,128]{1,0:T(8,128)S(1)}, f32[256,128]{1,0:T(8,128)S(1)}, u32[]{:S(2)}, u32[]{:S(2)}) collective-permute-start(f32[256,128]{1,0:T(8,128)S(1)} %fusion), channel_id=1, source_target_pairs={{144,0},{176,32},{208,16},{240,48},{145,1},{177,33},{209,17},{241,... | collective-permute-start | bytes 393224 | tf_op jit(solution)/shard_map/ppermute | solution.py:473
  160.5 16.6 %collective-permute-start.41 = (f32[256,128]{1,0:T(8,128)S(1)}, f32[256,128]{1,0:T(8,128)S(1)}, u32[]{:S(2)}, u32[]{:S(2)}) collective-permute-start(f32[256,128]{1,0:T(8,128)S(1)} %fusion), channel_id=1, source_target_pairs={{144,64},{176,96},{208,80},{240,112},{145,65},{177,97},{209,81},{2... | collective-permute-start | bytes 393224 | tf_op jit(solution)/shard_map/ppermute | solution.py:473
  161.8 15.3 %collective-permute-start.42 = (f32[256,128]{1,0:T(8,128)S(1)}, f32[256,128]{1,0:T(8,128)S(1)}, u32[]{:S(2)}, u32[]{:S(2)}) collective-permute-start(f32[256,128]{1,0:T(8,128)S(1)} %fusion), channel_id=1, source_target_pairs={{144,128},{176,160},{208,144},{240,176},{145,129},{177,161},{209,1... | collective-permute-start | bytes 393224 | tf_op jit(solution)/shard_map/ppermute | solution.py:473
  162.5 14.7 %collective-permute-start.43 = (f32[256,128]{1,0:T(8,128)S(1)}, f32[256,128]{1,0:T(8,128)S(1)}, u32[]{:S(2)}, u32[]{:S(2)}) collective-permute-start(f32[256,128]{1,0:T(8,128)S(1)} %fusion), channel_id=1, source_target_pairs={{144,192},{176,224},{208,208},{240,240},{145,193},{177,225},{209,2... | collective-permute-start | bytes 393224 | tf_op jit(solution)/shard_map/ppermute | solution.py:473
